TPU v7x, 32 devices: a whole 2x2x4 slice. The times are simulated.
32 devices in a mesh: grp: 4 (over x, core), dev: 8 (over z, y).
Axes of the slice: x: 2, y: 2, z: 4, core: 2. Of those that a mesh axis runs over, the one named last changes fastest.
Arguments:
- ladder_amps: bfloat16 [16, 72, 4096], P('dev', 'grp'), may hold values from -6 to 6
- ladder_ids: int32 [16, 72], P('dev', 'grp'), may hold values from 0 to 23, as said below
- ladder_count: int32 [16, 4], P('dev', 'grp'), may hold values from 9 to 18, as said below
- cycle_amps: bfloat16 [16, 24, 4096], P('dev', 'grp'), may hold values from -6 to 6
- cycle_ids: int32 [16, 24], P('dev', 'grp'), may hold values from 0 to 7, as said below
- cycle_count: int32 [16, 4], P('dev', 'grp'), may hold values from 3 to 6, as said below
- ladder_panel: bfloat16 [6144, 4096], P('grp', 'dev'), may hold values from -0.078125 to 0.078125
- cycle_panel: bfloat16 [2048, 4096], P('grp', 'dev'), may hold values from -0.125 to 0.125
- owners: int32 [16], replicated, may hold values from 0 to 15, each once
- base: float32 [1024, 4096], P('grp', 'dev'), may hold values from -6 to 6
Outputs:
- residual: float32 [1024, 4096], P('grp', 'dev')
Inputs may be any that keep to these rules, and one draw needn't show every extreme that they name: `ladder_ids`: within one row tile and group the slots name distinct tiles of 0 to 23. `cycle_ids`: within one row tile and group the slots name distinct tiles of 0 to 7. `ladder_count`: slots at or past the count are not live; in every group some row tile has all 18 slots live. `cycle_count`: slots at or past the count are not live; in every group some row tile has all 6 slots live.
All inputs are finite; a program needn't handle non-finite values.
Results may differ from a plain program's by a relative error of at most 0.0003.
Values may be sent and summed in bfloat16 or wider, within the bound.
No kernel may reach another device: no remote copies, remote signals or barrier semaphores. Data moves between devices by JAX's collectives and lax.ppermute only.
A program may use at most 128 MiB of HBM per device.

v0:
```python
import jax
import jax.numpy as jnp
from jax import lax
from jax.sharding import PartitionSpec as P

TS = 64
KLT = 24
KRT = 8


def live_mask(ids, count):
    slots = ids.shape[1]
    return (jnp.arange(slots, dtype=jnp.int32)[None, :] < count).astype(jnp.bfloat16)


def place_tiles(amps, ids, count, ktiles):
    tile_rows, slots = ids.shape
    onehot = (ids[:, :, None] == jnp.arange(ktiles, dtype=jnp.int32)[None, None, :]).astype(
        jnp.bfloat16
    )
    onehot = onehot * live_mask(ids, count)[:, :, None]
    tiles = amps.reshape(tile_rows, slots, TS, TS)
    dense = jnp.einsum("rjk,rjab->rakb", onehot, tiles, preferred_element_type=jnp.float32)
    return dense.astype(jnp.bfloat16).reshape(tile_rows * TS, ktiles * TS)


def per_device(
    ladder_amps,
    ladder_ids,
    ladder_count,
    cycle_amps,
    cycle_ids,
    cycle_count,
    ladder_panel,
    cycle_panel,
    owners,
    base,
):
    own_ladder = place_tiles(ladder_amps, ladder_ids, ladder_count, KLT)
    own_cycle = place_tiles(cycle_amps, cycle_ids, cycle_count, KRT)
    all_ladder, all_cycle = (
        lax.all_gather(own_ladder, "dev", axis=0, tiled=True),
        lax.all_gather(own_cycle, "dev", axis=0, tiled=True),
    )
    count = base.shape[0] * lax.axis_size("grp")
    ladder_rows = all_ladder.reshape(-1, TS, KLT * TS)[owners].reshape(count, KLT * TS)
    cycle_rows = all_cycle.reshape(-1, TS, KRT * TS)[owners].reshape(count, KRT * TS)
    result = jnp.dot(ladder_rows, ladder_panel, preferred_element_type=jnp.float32)
    summed = lax.psum_scatter(
        result + jnp.dot(cycle_rows, cycle_panel, preferred_element_type=jnp.float32),
        "grp",
        scatter_dimension=0,
        tiled=True,
    )
    return base + summed


def solution(mesh):
    placed = (
        P("dev", "grp", None),
        P("dev", "grp"),
        P("dev", "grp"),
        P("dev", "grp", None),
        P("dev", "grp"),
        P("dev", "grp"),
        P("grp", "dev"),
        P("grp", "dev"),
        P(),
        P("grp", "dev"),
    )
    return jax.shard_map(
        per_device, mesh=mesh, in_specs=placed, out_specs=P("grp", "dev"), check_vma=False
    )
```

profile of v0, /device:TPU:0, one launch (start us, length us, event | category | flops | bytes accessed | tf_op | source)
XLA Modules:
  0.0 163.5 jit_solution(10681224621588605505)
XLA Ops:
  6.5 0.0 copy-start
  6.5 0.0 copy-start.4
  6.5 0.0 copy-start.3
  6.5 0.0 all-gather.5.cloned.1.call-start
  6.5 1.2 reshape.76
  7.7 0.7 compare_convert_fusion
  8.5 0.9 fusion.1
  9.4 0.9 reshape.77
  10.2 0.0 copy-start.5
  10.3 0.0 all-gather.5.cloned.1.call-update
  10.3 0.0 all-gather.3.cloned.1.call-start
  10.3 1.4 reshape.72
  11.7 0.0 copy-done.4
  11.7 0.1 compare_convert_fusion.1
  11.8 0.0 copy-done.3
  11.8 0.6 fusion
  12.4 1.2 reshape.73
  13.6 0.0 all-gather.3.cloned.1.call-update
  13.6 0.0 reduce-scatter.2.cloned.1.call-start
  13.7 0.0 copy-done.5
  13.7 39.5 %all-gather.5.cloned.1.call-done = bf16[1024,512]{1,0:T(8,128)(2,1)} async-done(((bf16[128,512]{1,0:T(8,128)(2,1)}), bf16[1024,512]{1,0:T(8,128)(2,1)}) %all-gather.5.cloned.1.call-update) | async-done | bytes 1048592 | tf_op jit(solution)/shard_map/all_gather | solution.py:43
  53.3 1.8 %gather_fusion.1 = bf16[16,64,512]{2,1,0:T(8,128)(2,1)S(1)} fusion(bf16[16,64,512]{2,1,0:T(8,128)(2,1)} %bitcast.35, s32[1024]{0:T(1024)S(1)} %pad_clamp_fusion), kind=kCustom, calls=%fused_computation.1 | custom fusion | bytes 2097216 | tf_op jit(solution)/shard_map/gather | solution.py:47
  55.1 59.6 %all-gather.3.cloned.1.call-done = bf16[1024,1536]{1,0:T(8,128)(2,1)} async-done(((bf16[128,1536]{1,0:T(8,128)(2,1)}), bf16[1024,1536]{1,0:T(8,128)(2,1)}) %all-gather.3.cloned.1.call-update) | async-done | bytes 3145744 | tf_op jit(solution)/shard_map/all_gather | solution.py:42
  114.7 4.3 %gather_fusion = bf16[16,64,1536]{2,1,0:T(8,128)(2,1)} fusion(bf16[16,64,1536]{2,1,0:T(8,128)(2,1)} %bitcast.33, s32[1024]{0:T(1024)S(1)} %pad_clamp_fusion), kind=kCustom, calls=%fused_computation | custom fusion | bytes 6291520 | tf_op jit(solution)/shard_map/gather | solution.py:46
  119.0 0.0 copy-done
  119.0 3.7 %fusion.18 = f32[1024,512]{1,0:T(8,128)S(1)} fusion(bf16[1024,1536]{1,0:T(8,128)(2,1)} %bitcast.34, bf16[1536,512]{1,0:T(8,128)(2,1)S(1)} %copy-done), kind=kOutput, calls=%fused_computation.27 | convolution fusion | flops 1610612736 | bytes 6815744 | tf_op jit(solution)/shard_map/dot_general | solution.py:48
  122.7 0.0 copy-done.2
  122.8 2.0 %convolution_add_fusion = f32[1024,512]{1,0:T(8,128)} fusion(f32[1024,512]{1,0:T(8,128)S(1)} %fusion.18, bf16[1024,512]{1,0:T(8,128)(2,1)S(1)} %bitcast.32, bf16[512,512]{1,0:T(8,128)(2,1)S(1)} %copy-done.2), kind=kOutput, calls=%fused_computation.2 | convolution fusion | flops 537395200 | bytes 5767168 | tf_op jit(solution)/shard_map/dot_general | solution.py:50
  124.8 0.0 reduce-scatter.2.cloned.1.call-update
  124.8 30.2 %reduce-scatter.2.cloned.1.call-done = f32[256,512]{1,0:T(8,128)} async-done(((f32[1024,512]{1,0:T(8,128)}), f32[256,512]{1,0:T(8,128)}) %reduce-scatter.2.cloned.1.call-update) | async-done | bytes 524304 | tf_op jit(solution)/shard_map/reduce_scatter | solution.py:49
  155.0 0.0 copy-done.1
  155.0 1.9 %add.14 = f32[256,512]{1,0:T(8,128)} add(f32[256,512]{1,0:T(8,128)S(1)} %copy-done.1, f32[256,512]{1,0:T(8,128)} %reduce-scatter.2.cloned.1.call-done) | non-fusion elementwise | flops 131072 | bytes 1572864 | tf_op jit(solution)/shard_map/add | solution.py:55
  (4 shorter events, 0.0 us)
Async XLA Ops:
  6.5 112.5 %copy-start = (bf16[1536,512]{1,0:T(8,128)(2,1)S(1)}, bf16[1536,512]{1,0:T(8,128)(2,1)}, u32[]{:S(2)}) copy-start(bf16[1536,512]{1,0:T(8,128)(2,1)} %param.16) | copy-start | bytes 4718596
  6.5 5.2 %copy-start.4 = (s32[2,1]{0,1:T(1,128)S(1)}, s32[2,1]{0,1:T(1,128)}, u32[]{:S(2)}) copy-start(s32[2,1]{0,1:T(1,128)} %param.12) | copy-start | bytes 28
  6.5 5.3 %copy-start.3 = (s32[2,18]{1,0:T(2,128)S(1)}, s32[2,18]{1,0:T(2,128)}, u32[]{:S(2)}) copy-start(s32[2,18]{1,0:T(2,128)} %param.11) | copy-start | bytes 436
  6.5 46.7 %all-gather.5.cloned.1.call-start = ((), (), s32[]{:S(2)}) async-start(), calls=%async_computation.2 | async-start | bytes 1179648 | tf_op jit(solution)/shard_map/all_gather | solution.py:43
  10.2 3.5 %copy-start.5 = (s32[16]{0:T(128)S(1)}, s32[16]{0:T(128)}, u32[]{:S(2)}) copy-start(s32[16]{0:T(128)} %param.18) | copy-start | bytes 196
  10.3 104.4 %all-gather.3.cloned.1.call-start = ((), (), s32[]{:S(2)}) async-start(), calls=%async_computation.1 | async-start | bytes 3538944 | tf_op jit(solution)/shard_map/all_gather | solution.py:42
  13.6 141.4 %reduce-scatter.2.cloned.1.call-start = ((), (), s32[]{:S(2)}) async-start(), calls=%async_computation.3 | async-start | bytes 2621440 | tf_op jit(solution)/shard_map/reduce_scatter | solution.py:49
  119.0 3.7 %copy-start.2 = (bf16[512,512]{1,0:T(8,128)(2,1)S(1)}, bf16[512,512]{1,0:T(8,128)(2,1)}, u32[]{:S(2)}) copy-start(bf16[512,512]{1,0:T(8,128)(2,1)} %param.17) | copy-start | bytes 1572868
  124.8 30.2 %copy-start.1 = (f32[256,512]{1,0:T(8,128)S(1)}, f32[256,512]{1,0:T(8,128)}, u32[]{:S(2)}) copy-start(f32[256,512]{1,0:T(8,128)} %param.19) | copy-start | bytes 1572868
Sparse Core Ops, SparseCore 0:
  10.4 42.8 all-gather.4
  55.5 59.1 all-gather.2
  124.9 30.0 reduce-scatter.1
where the time goes:
time: 164 us; the launch traced here: 163 us
  waiting for transfers between devices  129 us (79%)
  between operations  13.2 us (8%)
  local copies, waits for them, and re-layouts  10.8 us (7%)
  matrix products  7.27 us (4%)
  other arithmetic  2.72 us (2%)
    all_gather x1, waiting for transfers between devices, per_device(): lax.all_gather(own_ladder, 'dev', axis=0, tiled=True)  59.6 us
    all_gather x1, waiting for transfers between devices, per_device(): lax.all_gather(own_cycle, 'dev', axis=0, tiled=True)  39.5 us
    reduce_scatter x1, waiting for transfers between devices, per_device(): lax.psum_scatter(result + jnp.dot(cycle_rows, cycle_panel, preferred_elem...  30.2 us
    gather x1, local copies, waits for them, and re-layouts, per_device(): all_ladder.reshape(-1, TS, KLT * TS)[owners].reshape(count, KLT * TS)  4.31 us
    dot_general x1, matrix products, per_device(): jnp.dot(ladder_rows, ladder_panel, preferred_element_type=jnp.float32)  3.72 us
  transfers between devices with their start and end apart: 3, of which 3 were waited for; matrix products, arithmetic and copies ran while one was open for 3% of the time, Pallas kernels for 0%

commit v1 on v0

v1 whole, which is shorter than its diff:
```python
import functools

import jax
import jax.numpy as jnp
from jax import lax
from jax.experimental import pallas as pl
from jax.experimental.pallas import tpu as pltpu
from jax.sharding import PartitionSpec as P

TS = 64
HALF = TS // 2
VMEM = pl.BlockSpec(memory_space=pltpu.VMEM)
SMEM = pl.BlockSpec(memory_space=pltpu.SMEM)


def ring_order(n):
    return list(range(0, n, 2)) + list(range(n - 1, 0, -2))


def rows_of(amps, count):
    tiles, slots, _ = amps.shape
    live = jnp.arange(slots, dtype=jnp.int32)[None, :] < count
    amps = jnp.where(live[:, :, None], amps, jnp.zeros_like(amps))
    return amps.reshape(tiles, slots * HALF, 2 * TS)


def all_ids(own, n_dev):
    table = own[None]
    step = 1
    while step < n_dev:
        swap = [(d, d ^ step) for d in range(n_dev)]
        table = jnp.concatenate([table, lax.ppermute(table, "dev", swap)], axis=0)
        step *= 2
    return table


def tile_kernel(n_tiles, ladder_slots, at_ref, core_ref, ids_ref, *refs):
    amp_refs = refs[:n_tiles]
    ladder_ref, cycle_ref, keep_ref, send_ref = refs[n_tiles:]
    slots = amp_refs[0].shape[0] // HALF
    cols = ladder_ref.shape[1]
    core = core_ref[0]
    for t in range(n_tiles):
        first = at_ref[t]
        total = jnp.zeros((TS, cols), jnp.float32)
        for q in range(0, slots, 4):
            left, right = [], []
            for s in range(q, min(q + 4, slots)):
                k = pl.multiple_of(ids_ref[first + s] * TS, TS)
                panel_ref = ladder_ref if s < ladder_slots else cycle_ref
                right.append(panel_ref[pl.ds(k, TS), :])
                tile = amp_refs[t][s * HALF : (s + 1) * HALF, :]
                left.append(jnp.concatenate([tile[:, :TS], tile[:, TS:]], axis=0))
            total += jnp.dot(
                jnp.concatenate(left, axis=1),
                jnp.concatenate(right, axis=0),
                preferred_element_type=jnp.float32,
            )
        rows = slice(t * TS, (t + 1) * TS)

        @pl.when(core == 0)
        def _():
            keep_ref[rows, :] = total[:, : cols // 2]
            send_ref[rows, :] = total[:, cols // 2 :]

        @pl.when(core != 0)
        def _():
            keep_ref[rows, :] = total[:, cols // 2 :]
            send_ref[rows, :] = total[:, : cols // 2]


def tile_products(amps, at, core, ids, ladder_panel, cycle_panel, ladder_slots):
    n, cols = len(amps), ladder_panel.shape[1]
    half = jax.ShapeDtypeStruct((n * TS, cols // 2), jnp.float32)
    slots = amps[0].shape[0] // HALF
    return pl.pallas_call(
        functools.partial(tile_kernel, n, ladder_slots),
        out_shape=(half, half),
        in_specs=[SMEM, SMEM, SMEM] + [VMEM] * (n + 2),
        out_specs=(VMEM, VMEM),
        compiler_params=pltpu.CompilerParams(vmem_limit_bytes=24 << 20),
        cost_estimate=pl.CostEstimate(
            flops=2 * n * TS * slots * TS * cols, bytes_accessed=4 << 20, transcendentals=0
        ),
    )(at, core, ids, *amps, ladder_panel, cycle_panel)


def pick_kernel(n_early, slot_ref, early_ref, own_ref, other_ref, mine_ref, partner_ref):
    owned = mine_ref.shape[0] // TS
    for i in range(2 * owned):
        slot = slot_ref[i]
        old = pl.multiple_of(jnp.minimum(slot, n_early - 1) * TS, TS)
        new = pl.multiple_of(jnp.maximum(slot - n_early, 0) * TS, TS)
        late = own_ref[pl.ds(new, TS), :]
        for ref in other_ref:
            late = late + ref[pl.ds(new, TS), :]
        value = jnp.where(slot < n_early, early_ref[pl.ds(old, TS), :], late)
        out_ref, at = (mine_ref, i) if i < owned else (partner_ref, i - owned)
        out_ref[at * TS : (at + 1) * TS, :] = value


def finish_kernel(core_ref, mine_ref, got_ref, base_ref, out_ref, rows_ref):
    rows, cols = base_ref.shape[0], base_ref.shape[1] // 2
    core = core_ref[0]
    for c in range(cols // 128):
        lane = slice(c * 128, (c + 1) * 128)
        for tile in range(rows // TS):
            for part in range(2):
                take = slice(tile * TS + part * HALF, tile * TS + (part + 1) * HALF)
                put = pl.ds(tile * TS + part, HALF, stride=2)
                mine, got = mine_ref[take, lane], got_ref[take, lane]
                rows_ref[0, put, :] = jnp.where(core == 0, mine, got)
                rows_ref[1, put, :] = jnp.where(core == 0, got, mine)
        for side in range(2):
            lane = slice(side * cols + c * 128, side * cols + (c + 1) * 128)
            out_ref[:, lane] = base_ref[:, lane] + rows_ref[side]


def per_device(
    ladder_amps,
    ladder_ids,
    ladder_count,
    cycle_amps,
    cycle_ids,
    cycle_count,
    ladder_panel,
    cycle_panel,
    owners,
    base,
):
    n_dev, n_grp = lax.axis_size("dev"), lax.axis_size("grp")
    me, grp = lax.axis_index("dev"), lax.axis_index("grp")
    core = (grp % 2).reshape(1)
    tiles, ladder_slots, _ = ladder_amps.shape
    slots = ladder_slots + cycle_amps.shape[1]
    order = ring_order(n_dev)
    place = [order.index(d) for d in range(n_dev)]
    forward = [(order[i], order[(i + 1) % n_dev]) for i in range(n_dev)]
    backward = [(b, a) for a, b in forward]
    swap = [(g, g ^ 1) for g in range(n_grp)]
    order_of, place_of = jnp.array(order, jnp.int32), jnp.array(place, jnp.int32)

    own = jnp.concatenate(
        [rows_of(ladder_amps, ladder_count), rows_of(cycle_amps, cycle_count)], axis=1
    )
    own = [own[t] for t in range(tiles)]
    ids = all_ids(jnp.concatenate([ladder_ids, cycle_ids], axis=1), n_dev).reshape(-1)

    def source(back):
        return order_of[(place_of[me] - back + n_dev) % n_dev]

    batches = [[(own[t], 0, t) for t in range(tiles)]]
    ahead, behind = own, own
    for step in range(1, n_dev // 2):
        ahead = [lax.ppermute(a, "dev", forward) for a in ahead]
        behind = [lax.ppermute(b, "dev", backward) for b in behind]
        batches.append(
            [(a, step, t) for t, a in enumerate(ahead)]
            + [(b, -step, t) for t, b in enumerate(behind)]
        )
    cut = tiles // 2
    batches.append(
        [(lax.ppermute(ahead[t], "dev", forward), n_dev // 2, t) for t in range(cut)]
        + [(lax.ppermute(behind[t], "dev", backward), n_dev // 2, t) for t in range(cut, tiles)]
    )

    where, early = [], []
    for number, batch in enumerate(batches):
        at = jnp.stack([(jnp.bitwise_xor(source(b), me) * tiles + t) * slots for _, b, t in batch])
        where += [source(b) * tiles + t for _, b, t in batch]
        keep, send = tile_products(
            [a for a, _, _ in batch], at, core, ids, ladder_panel, cycle_panel, ladder_slots
        )
        mine = keep + lax.ppermute(send, "grp", swap)
        others = [
            lax.ppermute(mine, "grp", [(g, (g + k) % n_grp) for g in range(n_grp)])
            for k in range(2, n_grp, 2)
        ]
        if number < len(batches) - 1:
            early.append(functools.reduce(jnp.add, others, mine))
    early = jnp.concatenate(early, axis=0)
    n_early = early.shape[0] // TS

    owned = owners.shape[0] // n_grp
    slot_of = jnp.argmax(owners[:, None] == jnp.stack(where)[None, :], axis=1).astype(jnp.int32)
    picks = jnp.concatenate(
        [
            lax.dynamic_slice_in_dim(slot_of, grp * owned, owned),
            lax.dynamic_slice_in_dim(slot_of, jnp.bitwise_xor(grp, 1) * owned, owned),
        ]
    )
    rows, cols = base.shape
    half = jax.ShapeDtypeStruct((rows, cols // 2), jnp.float32)
    picked, given = pl.pallas_call(
        lambda slot, old, new, *rest: pick_kernel(n_early, slot, old, new, rest[:-2], *rest[-2:]),
        out_shape=(half, half),
        in_specs=[SMEM] + [VMEM] * (2 + len(others)),
        out_specs=(VMEM, VMEM),
        compiler_params=pltpu.CompilerParams(vmem_limit_bytes=32 << 20),
    )(picks, early, mine, *others)
    got = lax.ppermute(given, "grp", swap)
    return pl.pallas_call(
        finish_kernel,
        out_shape=jax.ShapeDtypeStruct(base.shape, jnp.float32),
        in_specs=[SMEM, VMEM, VMEM, VMEM],
        out_specs=VMEM,
        scratch_shapes=[pltpu.VMEM((2, rows, 128), jnp.float32)],
        compiler_params=pltpu.CompilerParams(vmem_limit_bytes=16 << 20),
    )(core, picked, got, base)


def solution(mesh):
    placed = (
        P("dev", "grp", None),
        P("dev", "grp"),
        P("dev", "grp"),
        P("dev", "grp", None),
        P("dev", "grp"),
        P("dev", "grp"),
        P("grp", "dev"),
        P("grp", "dev"),
        P(),
        P("grp", "dev"),
    )
    return jax.shard_map(
        per_device, mesh=mesh, in_specs=placed, out_specs=P("grp", "dev"), check_vma=False
    )
```

time: 164 us -> 94.3 us (0.57)
  waiting for transfers between devices: 129 us -> 20.1 us
  starting transfers between devices: 0.09 us -> 28.4 us
  Pallas kernels: 0 us -> 16.4 us
  local copies, waits for them, and re-layouts: 10.8 us -> 2.21 us
  other arithmetic: 2.72 us -> 11 us
  matrix products: 7.27 us -> 0 us
  between operations: 13.2 us -> 15.7 us
    all_gather x2 -> x0, waiting for transfers between devices: 99.1 us -> none  [the longest x1 59.6 us: per_device(): lax.all_gather(own_ladder, 'dev', axis=0, tiled=True)]
    reduce_scatter x1 -> x0, waiting for transfers between devices: 30.2 us -> none  [per_device(): lax.psum_scatter(result + jnp.dot(cycle_rows, cycle_panel, preferred_elem...]
    ppermute x0 -> x28, starting transfers between devices: none -> 28.4 us  [the longest x6 7.57 us: per_device(): behind = [lax.ppermute(b, 'dev', backward) for b in behind]]
    ppermute x0 -> x28, waiting for transfers between devices: none -> 20.1 us  [the longest x5 14.6 us: per_device(): lax.ppermute(mine, 'grp', [(g, (g + k) % n_grp) for g in range(n_grp)])]
    pallas_call x0 -> x7, Pallas kernels: none -> 16.4 us  [the longest x5 14.8 us: tile_products(): pl.pallas_call(functools.partial(tile_kernel, n, ladder_slots), out_shape...]
    dot_general x4 -> x0, matrix products: 7.27 us -> none  [the longest x1 3.72 us: per_device(): jnp.dot(ladder_rows, ladder_panel, preferred_element_type=jnp.float32)]
    gather x2 -> x0, local copies, waits for them, and re-layouts: 6.15 us -> none  [the longest x1 4.31 us: per_device(): all_ladder.reshape(-1, TS, KLT * TS)[owners].reshape(count, KLT * TS)]
    add x1 -> x9, other arithmetic: 1.91 us -> 7.48 us  [the longest x5 5.3 us: per_device(): mine = keep + lax.ppermute(send, 'grp', swap)]
  transfers between devices with their start and end apart: 3 -> 28, of which waited for: 3 -> 4; matrix products, arithmetic and copies ran while one was open for 3% -> 11% of each run, Pallas kernels for 0% -> 16%
where the time goes in v1:
time: 94.3 us; the launch traced here: 93.7 us
  starting transfers between devices  28.4 us (30%)
  waiting for transfers between devices  20.1 us (21%)
  Pallas kernels  16.4 us (17%)
  between operations  15.7 us (17%)
  other arithmetic  11 us (12%)
  local copies, waits for them, and re-layouts  2.21 us (2%)
    pallas_call x5, Pallas kernels, tile_products(): pl.pallas_call(functools.partial(tile_kernel, n, ladder_slots), out_shape...  14.8 us
    ppermute x5, waiting for transfers between devices, per_device(): lax.ppermute(mine, 'grp', [(g, (g + k) % n_grp) for g in range(n_grp)])  14.6 us
    ppermute x6, starting transfers between devices, per_device(): behind = [lax.ppermute(b, 'dev', backward) for b in behind]  7.57 us
    ppermute x3, starting transfers between devices, all_ids(): table = jnp.concatenate([table, lax.ppermute(table, 'dev', swap)], axis=0)  6.11 us
    ppermute x5, starting transfers between devices, per_device(): lax.ppermute(mine, 'grp', [(g, (g + k) % n_grp) for g in range(n_grp)])  5.74 us
    ppermute x6, starting transfers between devices, per_device(): ahead = [lax.ppermute(a, 'dev', forward) for a in ahead]  5.71 us
    add x5, other arithmetic, per_device(): mine = keep + lax.ppermute(send, 'grp', swap)  5.3 us
    ppermute x3, waiting for transfers between devices, all_ids(): table = jnp.concatenate([table, lax.ppermute(table, 'dev', swap)], axis=0)  3.92 us
  transfers between devices with their start and end apart: 28, of which 4 were waited for; matrix products, arithmetic and copies ran while one was open for 11% of the time, Pallas kernels for 16%

profile of v1, /device:TPU:0, one launch (start us, length us, event | category | flops | bytes accessed | tf_op | source)
XLA Modules:
  0.0 93.7 jit_solution(13714536553197632990)
XLA Ops:
  0.0 0.7 iota_compare_fusion
  0.7 1.3 %broadcast_select_fusion = bf16[2,18,4096]{2,0,1:T(2,128)(2,1)S(1)} fusion(bf16[2,18,4096]{2,0,1:T(2,128)(2,1)} %param.12, pred[2,18]{0,1:T(8,128)(4,1)S(1)} %iota_compare_fusion), kind=kLoop, calls=%fused_computation.1 | loop fusion | flops 147456 | bytes 589860 | tf_op jit(solution)/shard_map/jit(_where)/select_n | solution.py:23
  2.9 3.0 %collective-permute-start.8 = (bf16[768,128]{1,0:T(8,128)(2,1)S(1)}, bf16[768,128]{1,0:T(8,128)(2,1)S(1)}, u32[]{:S(2)}, u32[]{:S(2)}) collective-permute-start(bf16[768,128]{1,0:T(8,128)(2,1)S(1)} %get-tuple-element.31.refs_1_), channel_id=1, source_target_pairs={{2,0},{4,2},{6,4},{7,6},{5,7},{3,5},{1,3},{0,1},{10,8},{12,10},{14... | collective-permute-start | bytes 589832 | tf_op jit(solution)/shard_map/ppermute | solution.py:156
  6.1 2.0 %collective-permute-start.5 = (bf16[768,128]{1,0:T(8,128)(2,1)S(1)}, bf16[768,128]{1,0:T(8,128)(2,1)S(1)}, u32[]{:S(2)}, u32[]{:S(2)}) collective-permute-start(bf16[768,128]{1,0:T(8,128)(2,1)S(1)} %get-tuple-element.32.refs_0_), channel_id=1, source_target_pairs={{0,2},{2,4},{4,6},{6,7},{7,5},{5,3},{3,1},{1,0},{8,10},{10,12},{12... | collective-permute-start | bytes 589832 | tf_op jit(solution)/shard_map/ppermute | solution.py:155
  8.2 1.9 %collective-permute-start = (s32[1,2,24]{2,1,0:T(2,128)S(1)}, s32[1,2,24]{2,1,0:T(2,128)S(1)}, u32[]{:S(2)}, u32[]{:S(2)}) collective-permute-start(s32[1,2,24]{2,1,0:T(2,128)S(1)} %add_bitcast_fusion), channel_id=1, source_target_pairs={{0,1},{1,0},{2,3},{3,2},{4,5},{5,4},{6,7},{7,6},{8,9},{9,8},{10,11... | collective-permute-start | bytes 584 | tf_op jit(solution)/shard_map/ppermute | solution.py:32
  19.4 1.6 %collective-permute-start.11 = (bf16[768,128]{1,0:T(8,128)(2,1)S(1)}, bf16[768,128]{1,0:T(8,128)(2,1)}, u32[]{:S(2)}, u32[]{:S(2)}) collective-permute-start(bf16[768,128]{1,0:T(8,128)(2,1)S(1)} %collective-permute-done.5.refs_0_), channel_id=1, source_target_pairs={{0,2},{2,4},{4,6},{6,7},{7,5},{5,3},{3,1},{1,0},{8,10},{10,12},{12... | collective-permute-start | bytes 589832 | tf_op jit(solution)/shard_map/ppermute | solution.py:155
  21.4 1.6 %collective-permute-start.12 = (bf16[768,128]{1,0:T(8,128)(2,1)S(1)}, bf16[768,128]{1,0:T(8,128)(2,1)}, u32[]{:S(2)}, u32[]{:S(2)}) collective-permute-start(bf16[768,128]{1,0:T(8,128)(2,1)S(1)} %collective-permute-done.6.refs_1_), channel_id=1, source_target_pairs={{0,2},{2,4},{4,6},{6,7},{7,5},{5,3},{3,1},{1,0},{8,10},{10,12},{12... | collective-permute-start | bytes 589832 | tf_op jit(solution)/shard_map/ppermute | solution.py:155
  23.4 1.6 %collective-permute-start.1 = (s32[2,2,24]{2,1,0:T(2,128)S(1)}, s32[2,2,24]{2,1,0:T(2,128)S(1)}, u32[]{:S(2)}, u32[]{:S(2)}) collective-permute-start(s32[2,2,24]{2,1,0:T(2,128)S(1)} %pad_add_fusion.2), channel_id=1, source_target_pairs={{0,2},{1,3},{2,0},{3,1},{4,6},{5,7},{6,4},{7,5},{8,10},{9,11},{10,... | collective-permute-start | bytes 1160 | tf_op jit(solution)/shard_map/ppermute | solution.py:32
  26.3 3.9 %collective-permute-done.1 = s32[2,2,24]{2,1,0:T(2,128)S(1)} collective-permute-done((s32[2,2,24]{2,1,0:T(2,128)S(1)}, s32[2,2,24]{2,1,0:T(2,128)S(1)}, u32[]{:S(2)}, u32[]{:S(2)}) %collective-permute-start.1) | collective-permute-done | bytes 416 | tf_op jit(solution)/shard_map/ppermute | solution.py:32
  30.3 2.6 %collective-permute-start.2 = (s32[4,2,24]{2,1,0:T(2,128)S(1)}, s32[4,2,24]{2,1,0:T(2,128)S(1)}, u32[]{:S(2)}, u32[]{:S(2)}) collective-permute-start(s32[4,2,24]{2,1,0:T(2,128)S(1)} %pad_add_fusion.1), channel_id=1, source_target_pairs={{0,4},{1,5},{2,6},{3,7},{4,0},{5,1},{6,2},{7,3},{8,12},{9,13},{10,... | collective-permute-start | bytes 2312 | tf_op jit(solution)/shard_map/ppermute | solution.py:32
  33.1 1.8 %collective-permute-start.20 = (bf16[768,128]{1,0:T(8,128)(2,1)}, bf16[768,128]{1,0:T(8,128)(2,1)}, u32[]{:S(2)}, u32[]{:S(2)}) collective-permute-start(bf16[768,128]{1,0:T(8,128)(2,1)} %collective-permute-done.14.refs_3_), channel_id=1, source_target_pairs={{2,0},{4,2},{6,4},{7,6},{5,7},{3,5},{1,3},{0,1},{10,8},{12,10},{14... | collective-permute-start | bytes 589832 | tf_op jit(solution)/shard_map/ppermute | solution.py:156
  35.2 1.8 %collective-permute-start.19 = (bf16[768,128]{1,0:T(8,128)(2,1)}, bf16[768,128]{1,0:T(8,128)(2,1)}, u32[]{:S(2)}, u32[]{:S(2)}) collective-permute-start(bf16[768,128]{1,0:T(8,128)(2,1)} %collective-permute-done.13.refs_2_), channel_id=1, source_target_pairs={{2,0},{4,2},{6,4},{7,6},{5,7},{3,5},{1,3},{0,1},{10,8},{12,10},{14... | collective-permute-start | bytes 589832 | tf_op jit(solution)/shard_map/ppermute | solution.py:156
  37.1 3.3 %shard_map.125 = (f32[256,256]{1,0:T(8,128)S(1)}, f32[256,256]{1,0:T(8,128)}) custom-call(s32[4]{0:T(128)S(1)} %pad_add_fusion.5.at_ref, s32[1]{0:T(128)} %bitcast.core_ref, s32[384]{0:T(512)S(1)} %reshape.75.ids_ref, bf16[768,128]{1,0:T(8,128)(2,1)S(1)} %collective-permute-done.5.refs_0_, bf16[768,128]{1,0:T(8,128)(2,1)S(1)} %collective-permute-done.6.refs_1_, ...), custom_call_target="tpu_custom_call" | custom-call | flops 402653184 | bytes 4194304 | tf_op jit(solution)/shard_map/pallas_call | solution.py:76
  41.0 3.9 %shard_map.126 = (f32[256,256]{1,0:T(8,128)S(1)}, f32[256,256]{1,0:T(8,128)}) custom-call(s32[4]{0:T(128)S(1)} %pad_add_fusion.6.at_ref, s32[1]{0:T(128)} %bitcast.core_ref, s32[384]{0:T(512)S(1)} %reshape.75.ids_ref, bf16[768,128]{1,0:T(8,128)(2,1)} %collective-permute-done.11.refs_0_, bf16[768,128]{1,0:T(8,128)(2,1)} %collective-permute-done.12.refs_1_, ...), custom_call_target="tpu_custom_call" | custom-call | flops 402653184 | bytes 4194304 | tf_op jit(solution)/shard_map/pallas_call | solution.py:76
  45.5 3.9 %shard_map.127 = (f32[256,256]{1,0:T(8,128)S(1)}, f32[256,256]{1,0:T(8,128)}) custom-call(s32[4]{0:T(128)S(1)} %pad_add_fusion.7.at_ref, s32[1]{0:T(128)} %bitcast.core_ref, s32[384]{0:T(512)S(1)} %reshape.75.ids_ref, bf16[768,128]{1,0:T(8,128)(2,1)} %collective-permute-done.17.refs_0_, bf16[768,128]{1,0:T(8,128)(2,1)} %collective-permute-done.18.refs_1_, ...), custom_call_target="tpu_custom_call" | custom-call | flops 402653184 | bytes 4194304 | tf_op jit(solution)/shard_map/pallas_call | solution.py:76
  54.6 2.2 %shard_map.124 = (f32[128,256]{1,0:T(8,128)S(1)}, f32[128,256]{1,0:T(8,128)}) custom-call(s32[2]{0:T(128)S(1)} %pad_add_fusion.4.at_ref, s32[1]{0:T(128)} %bitcast.core_ref, s32[384]{0:T(512)S(1)} %reshape.75.ids_ref, bf16[768,128]{1,0:T(8,128)(2,1)S(1)} %get-tuple-element.32.refs_0_, bf16[768,128]{1,0:T(8,128)(2,1)S(1)} %get-tuple-element.31.refs_1_, ...), custom_call_target="tpu_custom_call" | custom-call | flops 201326592 | bytes 4194304 | tf_op jit(solution)/shard_map/pallas_call | solution.py:76
  57.5 1.8 %collective-permute-start.24 = (bf16[768,128]{1,0:T(8,128)(2,1)}, bf16[768,128]{1,0:T(8,128)(2,1)S(1)}, u32[]{:S(2)}, u32[]{:S(2)}) collective-permute-start(bf16[768,128]{1,0:T(8,128)(2,1)} %collective-permute-done.20.refs_3_), channel_id=1, source_target_pairs={{2,0},{4,2},{6,4},{7,6},{5,7},{3,5},{1,3},{0,1},{10,8},{12,10},{14... | collective-permute-start | bytes 589832 | tf_op jit(solution)/shard_map/ppermute | solution.py:164
  59.3 0.8 iota_reduce_fusion
  60.8 1.7 %add.357 = f32[256,256]{1,0:T(8,128)} add(f32[256,256]{1,0:T(8,128)S(1)} %get-tuple-element.21, f32[256,256]{1,0:T(8,128)} %collective-permute-done.9) | non-fusion elementwise | flops 65536 | bytes 786432 | tf_op jit(solution)/shard_map/add | solution.py:174
  62.5 1.5 %collective-permute-start.10 = (f32[256,256]{1,0:T(8,128)}, f32[256,256]{1,0:T(8,128)}, u32[]{:S(2)}, u32[]{:S(2)}) collective-permute-start(f32[256,256]{1,0:T(8,128)} %add.357), channel_id=1, source_target_pairs={{0,16},{8,24},{16,0},{24,8},{1,17},{9,25},{17,1},{25,9},{2,18},{10... | collective-permute-start | bytes 786440 | tf_op jit(solution)/shard_map/ppermute | solution.py:176
  64.0 1.7 %add.361 = f32[256,256]{1,0:T(8,128)} add(f32[256,256]{1,0:T(8,128)S(1)} %get-tuple-element.23, f32[256,256]{1,0:T(8,128)} %collective-permute-done.15) | non-fusion elementwise | flops 65536 | bytes 786432 | tf_op jit(solution)/shard_map/add | solution.py:174
  66.2 1.0 %add.365 = f32[256,256]{1,0:T(8,128)S(1)} add(f32[256,256]{1,0:T(8,128)S(1)} %get-tuple-element.25, f32[256,256]{1,0:T(8,128)} %collective-permute-done.21) | non-fusion elementwise | flops 65536 | bytes 786432 | tf_op jit(solution)/shard_map/add | solution.py:174
  67.2 1.6 %collective-permute-start.22 = (f32[256,256]{1,0:T(8,128)S(1)}, f32[256,256]{1,0:T(8,128)S(1)}, u32[]{:S(2)}, u32[]{:S(2)}) collective-permute-start(f32[256,256]{1,0:T(8,128)S(1)} %add.365), channel_id=1, source_target_pairs={{0,16},{8,24},{16,0},{24,8},{1,17},{9,25},{17,1},{25,9},{2,18},{10... | collective-permute-start | bytes 786440 | tf_op jit(solution)/shard_map/ppermute | solution.py:176
  68.8 0.9 add.353
  70.4 1.5 %shard_map.128 = (f32[128,256]{1,0:T(8,128)S(1)}, f32[128,256]{1,0:T(8,128)S(1)}) custom-call(s32[2]{0:T(128)S(1)} %pad_add_fusion.8.at_ref, s32[1]{0:T(128)} %bitcast.core_ref, s32[384]{0:T(512)S(1)} %reshape.75.ids_ref, bf16[768,128]{1,0:T(8,128)(2,1)S(1)} %collective-permute-done.23.refs_0_, bf16[768,128]{1,0:T(8,128)(2,1)S(1)} %collective-permute-done.24.refs_1_, ...), custom_call_target="tpu_custom_call" | custom-call | flops 201326592 | bytes 4194304 | tf_op jit(solution)/shard_map/pallas_call | solution.py:76
  72.1 12.3 %collective-permute-done.4 = f32[128,256]{1,0:T(8,128)S(1)} collective-permute-done((f32[128,256]{1,0:T(8,128)S(1)}, f32[128,256]{1,0:T(8,128)S(1)}, u32[]{:S(2)}, u32[]{:S(2)}) %collective-permute-start.4) | collective-permute-done | bytes 131104 | tf_op jit(solution)/shard_map/ppermute | solution.py:176
  84.5 1.1 %add.358 = f32[256,256]{1,0:T(8,128)S(1)} add(f32[256,256]{1,0:T(8,128)} %add.357, f32[256,256]{1,0:T(8,128)} %collective-permute-done.10) | non-fusion elementwise | flops 65536 | bytes 786432 | tf_op jit(solution)/shard_map/add | solution.py:180
  85.6 1.6 %collective-permute-start.26 = (f32[128,256]{1,0:T(8,128)S(1)}, f32[128,256]{1,0:T(8,128)S(1)}, u32[]{:S(2)}, u32[]{:S(2)}) collective-permute-start(f32[128,256]{1,0:T(8,128)S(1)} %add.368.new), channel_id=1, source_target_pairs={{0,16},{8,24},{16,0},{24,8},{1,17},{9,25},{17,1},{25,9},{2,18},{10... | collective-permute-start | bytes 393224 | tf_op jit(solution)/shard_map/ppermute | solution.py:176
  87.1 1.1 %add.362 = f32[256,256]{1,0:T(8,128)S(1)} add(f32[256,256]{1,0:T(8,128)} %add.361, f32[256,256]{1,0:T(8,128)} %collective-permute-done.16) | non-fusion elementwise | flops 65536 | bytes 786432 | tf_op jit(solution)/shard_map/add | solution.py:180
  88.3 2.3 %collective-permute-done.26.rest_0_ = f32[128,256]{1,0:T(8,128)S(1)} collective-permute-done((f32[128,256]{1,0:T(8,128)S(1)}, f32[128,256]{1,0:T(8,128)S(1)}, u32[]{:S(2)}, u32[]{:S(2)}) %collective-permute-start.26) | collective-permute-done | bytes 131104 | tf_op jit(solution)/shard_map/ppermute | solution.py:176
  91.3 1.5 %collective-permute-done.27.got_ref = f32[256,256]{1,0:T(8,128)S(1)} collective-permute-done((f32[256,256]{1,0:T(8,128)S(1)}, f32[256,256]{1,0:T(8,128)S(1)}, u32[]{:S(2)}, u32[]{:S(2)}) %collective-permute-start.27) | collective-permute-done | bytes 262176 | tf_op jit(solution)/shard_map/ppermute | solution.py:201
  92.8 0.9 shard_map.130
  (88 shorter events, 7.9 us)
Async XLA Ops:
  2.2 13.8 %copy-start.4 = (s32[8]{0:T(128)S(1)}, s32[8]{0:T(128)}, u32[]{:S(2)}) copy-start(s32[8]{0:T(128)} %constant.170.clone) | copy-start | bytes 100
  2.2 34.8 %copy-start = (bf16[1536,512]{1,0:T(8,128)(2,1)S(1)}, bf16[1536,512]{1,0:T(8,128)(2,1)}, u32[]{:S(2)}) copy-start(bf16[1536,512]{1,0:T(8,128)(2,1)} %refs_2_.3) | copy-start | bytes 4718596
  2.2 34.8 %copy-start.1 = (bf16[512,512]{1,0:T(8,128)(2,1)S(1)}, bf16[512,512]{1,0:T(8,128)(2,1)}, u32[]{:S(2)}) copy-start(bf16[512,512]{1,0:T(8,128)(2,1)} %refs_3_.3) | copy-start | bytes 1572868
  2.9 18.0 %collective-permute-start.8 = (bf16[768,128]{1,0:T(8,128)(2,1)S(1)}, bf16[768,128]{1,0:T(8,128)(2,1)S(1)}, u32[]{:S(2)}, u32[]{:S(2)}) collective-permute-start(bf16[768,128]{1,0:T(8,128)(2,1)S(1)} %get-tuple-element.31.refs_1_), channel_id=1, source_target_pairs={{2,0},{4,2},{6,4},{7,6},{5,7},{3,5},{1,3},{0,1},{10,8},{12,10},{14... | collective-permute-start | bytes 589832 | tf_op jit(solution)/shard_map/ppermute | solution.py:156
  6.0 15.4 %collective-permute-start.6 = (bf16[768,128]{1,0:T(8,128)(2,1)S(1)}, bf16[768,128]{1,0:T(8,128)(2,1)S(1)}, u32[]{:S(2)}, u32[]{:S(2)}) collective-permute-start(bf16[768,128]{1,0:T(8,128)(2,1)S(1)} %get-tuple-element.31.refs_1_), channel_id=1, source_target_pairs={{0,2},{2,4},{4,6},{6,7},{7,5},{5,3},{3,1},{1,0},{8,10},{10,12},{12... | collective-permute-start | bytes 589832 | tf_op jit(solution)/shard_map/ppermute | solution.py:155
  6.1 13.3 %collective-permute-start.5 = (bf16[768,128]{1,0:T(8,128)(2,1)S(1)}, bf16[768,128]{1,0:T(8,128)(2,1)S(1)}, u32[]{:S(2)}, u32[]{:S(2)}) collective-permute-start(bf16[768,128]{1,0:T(8,128)(2,1)S(1)} %get-tuple-element.32.refs_0_), channel_id=1, source_target_pairs={{0,2},{2,4},{4,6},{6,7},{7,5},{5,3},{3,1},{1,0},{8,10},{10,12},{12... | collective-permute-start | bytes 589832 | tf_op jit(solution)/shard_map/ppermute | solution.py:155
  8.0 14.9 %collective-permute-start.7 = (bf16[768,128]{1,0:T(8,128)(2,1)S(1)}, bf16[768,128]{1,0:T(8,128)(2,1)S(1)}, u32[]{:S(2)}, u32[]{:S(2)}) collective-permute-start(bf16[768,128]{1,0:T(8,128)(2,1)S(1)} %get-tuple-element.32.refs_0_), channel_id=1, source_target_pairs={{2,0},{4,2},{6,4},{7,6},{5,7},{3,5},{1,3},{0,1},{10,8},{12,10},{14... | collective-permute-start | bytes 589832 | tf_op jit(solution)/shard_map/ppermute | solution.py:156
  8.2 15.3 %collective-permute-start = (s32[1,2,24]{2,1,0:T(2,128)S(1)}, s32[1,2,24]{2,1,0:T(2,128)S(1)}, u32[]{:S(2)}, u32[]{:S(2)}) collective-permute-start(s32[1,2,24]{2,1,0:T(2,128)S(1)} %add_bitcast_fusion), channel_id=1, source_target_pairs={{0,1},{1,0},{2,3},{3,2},{4,5},{5,4},{6,7},{7,6},{8,9},{9,8},{10,11... | collective-permute-start | bytes 584 | tf_op jit(solution)/shard_map/ppermute | solution.py:32
  19.4 13.5 %collective-permute-start.11 = (bf16[768,128]{1,0:T(8,128)(2,1)S(1)}, bf16[768,128]{1,0:T(8,128)(2,1)}, u32[]{:S(2)}, u32[]{:S(2)}) collective-permute-start(bf16[768,128]{1,0:T(8,128)(2,1)S(1)} %collective-permute-done.5.refs_0_), channel_id=1, source_target_pairs={{0,2},{2,4},{4,6},{6,7},{7,5},{5,3},{3,1},{1,0},{8,10},{10,12},{12... | collective-permute-start | bytes 589832 | tf_op jit(solution)/shard_map/ppermute | solution.py:155
  20.9 12.2 %collective-permute-start.14 = (bf16[768,128]{1,0:T(8,128)(2,1)S(1)}, bf16[768,128]{1,0:T(8,128)(2,1)}, u32[]{:S(2)}, u32[]{:S(2)}) collective-permute-start(bf16[768,128]{1,0:T(8,128)(2,1)S(1)} %collective-permute-done.8.refs_3_), channel_id=1, source_target_pairs={{2,0},{4,2},{6,4},{7,6},{5,7},{3,5},{1,3},{0,1},{10,8},{12,10},{14... | collective-permute-start | bytes 589832 | tf_op jit(solution)/shard_map/ppermute | solution.py:156
  21.4 13.5 %collective-permute-start.12 = (bf16[768,128]{1,0:T(8,128)(2,1)S(1)}, bf16[768,128]{1,0:T(8,128)(2,1)}, u32[]{:S(2)}, u32[]{:S(2)}) collective-permute-start(bf16[768,128]{1,0:T(8,128)(2,1)S(1)} %collective-permute-done.6.refs_1_), channel_id=1, source_target_pairs={{0,2},{2,4},{4,6},{6,7},{7,5},{5,3},{3,1},{1,0},{8,10},{10,12},{12... | collective-permute-start | bytes 589832 | tf_op jit(solution)/shard_map/ppermute | solution.py:155
  23.0 12.2 %collective-permute-start.13 = (bf16[768,128]{1,0:T(8,128)(2,1)S(1)}, bf16[768,128]{1,0:T(8,128)(2,1)}, u32[]{:S(2)}, u32[]{:S(2)}) collective-permute-start(bf16[768,128]{1,0:T(8,128)(2,1)S(1)} %collective-permute-done.7.refs_2_), channel_id=1, source_target_pairs={{2,0},{4,2},{6,4},{7,6},{5,7},{3,5},{1,3},{0,1},{10,8},{12,10},{14... | collective-permute-start | bytes 589832 | tf_op jit(solution)/shard_map/ppermute | solution.py:156
  23.4 6.8 %collective-permute-start.1 = (s32[2,2,24]{2,1,0:T(2,128)S(1)}, s32[2,2,24]{2,1,0:T(2,128)S(1)}, u32[]{:S(2)}, u32[]{:S(2)}) collective-permute-start(s32[2,2,24]{2,1,0:T(2,128)S(1)} %pad_add_fusion.2), channel_id=1, source_target_pairs={{0,2},{1,3},{2,0},{3,1},{4,6},{5,7},{6,4},{7,5},{8,10},{9,11},{10,... | collective-permute-start | bytes 1160 | tf_op jit(solution)/shard_map/ppermute | solution.py:32
  30.3 6.7 %collective-permute-start.2 = (s32[4,2,24]{2,1,0:T(2,128)S(1)}, s32[4,2,24]{2,1,0:T(2,128)S(1)}, u32[]{:S(2)}, u32[]{:S(2)}) collective-permute-start(s32[4,2,24]{2,1,0:T(2,128)S(1)} %pad_add_fusion.1), channel_id=1, source_target_pairs={{0,4},{1,5},{2,6},{3,7},{4,0},{5,1},{6,2},{7,3},{8,12},{9,13},{10,... | collective-permute-start | bytes 2312 | tf_op jit(solution)/shard_map/ppermute | solution.py:32
  32.9 12.0 %collective-permute-start.17 = (bf16[768,128]{1,0:T(8,128)(2,1)}, bf16[768,128]{1,0:T(8,128)(2,1)}, u32[]{:S(2)}, u32[]{:S(2)}) collective-permute-start(bf16[768,128]{1,0:T(8,128)(2,1)} %collective-permute-done.11.refs_0_), channel_id=1, source_target_pairs={{0,2},{2,4},{4,6},{6,7},{7,5},{5,3},{3,1},{1,0},{8,10},{10,12},{12... | collective-permute-start | bytes 589832 | tf_op jit(solution)/shard_map/ppermute | solution.py:155
  33.1 12.3 %collective-permute-start.20 = (bf16[768,128]{1,0:T(8,128)(2,1)}, bf16[768,128]{1,0:T(8,128)(2,1)}, u32[]{:S(2)}, u32[]{:S(2)}) collective-permute-start(bf16[768,128]{1,0:T(8,128)(2,1)} %collective-permute-done.14.refs_3_), channel_id=1, source_target_pairs={{2,0},{4,2},{6,4},{7,6},{5,7},{3,5},{1,3},{0,1},{10,8},{12,10},{14... | collective-permute-start | bytes 589832 | tf_op jit(solution)/shard_map/ppermute | solution.py:156
  34.9 10.5 %collective-permute-start.18 = (bf16[768,128]{1,0:T(8,128)(2,1)}, bf16[768,128]{1,0:T(8,128)(2,1)}, u32[]{:S(2)}, u32[]{:S(2)}) collective-permute-start(bf16[768,128]{1,0:T(8,128)(2,1)} %collective-permute-done.12.refs_1_), channel_id=1, source_target_pairs={{0,2},{2,4},{4,6},{6,7},{7,5},{5,3},{3,1},{1,0},{8,10},{10,12},{12... | collective-permute-start | bytes 589832 | tf_op jit(solution)/shard_map/ppermute | solution.py:155
  35.2 10.3 %collective-permute-start.19 = (bf16[768,128]{1,0:T(8,128)(2,1)}, bf16[768,128]{1,0:T(8,128)(2,1)}, u32[]{:S(2)}, u32[]{:S(2)}) collective-permute-start(bf16[768,128]{1,0:T(8,128)(2,1)} %collective-permute-done.13.refs_2_), channel_id=1, source_target_pairs={{2,0},{4,2},{6,4},{7,6},{5,7},{3,5},{1,3},{0,1},{10,8},{12,10},{14... | collective-permute-start | bytes 589832 | tf_op jit(solution)/shard_map/ppermute | solution.py:156
  40.4 17.2 %collective-permute-start.9 = (f32[256,256]{1,0:T(8,128)}, f32[256,256]{1,0:T(8,128)}, u32[]{:S(2)}, u32[]{:S(2)}) collective-permute-start(f32[256,256]{1,0:T(8,128)} %get-tuple-element.22), channel_id=1, source_target_pairs={{0,8},{8,0},{16,24},{24,16},{1,9},{9,1},{17,25},{25,17},{2,10},{10... | collective-permute-start | bytes 786440 | tf_op jit(solution)/shard_map/ppermute | solution.py:174
  44.9 17.6 %collective-permute-start.15 = (f32[256,256]{1,0:T(8,128)}, f32[256,256]{1,0:T(8,128)}, u32[]{:S(2)}, u32[]{:S(2)}) collective-permute-start(f32[256,256]{1,0:T(8,128)} %get-tuple-element.24), channel_id=1, source_target_pairs={{0,8},{8,0},{16,24},{24,16},{1,9},{9,1},{17,25},{25,17},{2,10},{10... | collective-permute-start | bytes 786440 | tf_op jit(solution)/shard_map/ppermute | solution.py:174
  49.4 10.0 %copy-start.7 = (s32[16]{0:T(128)S(1)}, s32[16]{0:T(128)}, u32[]{:S(2)}) copy-start(s32[16]{0:T(128)} %param.20) | copy-start | bytes 196
  49.4 16.3 %collective-permute-start.21 = (f32[256,256]{1,0:T(8,128)}, f32[256,256]{1,0:T(8,128)}, u32[]{:S(2)}, u32[]{:S(2)}) collective-permute-start(f32[256,256]{1,0:T(8,128)} %get-tuple-element.26), channel_id=1, source_target_pairs={{0,8},{8,0},{16,24},{24,16},{1,9},{9,1},{17,25},{25,17},{2,10},{10... | collective-permute-start | bytes 786440 | tf_op jit(solution)/shard_map/ppermute | solution.py:174
  56.8 10.4 %collective-permute-start.3 = (f32[128,256]{1,0:T(8,128)}, f32[128,256]{1,0:T(8,128)}, u32[]{:S(2)}, u32[]{:S(2)}) collective-permute-start(f32[128,256]{1,0:T(8,128)} %get-tuple-element.20), channel_id=1, source_target_pairs={{0,8},{8,0},{16,24},{24,16},{1,9},{9,1},{17,25},{25,17},{2,10},{10... | collective-permute-start | bytes 393224 | tf_op jit(solution)/shard_map/ppermute | solution.py:174
  57.3 12.4 %collective-permute-start.23 = (bf16[768,128]{1,0:T(8,128)(2,1)}, bf16[768,128]{1,0:T(8,128)(2,1)S(1)}, u32[]{:S(2)}, u32[]{:S(2)}) collective-permute-start(bf16[768,128]{1,0:T(8,128)(2,1)} %collective-permute-done.17.refs_0_), channel_id=1, source_target_pairs={{0,2},{2,4},{4,6},{6,7},{7,5},{5,3},{3,1},{1,0},{8,10},{10,12},{12... | collective-permute-start | bytes 589832 | tf_op jit(solution)/shard_map/ppermute | solution.py:163
  57.5 12.8 %collective-permute-start.24 = (bf16[768,128]{1,0:T(8,128)(2,1)}, bf16[768,128]{1,0:T(8,128)(2,1)S(1)}, u32[]{:S(2)}, u32[]{:S(2)}) collective-permute-start(bf16[768,128]{1,0:T(8,128)(2,1)} %collective-permute-done.20.refs_3_), channel_id=1, source_target_pairs={{2,0},{4,2},{6,4},{7,6},{5,7},{3,5},{1,3},{0,1},{10,8},{12,10},{14... | collective-permute-start | bytes 589832 | tf_op jit(solution)/shard_map/ppermute | solution.py:164
  62.5 22.0 %collective-permute-start.10 = (f32[256,256]{1,0:T(8,128)}, f32[256,256]{1,0:T(8,128)}, u32[]{:S(2)}, u32[]{:S(2)}) collective-permute-start(f32[256,256]{1,0:T(8,128)} %add.357), channel_id=1, source_target_pairs={{0,16},{8,24},{16,0},{24,8},{1,17},{9,25},{17,1},{25,9},{2,18},{10... | collective-permute-start | bytes 786440 | tf_op jit(solution)/shard_map/ppermute | solution.py:176
  65.6 21.5 %collective-permute-start.16 = (f32[256,256]{1,0:T(8,128)}, f32[256,256]{1,0:T(8,128)}, u32[]{:S(2)}, u32[]{:S(2)}) collective-permute-start(f32[256,256]{1,0:T(8,128)} %add.361), channel_id=1, source_target_pairs={{0,16},{8,24},{16,0},{24,8},{1,17},{9,25},{17,1},{25,9},{2,18},{10... | collective-permute-start | bytes 786440 | tf_op jit(solution)/shard_map/ppermute | solution.py:176
  67.2 21.0 %collective-permute-start.22 = (f32[256,256]{1,0:T(8,128)S(1)}, f32[256,256]{1,0:T(8,128)S(1)}, u32[]{:S(2)}, u32[]{:S(2)}) collective-permute-start(f32[256,256]{1,0:T(8,128)S(1)} %add.365), channel_id=1, source_target_pairs={{0,16},{8,24},{16,0},{24,8},{1,17},{9,25},{17,1},{25,9},{2,18},{10... | collective-permute-start | bytes 786440 | tf_op jit(solution)/shard_map/ppermute | solution.py:176
  69.7 14.7 %collective-permute-start.4 = (f32[128,256]{1,0:T(8,128)S(1)}, f32[128,256]{1,0:T(8,128)S(1)}, u32[]{:S(2)}, u32[]{:S(2)}) collective-permute-start(f32[128,256]{1,0:T(8,128)S(1)} %add.353), channel_id=1, source_target_pairs={{0,16},{8,24},{16,0},{24,8},{1,17},{9,25},{17,1},{25,9},{2,18},{10... | collective-permute-start | bytes 393224 | tf_op jit(solution)/shard_map/ppermute | solution.py:176
  71.9 13.6 %collective-permute-start.25 = (f32[128,256]{1,0:T(8,128)S(1)}, f32[128,256]{1,0:T(8,128)S(1)}, u32[]{:S(2)}, u32[]{:S(2)}) collective-permute-start(f32[128,256]{1,0:T(8,128)S(1)} %get-tuple-element.28), channel_id=1, source_target_pairs={{0,8},{8,0},{16,24},{24,16},{1,9},{9,1},{17,25},{25,17},{2,10},{10... | collective-permute-start | bytes 393224 | tf_op jit(solution)/shard_map/ppermute | solution.py:174
  85.6 5.0 %collective-permute-start.26 = (f32[128,256]{1,0:T(8,128)S(1)}, f32[128,256]{1,0:T(8,128)S(1)}, u32[]{:S(2)}, u32[]{:S(2)}) collective-permute-start(f32[128,256]{1,0:T(8,128)S(1)} %add.368.new), channel_id=1, source_target_pairs={{0,16},{8,24},{16,0},{24,8},{1,17},{9,25},{17,1},{25,9},{2,18},{10... | collective-permute-start | bytes 393224 | tf_op jit(solution)/shard_map/ppermute | solution.py:176
  91.2 1.6 %collective-permute-start.27 = (f32[256,256]{1,0:T(8,128)S(1)}, f32[256,256]{1,0:T(8,128)S(1)}, u32[]{:S(2)}, u32[]{:S(2)}) collective-permute-start(f32[256,256]{1,0:T(8,128)S(1)} %get-tuple-element.30), channel_id=1, source_target_pairs={{0,8},{8,0},{16,24},{24,16},{1,9},{9,1},{17,25},{25,17},{2,10},{10... | collective-permute-start | bytes 786440 | tf_op jit(solution)/shard_map/ppermute | solution.py:201
  (6 other events, 29.3 us)

commit v2 on v0

v2 whole, which is shorter than its diff:
```python
import functools

import jax
import jax.numpy as jnp
from jax import lax
from jax.experimental import pallas as pl
from jax.experimental.pallas import tpu as pltpu
from jax.sharding import PartitionSpec as P

TS = 64
HALF = TS // 2
LANES = 128
SCALE = 16.0
DEAD = 128
VMEM = pl.BlockSpec(memory_space=pltpu.VMEM)
SMEM = pl.BlockSpec(memory_space=pltpu.SMEM)


def ring_order(n):
    return list(range(0, n, 2)) + list(range(n - 1, 0, -2))


def ring_place(d, n):
    return jnp.where(lax.rem(d, 2) == 0, lax.div(d, 2), n - 1 - lax.div(d, 2))


def rows_of(amps):
    tiles, slots, _ = amps.shape
    return amps.reshape(tiles, slots * HALF, 2 * TS)


def marked(ids, count):
    slot = jnp.arange(ids.shape[1], dtype=jnp.int32)[None, :]
    return jnp.where(slot < count, ids, ids + DEAD)


def tile_kernel(n_tiles, ladder_slots, slots, ids_ref, *refs):
    amp_refs = refs[:n_tiles]
    ladder_ref, cycle_ref, out_ref = refs[n_tiles:]
    cols = ladder_ref.shape[1]
    for t in range(n_tiles):
        total = jnp.zeros((TS, cols), jnp.float32)
        for q in range(0, slots, 4):
            left, right = [], []
            for s in range(q, min(q + 4, slots)):
                mark = ids_ref[t * slots + s]
                k = pl.multiple_of(lax.rem(mark, DEAD) * TS, TS)
                panel_ref = ladder_ref if s < ladder_slots else cycle_ref
                right.append(panel_ref[pl.ds(k, TS), :])
                tile = amp_refs[t][s * HALF : (s + 1) * HALF, :]
                tile = jnp.where(mark < DEAD, tile, jnp.zeros_like(tile))
                left.append(jnp.concatenate([tile[:, :TS], tile[:, TS:]], axis=0))
            total += jnp.dot(
                jnp.concatenate(left, axis=1),
                jnp.concatenate(right, axis=0),
                preferred_element_type=jnp.float32,
            )
        for part in range(2):
            for c in range(cols // LANES):
                out_ref[t, c, pl.ds(part, HALF, stride=2), :] = total[
                    part * HALF : (part + 1) * HALF, c * LANES : (c + 1) * LANES
                ]


def tile_products(amps, ids, ladder_panel, cycle_panel, ladder_slots, slots):
    n, cols = len(amps), ladder_panel.shape[1]
    return pl.pallas_call(
        functools.partial(tile_kernel, n, ladder_slots, slots),
        out_shape=jax.ShapeDtypeStruct((n, cols // LANES, TS, LANES), jnp.float32),
        in_specs=[SMEM] + [VMEM] * (n + 2),
        out_specs=VMEM,
        compiler_params=pltpu.CompilerParams(vmem_limit_bytes=10 << 20),
        cost_estimate=pl.CostEstimate(flops=1, bytes_accessed=1, transcendentals=0),
    )(ids, *amps, ladder_panel, cycle_panel)


def arrival(row_tile, place, tiles, n_dev):
    t = lax.rem(row_tile, tiles)
    back = lax.rem(place - ring_place(lax.div(row_tile, tiles), n_dev) + n_dev, n_dev)
    half = n_dev // 2
    ahead = tiles + (back - 1) * 2 * tiles + t
    behind = tiles + (n_dev - back - 1) * 2 * tiles + tiles + t
    last = tiles + (half - 1) * 2 * tiles + t
    slot = jnp.where(back < half, ahead, jnp.where(back > half, behind, last))
    return jnp.where(back == 0, t, slot)


def pick_kernel(tiles, n_dev, n_grp, shifts, n_parts, me_ref, owners_ref, *refs):
    part_refs, out_refs = refs[:n_parts], refs[n_parts:]
    grp, place = me_ref[0], ring_place(me_ref[1], n_dev)
    for shift, out_ref in zip(shifts, out_refs):
        owner = lax.rem(grp + (shift if shift >= 0 else ~shift), n_grp)
        if shift < 0:
            owner = owner + 1 - 2 * lax.rem(owner, 2)
        owned = out_ref.shape[0]
        for i in range(owned):
            slot = arrival(owners_ref[owner * owned + i], place, tiles, n_dev)
            low = 0
            for part_ref in part_refs:
                high = low + part_ref.shape[0]

                @pl.when((slot >= low) & (slot < high))
                def _():
                    out_ref[i] = part_ref[jnp.clip(slot - low, 0, high - low - 1)]

                low = high


def finish_kernel(base_ref, *refs):
    sum_refs, out_ref = refs[:-1], refs[-1]
    for i in range(sum_refs[0].shape[0]):
        for c in range(sum_refs[0].shape[1]):
            at = (slice(i * TS, (i + 1) * TS), slice(c * LANES, (c + 1) * LANES))
            total = sum_refs[0][i, c]
            for ref in sum_refs[1:]:
                total = total + ref[i, c]
            out_ref[at] = base_ref[at] + total


def per_device(
    ladder_amps,
    ladder_ids,
    ladder_count,
    cycle_amps,
    cycle_ids,
    cycle_count,
    ladder_panel,
    cycle_panel,
    owners,
    base,
):
    n_dev, n_grp = lax.axis_size("dev"), lax.axis_size("grp")
    me = jnp.stack([lax.axis_index("grp"), lax.axis_index("dev")])
    tiles, ladder_slots, _ = ladder_amps.shape
    slots = ladder_slots + cycle_amps.shape[1]
    order = ring_order(n_dev)
    forward = [(order[i], order[(i + 1) % n_dev]) for i in range(n_dev)]
    backward = [(b, a) for a, b in forward]
    swap = [(g, g ^ 1) for g in range(n_grp)]

    own = jnp.concatenate([rows_of(ladder_amps), rows_of(cycle_amps)], axis=1)
    marks = jnp.concatenate(
        [marked(ladder_ids, ladder_count), marked(cycle_ids, cycle_count)], axis=1
    ).reshape(1, -1)
    note = jnp.pad(marks.astype(jnp.bfloat16), ((0, 7), (0, 2 * TS - marks.size)))
    own = [jnp.concatenate([own[0], note], axis=0)] + [own[t] for t in range(1, tiles)]

    def marks_of(piece):
        return piece[slots * HALF, : tiles * slots].astype(jnp.int32)

    def products(amps, ids):
        return tile_products(amps, ids, ladder_panel, cycle_panel, ladder_slots, slots)

    cut = tiles // 2
    waves = [(range(cut), range(cut, tiles)), (range(cut, tiles), range(cut))]

    def hop(wave, pieces):
        ahead, behind = waves[wave]
        return {
            **{(0, t): lax.ppermute(pieces[0, t], "dev", forward) for t in ahead},
            **{(1, t): lax.ppermute(pieces[1, t], "dev", backward) for t in behind},
        }

    def landed_products(batches):
        amps = [piece for pieces, _ in batches for piece in pieces]
        return products(amps, jnp.concatenate([marks for _, marks in batches]))

    def batch(landed):
        pieces = [landed[side, t] for side in range(2) for t in range(tiles)]
        return pieces, jnp.concatenate([marks_of(landed[side, 0]) for side in range(2)])

    batches = [(own, marks.reshape(-1))]
    start = {(side, t): own[t] for side in range(2) for t in range(tiles)}
    flying = [hop(wave, start) for wave in range(2)]
    for _ in range(1, n_dev // 2 - 1):
        batches.append(batch({**flying[0], **flying[1]}))
        flying = [hop(wave, flying[wave]) for wave in range(2)]
    first, batches = lax.optimization_barrier((flying[0], batches))
    last = hop(0, first)
    parts = [landed_products(batches[i : i + 3]) for i in range(0, len(batches), 3)]
    second, parts = lax.optimization_barrier((flying[1], parts))
    parts.append(landed_products([batch({**first, **second})]))
    amps = [last[0 if t < cut else 1, t] for t in range(tiles)]
    parts.append(products(amps, marks_of(amps[0])))

    rows, cols = base.shape
    owned = jax.ShapeDtypeStruct((rows // TS, cols // LANES, TS, LANES), jnp.float32)

    def pick(*shifts):
        return pl.pallas_call(
            functools.partial(pick_kernel, tiles, n_dev, n_grp, shifts, len(parts)),
            out_shape=(owned,) * len(shifts),
            in_specs=[SMEM, SMEM] + [VMEM] * len(parts),
            out_specs=(VMEM,) * len(shifts),
            compiler_params=pltpu.CompilerParams(vmem_limit_bytes=10 << 20),
            cost_estimate=pl.CostEstimate(flops=1, bytes_accessed=1, transcendentals=0),
        )(me, owners, *parts)

    others = []
    for shift in range(2, n_grp, 2):
        mine, partners = pick(shift, ~shift)
        chip = mine + lax.ppermute(partners, "grp", swap)
        sent = lax.ppermute(
            (chip * SCALE).astype(jnp.float16), "grp", [(g, (g + shift) % n_grp) for g in range(n_grp)]
        )
        others.append(sent.astype(jnp.float32) * (1 / SCALE))
    mine, partners = pick(0, ~0)
    chip = mine + lax.ppermute(partners, "grp", swap)
    return pl.pallas_call(
        finish_kernel,
        out_shape=jax.ShapeDtypeStruct(base.shape, jnp.float32),
        in_specs=[VMEM] * (2 + len(others)),
        out_specs=VMEM,
        compiler_params=pltpu.CompilerParams(vmem_limit_bytes=10 << 20),
    )(base, chip, *others)


def solution(mesh):
    placed = (
        P("dev", "grp", None),
        P("dev", "grp"),
        P("dev", "grp"),
        P("dev", "grp", None),
        P("dev", "grp"),
        P("dev", "grp"),
        P("grp", "dev"),
        P("grp", "dev"),
        P(),
        P("grp", "dev"),
    )
    return jax.shard_map(
        per_device, mesh=mesh, in_specs=placed, out_specs=P("grp", "dev"), check_vma=False
    )
```

time: 164 us -> 56.3 us (0.34)
  waiting for transfers between devices: 129 us -> 25.8 us
  starting transfers between devices: 0.09 us -> 17.5 us
  between operations: 13.2 us -> 0.25 us
  Pallas kernels: 0 us -> 9.97 us
  local copies, waits for them, and re-layouts: 10.8 us -> 1.83 us
  matrix products: 7.27 us -> 0 us
  other arithmetic: 2.72 us -> 0.82 us
    all_gather x2 -> x0, waiting for transfers between devices: 99.1 us -> none  [the longest x1 59.6 us: per_device(): lax.all_gather(own_ladder, 'dev', axis=0, tiled=True)]
    reduce_scatter x1 -> x0, waiting for transfers between devices: 30.2 us -> none  [per_device(): lax.psum_scatter(result + jnp.dot(cycle_rows, cycle_panel, preferred_elem...]
    ppermute x0 -> x17, waiting for transfers between devices: none -> 25.8 us  [the longest x7 11 us: hop(): lax.ppermute(pieces[1, t], 'dev', backward)]
    ppermute x0 -> x17, starting transfers between devices: none -> 17.5 us  [the longest x7 12.8 us: hop(): lax.ppermute(pieces[1, t], 'dev', backward)]
    pallas_call x0 -> x6, Pallas kernels: none -> 9.97 us  [the longest x3 7.24 us: tile_products(): pl.pallas_call(functools.partial(tile_kernel, n, ladder_slots, slots), ou...]
    dot_general x4 -> x0, matrix products: 7.27 us -> none  [the longest x1 3.72 us: per_device(): jnp.dot(ladder_rows, ladder_panel, preferred_element_type=jnp.float32)]
    gather x2 -> x0, local copies, waits for them, and re-layouts: 6.15 us -> none  [the longest x1 4.31 us: per_device(): all_ladder.reshape(-1, TS, KLT * TS)[owners].reshape(count, KLT * TS)]
    reshape x4 -> x2, local copies, waits for them, and re-layouts: 4.67 us -> 0.32 us  [rows_of(): return amps.reshape(tiles, slots * HALF, 2 * TS)]
  transfers between devices with their start and end apart: 3 -> 17, of which waited for: 3 -> 7; matrix products, arithmetic and copies ran while one was open for 3% -> 1% of each run, Pallas kernels for 0% -> 12%
where the time goes in v2:
time: 56.3 us; the launch traced here: 56.2 us
  waiting for transfers between devices  25.8 us (46%)
  starting transfers between devices  17.5 us (31%)
  Pallas kernels  9.97 us (18%)
  local copies, waits for them, and re-layouts  1.83 us (3%)
  other arithmetic  0.82 us (1%)
    ppermute x7, starting transfers between devices, hop(): lax.ppermute(pieces[1, t], 'dev', backward)  12.8 us
    ppermute x7, waiting for transfers between devices, hop(): lax.ppermute(pieces[1, t], 'dev', backward)  11 us
    ppermute x7, waiting for transfers between devices, hop(): lax.ppermute(pieces[0, t], 'dev', forward)  7.52 us
    pallas_call x3, Pallas kernels, tile_products(): pl.pallas_call(functools.partial(tile_kernel, n, ladder_slots, slots), ou...  7.24 us
    ppermute x1, waiting for transfers between devices, per_device(): lax.ppermute((chip * SCALE).astype(jnp.float16), 'grp', [(g, (g + shift)...  6.79 us
    ppermute x7, starting transfers between devices, hop(): lax.ppermute(pieces[0, t], 'dev', forward)  2.6 us
    pallas_call x2, Pallas kernels, pick(): pl.pallas_call(functools.partial(pick_kernel, tiles, n_dev, n_grp, shifts...  1.84 us
    ppermute x1, starting transfers between devices, per_device(): lax.ppermute((chip * SCALE).astype(jnp.float16), 'grp', [(g, (g + shift)...  1.55 us
  transfers between devices with their start and end apart: 17, of which 7 were waited for; matrix products, arithmetic and copies ran while one was open for 1% of the time, Pallas kernels for 12%

profile of v2, /device:TPU:0, one launch (start us, length us, event | category | flops | bytes accessed | tf_op | source)
XLA Modules:
  0.0 56.2 jit_solution(8974178205214396569)
XLA Ops:
  0.0 1.2 %copy.13 = bf16[2,18,4096]{2,1,0:T(8,128)(2,1)S(1)} copy(bf16[2,18,4096]{2,0,1:T(2,128)(2,1)} %param.10) | data formatting | bytes 589824 | tf_op args[0]
  1.2 0.2 reshape.34
  1.5 0.1 reshape.35
  2.1 3.1 %collective-permute-start.3 = (bf16[776,128]{1,0:T(8,128)(2,1)S(1)}, bf16[776,128]{1,0:T(8,128)(2,1)S(1)}, u32[]{:S(2)}, u32[]{:S(2)}) collective-permute-start(bf16[776,128]{1,0:T(8,128)(2,1)S(1)} %fusion.1.refs_0_), channel_id=1, source_target_pairs={{2,0},{4,2},{6,4},{7,6},{5,7},{3,5},{1,3},{0,1},{10,8},{12,10},{14... | collective-permute-start | bytes 595976 | tf_op jit(solution)/shard_map/ppermute | solution.py:161
  5.1 1.6 %collective-permute-start.9 = (bf16[768,128]{1,0:T(8,128)(2,1)S(1)}, bf16[768,128]{1,0:T(8,128)(2,1)S(1)}, u32[]{:S(2)}, u32[]{:S(2)}) collective-permute-start(bf16[768,128]{1,0:T(8,128)(2,1)S(1)} %get-tuple-element.31.refs_1_), channel_id=1, source_target_pairs={{2,0},{4,2},{6,4},{7,6},{5,7},{3,5},{1,3},{0,1},{10,8},{12,10},{14... | collective-permute-start | bytes 589832 | tf_op jit(solution)/shard_map/ppermute | solution.py:161
  6.7 0.4 collective-permute-start
  7.2 0.1 collective-permute-start.6
  7.4 6.9 %collective-permute-done.9.refs_5_ = bf16[768,128]{1,0:T(8,128)(2,1)S(1)} collective-permute-done((bf16[768,128]{1,0:T(8,128)(2,1)S(1)}, bf16[768,128]{1,0:T(8,128)(2,1)S(1)}, u32[]{:S(2)}, u32[]{:S(2)}) %collective-permute-start.9) | collective-permute-done | bytes 196640 | tf_op jit(solution)/shard_map/ppermute | solution.py:161
  14.4 1.7 %collective-permute-start.10 = (bf16[768,128]{1,0:T(8,128)(2,1)S(1)}, bf16[768,128]{1,0:T(8,128)(2,1)S(1)}, u32[]{:S(2)}, u32[]{:S(2)}) collective-permute-start(bf16[768,128]{1,0:T(8,128)(2,1)S(1)} %collective-permute-done.9.refs_5_), channel_id=1, source_target_pairs={{2,0},{4,2},{6,4},{7,6},{5,7},{3,5},{1,3},{0,1},{10,8},{12,10},{14... | collective-permute-start | bytes 589832 | tf_op jit(solution)/shard_map/ppermute | solution.py:161
  16.0 0.3 collective-permute-start.1
  16.4 1.7 %collective-permute-start.4 = (bf16[776,128]{1,0:T(8,128)(2,1)S(1)}, bf16[776,128]{1,0:T(8,128)(2,1)S(1)}, u32[]{:S(2)}, u32[]{:S(2)}) collective-permute-start(bf16[776,128]{1,0:T(8,128)(2,1)S(1)} %collective-permute-done.3.refs_4_), channel_id=1, source_target_pairs={{2,0},{4,2},{6,4},{7,6},{5,7},{3,5},{1,3},{0,1},{10,8},{12,10},{14... | collective-permute-start | bytes 595976 | tf_op jit(solution)/shard_map/ppermute | solution.py:161
  18.1 0.3 collective-permute-start.7
  18.5 3.7 %collective-permute-done.10.refs_9_ = bf16[768,128]{1,0:T(8,128)(2,1)S(1)} collective-permute-done((bf16[768,128]{1,0:T(8,128)(2,1)S(1)}, bf16[768,128]{1,0:T(8,128)(2,1)S(1)}, u32[]{:S(2)}, u32[]{:S(2)}) %collective-permute-start.10) | collective-permute-done | bytes 196640 | tf_op jit(solution)/shard_map/ppermute | solution.py:161
  22.2 1.7 %collective-permute-start.11 = (bf16[768,128]{1,0:T(8,128)(2,1)S(1)}, bf16[768,128]{1,0:T(8,128)(2,1)S(1)}, u32[]{:S(2)}, u32[]{:S(2)}) collective-permute-start(bf16[768,128]{1,0:T(8,128)(2,1)S(1)} %collective-permute-done.10.refs_9_), channel_id=1, source_target_pairs={{2,0},{4,2},{6,4},{7,6},{5,7},{3,5},{1,3},{0,1},{10,8},{12,10},{14... | collective-permute-start | bytes 589832 | tf_op jit(solution)/shard_map/ppermute | solution.py:161
  23.9 0.3 collective-permute-start.2
  24.2 3.9 %collective-permute-done.7.refs_6_ = bf16[776,128]{1,0:T(8,128)(2,1)S(1)} collective-permute-done((bf16[776,128]{1,0:T(8,128)(2,1)S(1)}, bf16[776,128]{1,0:T(8,128)(2,1)S(1)}, u32[]{:S(2)}, u32[]{:S(2)}) %collective-permute-start.7) | collective-permute-done | bytes 198688 | tf_op jit(solution)/shard_map/ppermute | solution.py:160
  28.1 0.3 collective-permute-start.8
  28.5 1.7 %collective-permute-start.5 = (bf16[776,128]{1,0:T(8,128)(2,1)S(1)}, bf16[776,128]{1,0:T(8,128)(2,1)S(1)}, u32[]{:S(2)}, u32[]{:S(2)}) collective-permute-start(bf16[776,128]{1,0:T(8,128)(2,1)S(1)} %collective-permute-done.4.refs_8_), channel_id=1, source_target_pairs={{2,0},{4,2},{6,4},{7,6},{5,7},{3,5},{1,3},{0,1},{10,8},{12,10},{14... | collective-permute-start | bytes 595976 | tf_op jit(solution)/shard_map/ppermute | solution.py:161
  30.3 0.4 collective-permute-done.11.refs_3_
  30.7 3.6 %collective-permute-done.8.refs_0_ = bf16[776,128]{1,0:T(8,128)(2,1)S(1)} collective-permute-done((bf16[776,128]{1,0:T(8,128)(2,1)S(1)}, bf16[776,128]{1,0:T(8,128)(2,1)S(1)}, u32[]{:S(2)}, u32[]{:S(2)}) %collective-permute-start.8) | collective-permute-done | bytes 198688 | tf_op jit(solution)/shard_map/ppermute | solution.py:160
  34.3 0.7 %collective-permute-start.12 = (bf16[776,128]{1,0:T(8,128)(2,1)S(1)}, bf16[776,128]{1,0:T(8,128)(2,1)S(1)}, u32[]{:S(2)}, u32[]{:S(2)}) collective-permute-start(bf16[776,128]{1,0:T(8,128)(2,1)S(1)} %collective-permute-done.8.refs_0_), channel_id=1, source_target_pairs={{0,2},{2,4},{4,6},{6,7},{7,5},{5,3},{3,1},{1,0},{8,10},{10,12},{12... | collective-permute-start | bytes 595976 | tf_op jit(solution)/shard_map/ppermute | solution.py:160
  34.9 1.4 %collective-permute-start.13 = (bf16[768,128]{1,0:T(8,128)(2,1)S(1)}, bf16[768,128]{1,0:T(8,128)(2,1)S(1)}, u32[]{:S(2)}, u32[]{:S(2)}) collective-permute-start(bf16[768,128]{1,0:T(8,128)(2,1)S(1)} %collective-permute-done.11.refs_3_), channel_id=1, source_target_pairs={{2,0},{4,2},{6,4},{7,6},{5,7},{3,5},{1,3},{0,1},{10,8},{12,10},{14... | collective-permute-start | bytes 589832 | tf_op jit(solution)/shard_map/ppermute | solution.py:161
  36.4 3.9 %shard_map.100.refs_0_ = f32[10,4,64,128]{3,2,1,0:T(8,128)S(1)} custom-call(s32[240]{0:T(256)S(1)} %pad_add_fusion.1.ids_ref, bf16[776,128]{1,0:T(8,128)(2,1)S(1)} %fusion.1.refs_0_, bf16[768,128]{1,0:T(8,128)(2,1)S(1)} %get-tuple-element.31.refs_1_, bf16[776,128]{1,0:T(8,128)(2,1)S(1)} %collective-permute-done.6.refs_2_, ...), custom_call_target="tpu_custom_call" | custom-call | flops 1 | bytes 1 | tf_op jit(solution)/shard_map/pallas_call | solution.py:67
  40.4 2.0 %shard_map.101.refs_1_ = f32[4,4,64,128]{3,2,1,0:T(8,128)S(1)} custom-call(s32[96]{0:T(128)S(1)} %maximum_convert_fusion.2.ids_ref, bf16[776,128]{1,0:T(8,128)(2,1)S(1)} %collective-permute-done.8.refs_0_, bf16[768,128]{1,0:T(8,128)(2,1)S(1)} %collective-permute-done.2.refs_1_, bf16[776,128]{1,0:T(8,128)(2,1)S(1)} %collective-permute-done.5.refs_2_, ...), custom_call_target="tpu_custom_call" | custom-call | flops 1 | bytes 1 | tf_op jit(solution)/shard_map/pallas_call | solution.py:67
  42.4 1.3 %shard_map.102.refs_2_ = f32[2,4,64,128]{3,2,1,0:T(8,128)S(1)} custom-call(s32[48]{0:T(128)S(1)} %fusion.2.ids_ref, bf16[776,128]{1,0:T(8,128)(2,1)S(1)} %collective-permute-done.12.refs_0_, bf16[768,128]{1,0:T(8,128)(2,1)S(1)} %collective-permute-done.13.refs_1_, bf16[1536,512]{1,0:T(8,128)(2,1)S(1)} %copy-done, bf16[512,512]{1,0:T(8,128)(2,1)S(1)} %copy-done.1), custom_call_target="tpu_custom_call" | custom-call | flops 1 | bytes 1 | tf_op jit(solution)/shard_map/pallas_call | solution.py:67
  43.8 0.9 %shard_map.104 = (f32[4,4,64,128]{3,2,1,0:T(8,128)S(1)}, f32[4,4,64,128]{3,2,1,0:T(8,128)S(1)}) custom-call(s32[2]{0:T(128)S(1)} %pad_add_fusion.2.me_ref, s32[16]{0:T(128)S(1)} %copy-done.3, f32[10,4,64,128]{3,2,1,0:T(8,128)S(1)} %shard_map.100.refs_0_, f32[4,4,64,128]{3,2,1,0:T(8,128)S(1)} %shard_map.101.refs_1_, f32[2,4,64,128]{3,2,1,0:T(8,128)S(1)} %shard_map.102.refs_2_), custom_call_target="tpu_custom_call" | custom-call | flops 1 | bytes 1 | tf_op jit(solution)/shard_map/pallas_call | solution.py:190
  44.8 0.9 %shard_map.103 = (f32[4,4,64,128]{3,2,1,0:T(8,128)S(1)}, f32[4,4,64,128]{3,2,1,0:T(8,128)S(1)}) custom-call(s32[2]{0:T(128)S(1)} %pad_add_fusion.2.me_ref, s32[16]{0:T(128)S(1)} %copy-done.3, f32[10,4,64,128]{3,2,1,0:T(8,128)S(1)} %shard_map.100.refs_0_, f32[4,4,64,128]{3,2,1,0:T(8,128)S(1)} %shard_map.101.refs_1_, f32[2,4,64,128]{3,2,1,0:T(8,128)S(1)} %shard_map.102.refs_2_), custom_call_target="tpu_custom_call" | custom-call | flops 1 | bytes 1 | tf_op jit(solution)/shard_map/pallas_call | solution.py:190
  45.7 0.6 collective-permute-start.14
  46.3 0.4 collective-permute-done.15
  46.8 1.6 %collective-permute-start.16 = (f16[4,4,64,128]{3,2,1,0:T(8,128)(2,1)S(1)}, f16[4,4,64,128]{3,2,1,0:T(8,128)(2,1)S(1)}, u32[]{:S(2)}, u32[]{:S(2)}) collective-permute-start(f16[4,4,64,128]{3,2,1,0:T(8,128)(2,1)S(1)} %multiply_convert_fusion), channel_id=1, source_target_pairs={{0,16},{8,24},{16,0},{24,8},{1,17},{9,25},{17,1},{25,9},{2,18},{10... | collective-permute-start | bytes 786440 | tf_op jit(solution)/shard_map/ppermute | solution.py:203
  48.4 6.8 %collective-permute-done.16 = f16[4,4,64,128]{3,2,1,0:T(8,128)(2,1)S(1)} collective-permute-done((f16[4,4,64,128]{3,2,1,0:T(8,128)(2,1)S(1)}, f16[4,4,64,128]{3,2,1,0:T(8,128)(2,1)S(1)}, u32[]{:S(2)}, u32[]{:S(2)}) %collective-permute-start.16) | collective-permute-done | bytes 262176 | tf_op jit(solution)/shard_map/ppermute | solution.py:203
  55.3 0.9 %shard_map.105 = f32[256,512]{1,0:T(8,128)} custom-call(f32[256,512]{1,0:T(8,128)S(1)} %copy-done.2, f32[4,4,64,128]{3,2,1,0:T(8,128)S(1)} %add.20.refs_0_, f32[4,4,64,128]{3,2,1,0:T(8,128)S(1)} %convert_multiply_fusion.refs_1_), custom_call_target="tpu_custom_call" | custom-call | tf_op jit(solution)/shard_map/pallas_call | solution.py:209
  (54 shorter events, 1.3 us)
Async XLA Ops:
  0.0 1.4 %copy-start.4 = (bf16[2,6,4096]{2,0,1:T(2,128)(2,1)S(1)}, bf16[2,6,4096]{2,0,1:T(2,128)(2,1)}, u32[]{:S(2)}) copy-start(bf16[2,6,4096]{2,0,1:T(2,128)(2,1)} %param.13) | copy-start | bytes 294916
  0.0 1.7 %copy-start.7 = (s32[2,1]{0,1:T(1,128)S(1)}, s32[2,1]{0,1:T(1,128)}, u32[]{:S(2)}) copy-start(s32[2,1]{0,1:T(1,128)} %param.15) | copy-start | bytes 28
  0.0 1.7 %copy-start.5 = (s32[2,6]{1,0:T(2,128)S(1)}, s32[2,6]{1,0:T(2,128)}, u32[]{:S(2)}) copy-start(s32[2,6]{1,0:T(2,128)} %param.14) | copy-start | bytes 148
  0.0 1.8 %copy-start.8 = (s32[2,1]{0,1:T(1,128)S(1)}, s32[2,1]{0,1:T(1,128)}, u32[]{:S(2)}) copy-start(s32[2,1]{0,1:T(1,128)} %param.12) | copy-start | bytes 28
  0.0 1.8 %copy-start.6 = (s32[2,18]{1,0:T(2,128)S(1)}, s32[2,18]{1,0:T(2,128)}, u32[]{:S(2)}) copy-start(s32[2,18]{1,0:T(2,128)} %param.11) | copy-start | bytes 436
  1.2 35.2 %copy-start = (bf16[1536,512]{1,0:T(8,128)(2,1)S(1)}, bf16[1536,512]{1,0:T(8,128)(2,1)}, u32[]{:S(2)}) copy-start(bf16[1536,512]{1,0:T(8,128)(2,1)} %refs_2_.1) | copy-start | bytes 4718596
  1.2 35.2 %copy-start.1 = (bf16[512,512]{1,0:T(8,128)(2,1)S(1)}, bf16[512,512]{1,0:T(8,128)(2,1)}, u32[]{:S(2)}) copy-start(bf16[512,512]{1,0:T(8,128)(2,1)} %refs_3_.1) | copy-start | bytes 1572868
  2.1 14.3 %collective-permute-start.3 = (bf16[776,128]{1,0:T(8,128)(2,1)S(1)}, bf16[776,128]{1,0:T(8,128)(2,1)S(1)}, u32[]{:S(2)}, u32[]{:S(2)}) collective-permute-start(bf16[776,128]{1,0:T(8,128)(2,1)S(1)} %fusion.1.refs_0_), channel_id=1, source_target_pairs={{2,0},{4,2},{6,4},{7,6},{5,7},{3,5},{1,3},{0,1},{10,8},{12,10},{14... | collective-permute-start | bytes 595976 | tf_op jit(solution)/shard_map/ppermute | solution.py:161
  5.1 9.2 %collective-permute-start.9 = (bf16[768,128]{1,0:T(8,128)(2,1)S(1)}, bf16[768,128]{1,0:T(8,128)(2,1)S(1)}, u32[]{:S(2)}, u32[]{:S(2)}) collective-permute-start(bf16[768,128]{1,0:T(8,128)(2,1)S(1)} %get-tuple-element.31.refs_1_), channel_id=1, source_target_pairs={{2,0},{4,2},{6,4},{7,6},{5,7},{3,5},{1,3},{0,1},{10,8},{12,10},{14... | collective-permute-start | bytes 589832 | tf_op jit(solution)/shard_map/ppermute | solution.py:161
  6.7 9.3 %collective-permute-start = (bf16[768,128]{1,0:T(8,128)(2,1)S(1)}, bf16[768,128]{1,0:T(8,128)(2,1)S(1)}, u32[]{:S(2)}, u32[]{:S(2)}) collective-permute-start(bf16[768,128]{1,0:T(8,128)(2,1)S(1)} %get-tuple-element.31.refs_1_), channel_id=1, source_target_pairs={{0,2},{2,4},{4,6},{6,7},{7,5},{5,3},{3,1},{1,0},{8,10},{10,12},{12... | collective-permute-start | bytes 589832 | tf_op jit(solution)/shard_map/ppermute | solution.py:160
  7.2 10.9 %collective-permute-start.6 = (bf16[776,128]{1,0:T(8,128)(2,1)S(1)}, bf16[776,128]{1,0:T(8,128)(2,1)S(1)}, u32[]{:S(2)}, u32[]{:S(2)}) collective-permute-start(bf16[776,128]{1,0:T(8,128)(2,1)S(1)} %fusion.1.refs_0_), channel_id=1, source_target_pairs={{0,2},{2,4},{4,6},{6,7},{7,5},{5,3},{3,1},{1,0},{8,10},{10,12},{12... | collective-permute-start | bytes 595976 | tf_op jit(solution)/shard_map/ppermute | solution.py:160
  14.4 7.8 %collective-permute-start.10 = (bf16[768,128]{1,0:T(8,128)(2,1)S(1)}, bf16[768,128]{1,0:T(8,128)(2,1)S(1)}, u32[]{:S(2)}, u32[]{:S(2)}) collective-permute-start(bf16[768,128]{1,0:T(8,128)(2,1)S(1)} %collective-permute-done.9.refs_5_), channel_id=1, source_target_pairs={{2,0},{4,2},{6,4},{7,6},{5,7},{3,5},{1,3},{0,1},{10,8},{12,10},{14... | collective-permute-start | bytes 589832 | tf_op jit(solution)/shard_map/ppermute | solution.py:161
  16.0 7.8 %collective-permute-start.1 = (bf16[768,128]{1,0:T(8,128)(2,1)S(1)}, bf16[768,128]{1,0:T(8,128)(2,1)S(1)}, u32[]{:S(2)}, u32[]{:S(2)}) collective-permute-start(bf16[768,128]{1,0:T(8,128)(2,1)S(1)} %collective-permute-done.refs_3_), channel_id=1, source_target_pairs={{0,2},{2,4},{4,6},{6,7},{7,5},{5,3},{3,1},{1,0},{8,10},{10,12},{12... | collective-permute-start | bytes 589832 | tf_op jit(solution)/shard_map/ppermute | solution.py:160
  16.4 12.1 %collective-permute-start.4 = (bf16[776,128]{1,0:T(8,128)(2,1)S(1)}, bf16[776,128]{1,0:T(8,128)(2,1)S(1)}, u32[]{:S(2)}, u32[]{:S(2)}) collective-permute-start(bf16[776,128]{1,0:T(8,128)(2,1)S(1)} %collective-permute-done.3.refs_4_), channel_id=1, source_target_pairs={{2,0},{4,2},{6,4},{7,6},{5,7},{3,5},{1,3},{0,1},{10,8},{12,10},{14... | collective-permute-start | bytes 595976 | tf_op jit(solution)/shard_map/ppermute | solution.py:161
  18.1 10.1 %collective-permute-start.7 = (bf16[776,128]{1,0:T(8,128)(2,1)S(1)}, bf16[776,128]{1,0:T(8,128)(2,1)S(1)}, u32[]{:S(2)}, u32[]{:S(2)}) collective-permute-start(bf16[776,128]{1,0:T(8,128)(2,1)S(1)} %collective-permute-done.6.refs_2_), channel_id=1, source_target_pairs={{0,2},{2,4},{4,6},{6,7},{7,5},{5,3},{3,1},{1,0},{8,10},{10,12},{12... | collective-permute-start | bytes 595976 | tf_op jit(solution)/shard_map/ppermute | solution.py:160
  22.2 8.5 %collective-permute-start.11 = (bf16[768,128]{1,0:T(8,128)(2,1)S(1)}, bf16[768,128]{1,0:T(8,128)(2,1)S(1)}, u32[]{:S(2)}, u32[]{:S(2)}) collective-permute-start(bf16[768,128]{1,0:T(8,128)(2,1)S(1)} %collective-permute-done.10.refs_9_), channel_id=1, source_target_pairs={{2,0},{4,2},{6,4},{7,6},{5,7},{3,5},{1,3},{0,1},{10,8},{12,10},{14... | collective-permute-start | bytes 589832 | tf_op jit(solution)/shard_map/ppermute | solution.py:161
  23.9 16.4 %collective-permute-start.2 = (bf16[768,128]{1,0:T(8,128)(2,1)S(1)}, bf16[768,128]{1,0:T(8,128)(2,1)S(1)}, u32[]{:S(2)}, u32[]{:S(2)}) collective-permute-start(bf16[768,128]{1,0:T(8,128)(2,1)S(1)} %collective-permute-done.1.refs_7_), channel_id=1, source_target_pairs={{0,2},{2,4},{4,6},{6,7},{7,5},{5,3},{3,1},{1,0},{8,10},{10,12},{12... | collective-permute-start | bytes 589832 | tf_op jit(solution)/shard_map/ppermute | solution.py:160
  28.1 6.1 %collective-permute-start.8 = (bf16[776,128]{1,0:T(8,128)(2,1)S(1)}, bf16[776,128]{1,0:T(8,128)(2,1)S(1)}, u32[]{:S(2)}, u32[]{:S(2)}) collective-permute-start(bf16[776,128]{1,0:T(8,128)(2,1)S(1)} %collective-permute-done.7.refs_6_), channel_id=1, source_target_pairs={{0,2},{2,4},{4,6},{6,7},{7,5},{5,3},{3,1},{1,0},{8,10},{10,12},{12... | collective-permute-start | bytes 595976 | tf_op jit(solution)/shard_map/ppermute | solution.py:160
  28.5 11.8 %collective-permute-start.5 = (bf16[776,128]{1,0:T(8,128)(2,1)S(1)}, bf16[776,128]{1,0:T(8,128)(2,1)S(1)}, u32[]{:S(2)}, u32[]{:S(2)}) collective-permute-start(bf16[776,128]{1,0:T(8,128)(2,1)S(1)} %collective-permute-done.4.refs_8_), channel_id=1, source_target_pairs={{2,0},{4,2},{6,4},{7,6},{5,7},{3,5},{1,3},{0,1},{10,8},{12,10},{14... | collective-permute-start | bytes 595976 | tf_op jit(solution)/shard_map/ppermute | solution.py:161
  34.3 8.2 %collective-permute-start.12 = (bf16[776,128]{1,0:T(8,128)(2,1)S(1)}, bf16[776,128]{1,0:T(8,128)(2,1)S(1)}, u32[]{:S(2)}, u32[]{:S(2)}) collective-permute-start(bf16[776,128]{1,0:T(8,128)(2,1)S(1)} %collective-permute-done.8.refs_0_), channel_id=1, source_target_pairs={{0,2},{2,4},{4,6},{6,7},{7,5},{5,3},{3,1},{1,0},{8,10},{10,12},{12... | collective-permute-start | bytes 595976 | tf_op jit(solution)/shard_map/ppermute | solution.py:160
  34.9 7.5 %collective-permute-start.13 = (bf16[768,128]{1,0:T(8,128)(2,1)S(1)}, bf16[768,128]{1,0:T(8,128)(2,1)S(1)}, u32[]{:S(2)}, u32[]{:S(2)}) collective-permute-start(bf16[768,128]{1,0:T(8,128)(2,1)S(1)} %collective-permute-done.11.refs_3_), channel_id=1, source_target_pairs={{2,0},{4,2},{6,4},{7,6},{5,7},{3,5},{1,3},{0,1},{10,8},{12,10},{14... | collective-permute-start | bytes 589832 | tf_op jit(solution)/shard_map/ppermute | solution.py:161
  42.4 1.4 %copy-start.3 = (s32[16]{0:T(128)S(1)}, s32[16]{0:T(128)}, u32[]{:S(2)}) copy-start(s32[16]{0:T(128)} %owners_ref.3) | copy-start | bytes 196
  44.7 2.0 %collective-permute-start.15 = (f32[4,4,64,128]{3,2,1,0:T(8,128)S(1)}, f32[4,4,64,128]{3,2,1,0:T(8,128)S(1)}, u32[]{:S(2)}, u32[]{:S(2)}) collective-permute-start(f32[4,4,64,128]{3,2,1,0:T(8,128)S(1)} %get-tuple-element.48), channel_id=1, source_target_pairs={{0,8},{8,0},{16,24},{24,16},{1,9},{9,1},{17,25},{25,17},{2,10},{10... | collective-permute-start | bytes 1572872 | tf_op jit(solution)/shard_map/ppermute | solution.py:202
  45.7 2.6 %collective-permute-start.14 = (f32[4,4,64,128]{3,2,1,0:T(8,128)S(1)}, f32[4,4,64,128]{3,2,1,0:T(8,128)S(1)}, u32[]{:S(2)}, u32[]{:S(2)}) collective-permute-start(f32[4,4,64,128]{3,2,1,0:T(8,128)S(1)} %get-tuple-element.46), channel_id=1, source_target_pairs={{0,8},{8,0},{16,24},{24,16},{1,9},{9,1},{17,25},{25,17},{2,10},{10... | collective-permute-start | bytes 1572872 | tf_op jit(solution)/shard_map/ppermute | solution.py:208
  46.7 8.6 %copy-start.2 = (f32[256,512]{1,0:T(8,128)S(1)}, f32[256,512]{1,0:T(8,128)}, u32[]{:S(2)}) copy-start(f32[256,512]{1,0:T(8,128)} %base_ref.1) | copy-start | bytes 1572868
  46.8 8.4 %collective-permute-start.16 = (f16[4,4,64,128]{3,2,1,0:T(8,128)(2,1)S(1)}, f16[4,4,64,128]{3,2,1,0:T(8,128)(2,1)S(1)}, u32[]{:S(2)}, u32[]{:S(2)}) collective-permute-start(f16[4,4,64,128]{3,2,1,0:T(8,128)(2,1)S(1)} %multiply_convert_fusion), channel_id=1, source_target_pairs={{0,16},{8,24},{16,0},{24,8},{1,17},{9,25},{17,1},{25,9},{2,18},{10... | collective-permute-start | bytes 786440 | tf_op jit(solution)/shard_map/ppermute | solution.py:203

commit v3 on v2

v3 whole, which is shorter than its diff:
```python
import functools

import jax
import jax.numpy as jnp
from jax import lax
from jax.experimental import pallas as pl
from jax.experimental.pallas import tpu as pltpu
from jax.sharding import PartitionSpec as P

TS = 64
HALF = TS // 2
LANES = 128
SCALE = 16.0
DEAD = 128
VMEM = pl.BlockSpec(memory_space=pltpu.VMEM)
SMEM = pl.BlockSpec(memory_space=pltpu.SMEM)


def ring_order(n):
    return list(range(0, n, 2)) + list(range(n - 1, 0, -2))


def ring_place(d, n):
    return jnp.where(lax.rem(d, 2) == 0, lax.div(d, 2), n - 1 - lax.div(d, 2))


def rows_of(amps):
    tiles, slots, _ = amps.shape
    return amps.reshape(tiles, slots * HALF, 2 * TS)


def marked(ids, count):
    slot = jnp.arange(ids.shape[1], dtype=jnp.int32)[None, :]
    return jnp.where(slot < count, ids, ids + DEAD)


def multiply(ids_ref, amp_refs, ladder_ref, cycle_ref, ladder_slots, slots, rows_ref, out_ref):
    cols = ladder_ref.shape[1]
    for t, amp_ref in enumerate(amp_refs):
        total = jnp.zeros((TS, cols), jnp.float32)
        for q in range(0, slots, 4):
            left, right = [], []
            for s in range(q, min(q + 4, slots)):
                mark = ids_ref[t * slots + s]
                k = pl.multiple_of(lax.rem(mark, DEAD) * TS, TS)
                panel_ref = ladder_ref if s < ladder_slots else cycle_ref
                right.append(panel_ref[pl.ds(k, TS), :])
                tile = amp_ref[s * HALF : (s + 1) * HALF, :]
                tile = jnp.where(mark < DEAD, tile, jnp.zeros_like(tile))
                left.append(jnp.concatenate([tile[:, :TS], tile[:, TS:]], axis=0))
            total += jnp.dot(
                jnp.concatenate(left, axis=1),
                jnp.concatenate(right, axis=0),
                preferred_element_type=jnp.float32,
            )
        for c in range(cols // LANES):
            lanes = slice(c * LANES, (c + 1) * LANES)
            for part in range(2):
                rows_ref[t % 2, c, pl.ds(part, HALF, stride=2), :] = total[
                    part * HALF : (part + 1) * HALF, lanes
                ]
            out_ref[t * TS : (t + 1) * TS, lanes] = rows_ref[t % 2, c]


def pick(slot_ref, first, part_refs, out_ref):
    for i in range(out_ref.shape[0] // TS):
        slot = slot_ref[first + i]
        low = 0
        for part_ref in part_refs:
            high = low + part_ref.shape[0] // TS

            @pl.when((slot >= low) & (slot < high))
            def _():
                at = pl.multiple_of(jnp.clip(slot - low, 0, high - low - 1) * TS, TS)
                out_ref[i * TS : (i + 1) * TS, :] = part_ref[pl.ds(at, TS), :]

            low = high


def tile_kernel(n, ladder_slots, slots, ids_ref, *refs):
    ladder_ref, cycle_ref, out_ref, rows_ref = refs[n:]
    multiply(ids_ref, refs[:n], ladder_ref, cycle_ref, ladder_slots, slots, rows_ref, out_ref)


def last_kernel(n, ladder_slots, slots, n_parts, ids_ref, slot_ref, *refs):
    amp_refs, (ladder_ref, cycle_ref), part_refs = refs[:n], refs[n : n + 2], refs[n + 2 :][:n_parts]
    late_ref, *out_refs, rows_ref = refs[n + 2 + n_parts :]
    multiply(ids_ref, amp_refs, ladder_ref, cycle_ref, ladder_slots, slots, rows_ref, late_ref)
    first = 0
    for out_ref in out_refs:
        pick(slot_ref, first, part_refs + (late_ref,), out_ref)
        first += out_ref.shape[0] // TS


def own_kernel(first, n_parts, slot_ref, *refs):
    for out_ref in refs[n_parts:]:
        pick(slot_ref, first, refs[:n_parts], out_ref)
        first += out_ref.shape[0] // TS


def call(kernel, out_shape, n_smem, args, scratch=()):
    return pl.pallas_call(
        kernel,
        out_shape=out_shape,
        in_specs=[SMEM] * n_smem + [VMEM] * (len(args) - n_smem),
        out_specs=jax.tree.map(lambda _: VMEM, out_shape),
        scratch_shapes=list(scratch),
        compiler_params=pltpu.CompilerParams(vmem_limit_bytes=12 << 20),
        cost_estimate=pl.CostEstimate(flops=1, bytes_accessed=1, transcendentals=0),
    )(*args)


def arrival(row_tile, place, tiles, n_dev):
    t = lax.rem(row_tile, tiles)
    back = lax.rem(place - ring_place(lax.div(row_tile, tiles), n_dev) + n_dev, n_dev)
    half = n_dev // 2
    ahead = tiles + (back - 1) * 2 * tiles + t
    behind = tiles + (n_dev - back - 1) * 2 * tiles + tiles + t
    last = tiles + (half - 1) * 2 * tiles + t
    slot = jnp.where(back < half, ahead, jnp.where(back > half, behind, last))
    return jnp.where(back == 0, t, slot)


def per_device(
    ladder_amps,
    ladder_ids,
    ladder_count,
    cycle_amps,
    cycle_ids,
    cycle_count,
    ladder_panel,
    cycle_panel,
    owners,
    base,
):
    n_dev, n_grp = lax.axis_size("dev"), lax.axis_size("grp")
    tiles, ladder_slots, _ = ladder_amps.shape
    slots = ladder_slots + cycle_amps.shape[1]
    order = ring_order(n_dev)
    forward = [(order[i], order[(i + 1) % n_dev]) for i in range(n_dev)]
    backward = [(b, a) for a, b in forward]
    swap = [(g, g ^ 1) for g in range(n_grp)]

    own = jnp.concatenate([rows_of(ladder_amps), rows_of(cycle_amps)], axis=1)
    marks = jnp.concatenate(
        [marked(ladder_ids, ladder_count), marked(cycle_ids, cycle_count)], axis=1
    ).reshape(1, -1)
    note = jnp.pad(marks.astype(jnp.bfloat16), ((0, 7), (0, 2 * TS - marks.size)))
    own = [jnp.concatenate([own[0], note], axis=0)] + [own[t] for t in range(1, tiles)]

    def marks_of(piece):
        return piece[slots * HALF, : tiles * slots].astype(jnp.int32)

    cols = base.shape[1]
    rows_scratch = [pltpu.VMEM((2, cols // LANES, TS, LANES), jnp.float32)]

    def products(amps, ids):
        return call(
            functools.partial(tile_kernel, len(amps), ladder_slots, slots),
            jax.ShapeDtypeStruct((len(amps) * TS, cols), jnp.float32),
            1,
            [ids, *amps, ladder_panel, cycle_panel],
            rows_scratch,
        )

    grp, place = lax.axis_index("grp"), ring_place(lax.axis_index("dev"), n_dev)
    owned = owners.shape[0] // n_grp
    slot_of = arrival(owners, place, tiles, n_dev).reshape(n_grp, owned)
    shifts = [*range(2, n_grp, 2), 0]
    ahead = (grp + jnp.array(shifts, jnp.int32)) % n_grp
    chosen = jnp.stack([ahead, ahead ^ 1], axis=1).reshape(-1, 1)
    picked = chosen == jnp.arange(n_grp, dtype=jnp.int32)[None, :]
    slot_of = jnp.sum(jnp.where(picked[:, :, None], slot_of[None], 0), axis=1).reshape(-1)

    cut = tiles // 2
    waves = [(range(cut), range(cut, tiles)), (range(cut, tiles), range(cut))]

    def hop(wave, pieces):
        ahead, behind = waves[wave]
        return {
            **{(0, t): lax.ppermute(pieces[0, t], "dev", forward) for t in ahead},
            **{(1, t): lax.ppermute(pieces[1, t], "dev", backward) for t in behind},
        }

    def batch(landed):
        pieces = [landed[side, t] for side in range(2) for t in range(tiles)]
        return pieces, jnp.concatenate([marks_of(landed[side, 0]) for side in range(2)])

    start = {(side, t): own[t] for side in range(2) for t in range(tiles)}
    flying = [hop(wave, start) for wave in range(2)]
    parts = [products(own, marks.reshape(-1))]
    for _ in range(1, n_dev // 2 - 1):
        first, parts = lax.optimization_barrier((flying[0], parts))
        landed = batch({**first, **flying[1]})
        flying = [hop(0, first), hop(1, flying[1])]
        parts.append(products(*landed))
    first, parts = lax.optimization_barrier((flying[0], parts))
    last = hop(0, first)
    parts.append(products(*batch({**first, **flying[1]})))
    amps = [last[0 if t < cut else 1, t] for t in range(tiles)]
    tile_rows = jax.ShapeDtypeStruct((owned * TS, cols), jnp.float32)
    late, *rows_for = call(
        functools.partial(last_kernel, len(amps), ladder_slots, slots, len(parts)),
        (jax.ShapeDtypeStruct((len(amps) * TS, cols), jnp.float32),) + (tile_rows,) * (n_grp - 2),
        2,
        [marks_of(amps[0]), slot_of, *amps, ladder_panel, cycle_panel, *parts],
        rows_scratch,
    )
    total = base
    for k, shift in enumerate(shifts[:-1]):
        chip = rows_for[2 * k] + lax.ppermute(rows_for[2 * k + 1], "grp", swap)
        sent = lax.ppermute(
            (chip * SCALE).astype(jnp.float16), "grp", [(g, (g + shift) % n_grp) for g in range(n_grp)]
        )
        total = total + sent.astype(jnp.float32) * (1 / SCALE)
    mine, partners = call(
        functools.partial(own_kernel, (n_grp - 2) * owned, len(parts) + 1),
        (tile_rows, tile_rows),
        1,
        [slot_of, *parts, late],
    )
    return total + (mine + lax.ppermute(partners, "grp", swap))


def solution(mesh):
    placed = (
        P("dev", "grp", None),
        P("dev", "grp"),
        P("dev", "grp"),
        P("dev", "grp", None),
        P("dev", "grp"),
        P("dev", "grp"),
        P("grp", "dev"),
        P("grp", "dev"),
        P(),
        P("grp", "dev"),
    )
    return jax.shard_map(
        per_device, mesh=mesh, in_specs=placed, out_specs=P("grp", "dev"), check_vma=False
    )
```

time: 56.3 us -> 54.5 us (0.968)
  waiting for transfers between devices: 25.8 us -> 17.5 us
  other arithmetic: 0.82 us -> 4.02 us
  local copies, waits for them, and re-layouts: 1.83 us -> 3.52 us
  starting transfers between devices: 17.5 us -> 19 us
    ppermute x7, starting transfers between devices: 2.6 us -> 11.8 us  [hop(): lax.ppermute(pieces[0, t], 'dev', forward)]
    ppermute x7, starting transfers between devices: 12.8 us -> 5.07 us  [hop(): lax.ppermute(pieces[1, t], 'dev', backward)]
    ppermute x7, waiting for transfers between devices: 11 us -> 5.29 us  [hop(): lax.ppermute(pieces[1, t], 'dev', backward)]
    ppermute x7, waiting for transfers between devices: 7.52 us -> 4.95 us  [hop(): lax.ppermute(pieces[0, t], 'dev', forward)]
    reduce_sum x0 -> x1, other arithmetic: none -> 1.29 us  [per_device(): jnp.sum(jnp.where(picked[:, :, None], slot_of[None], 0), axis=1).reshape(-1)]
    add x1, other arithmetic: 0.06 us -> 0.98 us  [per_device(): return total + (mine + lax.ppermute(partners, 'grp', swap))]
    reshape x0 -> x1, local copies, waits for them, and re-layouts: none -> 0.76 us  [per_device(): jnp.sum(jnp.where(picked[:, :, None], slot_of[None], 0), axis=1).reshape(-1)]
    broadcast_in_dim x0 -> x1, local copies, waits for them, and re-layouts: none -> 0.74 us  [per_device(): jnp.where(picked[:, :, None], slot_of[None], 0)]
  transfers between devices with their start and end apart: 17 -> 17, of which waited for: 7 -> 10; matrix products, arithmetic and copies ran while one was open for 1% -> 8% of each run, Pallas kernels for 12% -> 15%
where the time goes in v3:
time: 54.5 us; the launch traced here: 54.3 us
  starting transfers between devices  19 us (35%)
  waiting for transfers between devices  17.5 us (32%)
  Pallas kernels  10 us (18%)
  other arithmetic  4.02 us (7%)
  local copies, waits for them, and re-layouts  3.52 us (6%)
    ppermute x7, starting transfers between devices, hop(): lax.ppermute(pieces[0, t], 'dev', forward)  11.8 us
    pallas_call x6, Pallas kernels, call(): pl.pallas_call(kernel, out_shape=out_shape, in_specs=[SMEM] * n_smem + [V...  10 us
    ppermute x1, waiting for transfers between devices, per_device(): lax.ppermute((chip * SCALE).astype(jnp.float16), 'grp', [(g, (g + shift)...  6.85 us
    ppermute x7, waiting for transfers between devices, hop(): lax.ppermute(pieces[1, t], 'dev', backward)  5.29 us
    ppermute x7, starting transfers between devices, hop(): lax.ppermute(pieces[1, t], 'dev', backward)  5.07 us
    ppermute x7, waiting for transfers between devices, hop(): lax.ppermute(pieces[0, t], 'dev', forward)  4.95 us
    ppermute x1, starting transfers between devices, per_device(): lax.ppermute((chip * SCALE).astype(jnp.float16), 'grp', [(g, (g + shift)...  1.55 us
    unnamed x23, local copies, waits for them, and re-layouts  1.3 us
  transfers between devices with their start and end apart: 17, of which 10 were waited for; matrix products, arithmetic and copies ran while one was open for 8% of the time, Pallas kernels for 15%

profile of v3, /device:TPU:0, one launch (start us, length us, event | category | flops | bytes accessed | tf_op | source)
XLA Modules:
  0.0 54.3 jit_solution(15057908594922418464)
XLA Ops:
  0.0 1.2 %copy.18 = bf16[2,18,4096]{2,1,0:T(8,128)(2,1)S(1)} copy(bf16[2,18,4096]{2,0,1:T(2,128)(2,1)} %param.11) | data formatting | bytes 589824 | tf_op args[0]
  2.1 3.1 %collective-permute-start = (bf16[776,128]{1,0:T(8,128)(2,1)S(1)}, bf16[776,128]{1,0:T(8,128)(2,1)S(1)}, u32[]{:S(2)}, u32[]{:S(2)}) collective-permute-start(bf16[776,128]{1,0:T(8,128)(2,1)S(1)} %fusion.1.refs_0_), channel_id=1, source_target_pairs={{0,2},{2,4},{4,6},{6,7},{7,5},{5,3},{3,1},{1,0},{8,10},{10,12},{12... | collective-permute-start | bytes 595976 | tf_op jit(solution)/shard_map/ppermute | solution.py:181
  5.2 2.0 %collective-permute-start.1 = (bf16[768,128]{1,0:T(8,128)(2,1)S(1)}, bf16[768,128]{1,0:T(8,128)(2,1)S(1)}, u32[]{:S(2)}, u32[]{:S(2)}) collective-permute-start(bf16[768,128]{1,0:T(8,128)(2,1)S(1)} %get-tuple-element.43.refs_1_), channel_id=1, source_target_pairs={{2,0},{4,2},{6,4},{7,6},{5,7},{3,5},{1,3},{0,1},{10,8},{12,10},{14... | collective-permute-start | bytes 589832 | tf_op jit(solution)/shard_map/ppermute | solution.py:182
  7.5 0.6 %iota_compare_fusion.1 = pred[4,4]{1,0:T(4,128)(4,1)} fusion(s32[4]{0:T(128)S(1)} %eq.30), kind=kLoop, calls=%fused_computation.14 | loop fusion | flops 16 | bytes 32 | tf_op jit(solution)/shard_map/eq | solution.py:172
  8.1 0.5 compare_select_fusion.6
  8.7 1.4 %shard_map.113.refs_4_.refs_0_ = f32[128,512]{1,0:T(8,128)S(1)} custom-call(s32[48]{0:T(128)S(1)} %reshape_reshape.3.ids_ref, bf16[776,128]{1,0:T(8,128)(2,1)S(1)} %fusion.1.refs_0_, bf16[768,128]{1,0:T(8,128)(2,1)S(1)} %get-tuple-element.43.refs_1_, bf16[1536,512]{1,0:T(8,128)(2,1)S(1)} %copy-done, bf16[512,512]{1,0:T(8,128)(2,1)S(1)} %copy-done.1), custom_call_target="tpu_custom_call" | custom-call | flops 1 | bytes 1 | tf_op jit(solution)/shard_map/pallas_call | solution.py:102
  10.1 0.7 %broadcast_in_dim.27 = s32[4,4]{1,0:T(4,128)S(1)} reshape(s32[16]{0:T(128)} %compare_select_fusion.6) | data formatting | bytes 128 | tf_op jit(solution)/shard_map/jit(_where)/broadcast_in_dim | solution.py:173
  10.8 1.3 %select_reduce_fusion = s32[4,4]{1,0:T(4,128)} fusion(s32[4,4]{1,0:T(4,128)S(1)} %broadcast_in_dim.27, pred[4,4]{1,0:T(4,128)(4,1)} %iota_compare_fusion.1), kind=kLoop, calls=%fused_computation.7 | loop fusion | flops 112 | bytes 144 | tf_op jit(solution)/shard_map/reduce_sum | solution.py:173
  12.1 0.8 %reshape.65.slot_ref = s32[16]{0:T(128)S(1)} reshape(s32[4,4]{1,0:T(4,128)} %select_reduce_fusion) | data formatting | bytes 128 | tf_op jit(solution)/shard_map/reshape | solution.py:173
  12.9 1.4 %collective-permute-done.5.refs_1_ = bf16[768,128]{1,0:T(8,128)(2,1)S(1)} collective-permute-done((bf16[768,128]{1,0:T(8,128)(2,1)S(1)}, bf16[768,128]{1,0:T(8,128)(2,1)S(1)}, u32[]{:S(2)}, u32[]{:S(2)}) %collective-permute-start.5) | collective-permute-done | bytes 196640 | tf_op jit(solution)/shard_map/ppermute | solution.py:181
  14.3 1.8 %collective-permute-start.9 = (bf16[768,128]{1,0:T(8,128)(2,1)S(1)}, bf16[768,128]{1,0:T(8,128)(2,1)S(1)}, u32[]{:S(2)}, u32[]{:S(2)}) collective-permute-start(bf16[768,128]{1,0:T(8,128)(2,1)S(1)} %collective-permute-done.5.refs_1_), channel_id=1, source_target_pairs={{0,2},{2,4},{4,6},{6,7},{7,5},{5,3},{3,1},{1,0},{8,10},{10,12},{12... | collective-permute-start | bytes 589832 | tf_op jit(solution)/shard_map/ppermute | solution.py:181
  16.1 1.6 %collective-permute-start.2 = (bf16[776,128]{1,0:T(8,128)(2,1)S(1)}, bf16[776,128]{1,0:T(8,128)(2,1)S(1)}, u32[]{:S(2)}, u32[]{:S(2)}) collective-permute-start(bf16[776,128]{1,0:T(8,128)(2,1)S(1)} %collective-permute-done.refs_0_), channel_id=1, source_target_pairs={{0,2},{2,4},{4,6},{6,7},{7,5},{5,3},{3,1},{1,0},{8,10},{10,12},{12... | collective-permute-start | bytes 595976 | tf_op jit(solution)/shard_map/ppermute | solution.py:181
  18.5 2.0 %shard_map.114.refs_5_.refs_1_ = f32[256,512]{1,0:T(8,128)S(1)} custom-call(s32[96]{0:T(128)S(1)} %maximum_convert_fusion.ids_ref, bf16[776,128]{1,0:T(8,128)(2,1)S(1)} %collective-permute-done.refs_0_, bf16[768,128]{1,0:T(8,128)(2,1)S(1)} %collective-permute-done.5.refs_1_, bf16[776,128]{1,0:T(8,128)(2,1)S(1)} %collective-permute-done.4.refs_2_, ...), custom_call_target="tpu_custom_call" | custom-call | flops 1 | bytes 1 | tf_op jit(solution)/shard_map/pallas_call | solution.py:102
  20.5 1.7 %collective-permute-done.9.refs_1_ = bf16[768,128]{1,0:T(8,128)(2,1)S(1)} collective-permute-done((bf16[768,128]{1,0:T(8,128)(2,1)S(1)}, bf16[768,128]{1,0:T(8,128)(2,1)S(1)}, u32[]{:S(2)}, u32[]{:S(2)}) %collective-permute-start.9) | collective-permute-done | bytes 196640 | tf_op jit(solution)/shard_map/ppermute | solution.py:181
  22.2 1.8 %collective-permute-start.13 = (bf16[768,128]{1,0:T(8,128)(2,1)S(1)}, bf16[768,128]{1,0:T(8,128)(2,1)S(1)}, u32[]{:S(2)}, u32[]{:S(2)}) collective-permute-start(bf16[768,128]{1,0:T(8,128)(2,1)S(1)} %collective-permute-done.9.refs_1_), channel_id=1, source_target_pairs={{0,2},{2,4},{4,6},{6,7},{7,5},{5,3},{3,1},{1,0},{8,10},{10,12},{12... | collective-permute-start | bytes 589832 | tf_op jit(solution)/shard_map/ppermute | solution.py:181
  24.0 1.1 %collective-permute-done.3.refs_3_ = bf16[768,128]{1,0:T(8,128)(2,1)S(1)} collective-permute-done((bf16[768,128]{1,0:T(8,128)(2,1)S(1)}, bf16[768,128]{1,0:T(8,128)(2,1)S(1)}, u32[]{:S(2)}, u32[]{:S(2)}) %collective-permute-start.3) | collective-permute-done | bytes 196640 | tf_op jit(solution)/shard_map/ppermute | solution.py:182
  25.0 1.4 %collective-permute-done.2.refs_0_ = bf16[776,128]{1,0:T(8,128)(2,1)S(1)} collective-permute-done((bf16[776,128]{1,0:T(8,128)(2,1)S(1)}, bf16[776,128]{1,0:T(8,128)(2,1)S(1)}, u32[]{:S(2)}, u32[]{:S(2)}) %collective-permute-start.2) | collective-permute-done | bytes 198688 | tf_op jit(solution)/shard_map/ppermute | solution.py:181
  26.4 1.8 %collective-permute-start.6 = (bf16[776,128]{1,0:T(8,128)(2,1)S(1)}, bf16[776,128]{1,0:T(8,128)(2,1)S(1)}, u32[]{:S(2)}, u32[]{:S(2)}) collective-permute-start(bf16[776,128]{1,0:T(8,128)(2,1)S(1)} %collective-permute-done.2.refs_0_), channel_id=1, source_target_pairs={{0,2},{2,4},{4,6},{6,7},{7,5},{5,3},{3,1},{1,0},{8,10},{10,12},{12... | collective-permute-start | bytes 595976 | tf_op jit(solution)/shard_map/ppermute | solution.py:181
  28.5 1.7 %collective-permute-start.12 = (bf16[776,128]{1,0:T(8,128)(2,1)S(1)}, bf16[776,128]{1,0:T(8,128)(2,1)S(1)}, u32[]{:S(2)}, u32[]{:S(2)}) collective-permute-start(bf16[776,128]{1,0:T(8,128)(2,1)S(1)} %collective-permute-done.8.refs_2_), channel_id=1, source_target_pairs={{2,0},{4,2},{6,4},{7,6},{5,7},{3,5},{1,3},{0,1},{10,8},{12,10},{14... | collective-permute-start | bytes 595976 | tf_op jit(solution)/shard_map/ppermute | solution.py:182
  30.3 2.0 %shard_map.115.refs_6_.refs_2_ = f32[256,512]{1,0:T(8,128)S(1)} custom-call(s32[96]{0:T(128)S(1)} %maximum_convert_fusion.1.ids_ref, bf16[776,128]{1,0:T(8,128)(2,1)S(1)} %collective-permute-done.2.refs_0_, bf16[768,128]{1,0:T(8,128)(2,1)S(1)} %collective-permute-done.9.refs_1_, bf16[776,128]{1,0:T(8,128)(2,1)S(1)} %collective-permute-done.8.refs_2_, ...), custom_call_target="tpu_custom_call" | custom-call | flops 1 | bytes 1 | tf_op jit(solution)/shard_map/pallas_call | solution.py:102
  32.3 1.6 %collective-permute-done.7.refs_3_ = bf16[768,128]{1,0:T(8,128)(2,1)S(1)} collective-permute-done((bf16[768,128]{1,0:T(8,128)(2,1)S(1)}, bf16[768,128]{1,0:T(8,128)(2,1)S(1)}, u32[]{:S(2)}, u32[]{:S(2)}) %collective-permute-start.7) | collective-permute-done | bytes 196640 | tf_op jit(solution)/shard_map/ppermute | solution.py:182
  33.9 1.6 %collective-permute-start.10 = (bf16[776,128]{1,0:T(8,128)(2,1)S(1)}, bf16[776,128]{1,0:T(8,128)(2,1)S(1)}, u32[]{:S(2)}, u32[]{:S(2)}) collective-permute-start(bf16[776,128]{1,0:T(8,128)(2,1)S(1)} %collective-permute-done.6.refs_0_), channel_id=1, source_target_pairs={{0,2},{2,4},{4,6},{6,7},{7,5},{5,3},{3,1},{1,0},{8,10},{10,12},{12... | collective-permute-start | bytes 595976 | tf_op jit(solution)/shard_map/ppermute | solution.py:181
  35.9 1.1 %collective-permute-done.12.refs_2_ = bf16[776,128]{1,0:T(8,128)(2,1)S(1)} collective-permute-done((bf16[776,128]{1,0:T(8,128)(2,1)S(1)}, bf16[776,128]{1,0:T(8,128)(2,1)S(1)}, u32[]{:S(2)}, u32[]{:S(2)}) %collective-permute-start.12) | collective-permute-done | bytes 198688 | tf_op jit(solution)/shard_map/ppermute | solution.py:182
  37.1 2.0 %shard_map.116.refs_7_.refs_3_ = f32[256,512]{1,0:T(8,128)S(1)} custom-call(s32[96]{0:T(128)S(1)} %maximum_convert_fusion.2.ids_ref, bf16[776,128]{1,0:T(8,128)(2,1)S(1)} %collective-permute-done.6.refs_0_, bf16[768,128]{1,0:T(8,128)(2,1)S(1)} %collective-permute-done.13.refs_1_, bf16[776,128]{1,0:T(8,128)(2,1)S(1)} %collective-permute-done.12.refs_2_, ...), custom_call_target="tpu_custom_call" | custom-call | flops 1 | bytes 1 | tf_op jit(solution)/shard_map/pallas_call | solution.py:102
  39.1 0.5 collective-permute-done.10.refs_0_
  39.6 1.5 %collective-permute-done.11.refs_1_ = bf16[768,128]{1,0:T(8,128)(2,1)S(1)} collective-permute-done((bf16[768,128]{1,0:T(8,128)(2,1)S(1)}, bf16[768,128]{1,0:T(8,128)(2,1)S(1)}, u32[]{:S(2)}, u32[]{:S(2)}) %collective-permute-start.11) | collective-permute-done | bytes 196640 | tf_op jit(solution)/shard_map/ppermute | solution.py:182
  41.1 1.7 %shard_map.117 = (f32[128,512]{1,0:T(8,128)S(1)}, f32[256,512]{1,0:T(8,128)S(1)}, f32[256,512]{1,0:T(8,128)S(1)}) custom-call(s32[48]{0:T(128)S(1)} %fusion.4.ids_ref, s32[16]{0:T(128)S(1)} %reshape.65.slot_ref, bf16[776,128]{1,0:T(8,128)(2,1)S(1)} %collective-permute-done.10.refs_0_, bf16[768,128]{1,0:T(8,128)(2,1)S(1)} %collective-permute-done.11.refs_1_, ...), custom_call_target="tpu_custom_call" | custom-call | flops 1 | bytes 1 | tf_op jit(solution)/shard_map/pallas_call | solution.py:102
  42.9 0.9 %shard_map.118 = (f32[256,512]{1,0:T(8,128)S(1)}, f32[256,512]{1,0:T(8,128)S(1)}) custom-call(s32[16]{0:T(128)S(1)} %reshape.65.slot_ref, f32[128,512]{1,0:T(8,128)S(1)} %shard_map.113.refs_4_.refs_0_, f32[256,512]{1,0:T(8,128)S(1)} %shard_map.114.refs_5_.refs_1_, f32[256,512]{1,0:T(8,128)S(1)} %shard_map.115.refs_6_.refs_2_, ...), custom_call_target="tpu_custom_call" | custom-call | flops 1 | bytes 1 | tf_op jit(solution)/shard_map/pallas_call | solution.py:102
  43.8 0.5 %collective-permute-start.16 = (f32[256,512]{1,0:T(8,128)S(1)}, f32[256,512]{1,0:T(8,128)S(1)}, u32[]{:S(2)}, u32[]{:S(2)}) collective-permute-start(f32[256,512]{1,0:T(8,128)S(1)} %get-tuple-element.38), channel_id=1, source_target_pairs={{0,8},{8,0},{16,24},{24,16},{1,9},{9,1},{17,25},{25,17},{2,10},{10... | collective-permute-start | bytes 1572872 | tf_op jit(solution)/shard_map/ppermute | solution.py:222
  44.9 1.6 %collective-permute-start.15 = (f16[256,512]{1,0:T(8,128)(2,1)S(1)}, f16[256,512]{1,0:T(8,128)(2,1)S(1)}, u32[]{:S(2)}, u32[]{:S(2)}) collective-permute-start(f16[256,512]{1,0:T(8,128)(2,1)S(1)} %multiply_convert_fusion), channel_id=1, source_target_pairs={{0,16},{8,24},{16,0},{24,8},{1,17},{9,25},{17,1},{25,9},{2,18},{10... | collective-permute-start | bytes 786440 | tf_op jit(solution)/shard_map/ppermute | solution.py:212
  46.5 6.9 %collective-permute-done.15 = f16[256,512]{1,0:T(8,128)(2,1)S(1)} collective-permute-done((f16[256,512]{1,0:T(8,128)(2,1)S(1)}, f16[256,512]{1,0:T(8,128)(2,1)S(1)}, u32[]{:S(2)}, u32[]{:S(2)}) %collective-permute-start.15) | collective-permute-done | bytes 262176 | tf_op jit(solution)/shard_map/ppermute | solution.py:212
  53.4 1.0 %add_add_fusion = f32[256,512]{1,0:T(8,128)} fusion(f32[256,512]{1,0:T(8,128)S(1)} %get-tuple-element.37, f32[256,512]{1,0:T(8,128)S(1)} %collective-permute-done.16, f32[256,512]{1,0:T(8,128)S(1)} %copy-done.2, f16[256,512]{1,0:T(8,128)(2,1)S(1)} %collective-permute-done.15), kind=kLoop, calls=%fused_computation | loop fusion | flops 655360 | bytes 2359296 | tf_op jit(solution)/shard_map/add | solution.py:222
  (62 shorter events, 3.5 us)
Async XLA Ops:
  0.0 1.4 %copy-start.3 = (bf16[2,6,4096]{2,0,1:T(2,128)(2,1)S(1)}, bf16[2,6,4096]{2,0,1:T(2,128)(2,1)}, u32[]{:S(2)}) copy-start(bf16[2,6,4096]{2,0,1:T(2,128)(2,1)} %param.14) | copy-start | bytes 294916
  0.0 1.7 %copy-start.6 = (s32[2,1]{0,1:T(1,128)S(1)}, s32[2,1]{0,1:T(1,128)}, u32[]{:S(2)}) copy-start(s32[2,1]{0,1:T(1,128)} %param.16) | copy-start | bytes 28
  0.0 1.7 %copy-start.4 = (s32[2,6]{1,0:T(2,128)S(1)}, s32[2,6]{1,0:T(2,128)}, u32[]{:S(2)}) copy-start(s32[2,6]{1,0:T(2,128)} %param.15) | copy-start | bytes 148
  0.0 1.8 %copy-start.7 = (s32[2,1]{0,1:T(1,128)S(1)}, s32[2,1]{0,1:T(1,128)}, u32[]{:S(2)}) copy-start(s32[2,1]{0,1:T(1,128)} %param.13) | copy-start | bytes 28
  0.0 1.8 %copy-start.5 = (s32[2,18]{1,0:T(2,128)S(1)}, s32[2,18]{1,0:T(2,128)}, u32[]{:S(2)}) copy-start(s32[2,18]{1,0:T(2,128)} %param.12) | copy-start | bytes 436
  1.2 6.1 %copy-start.8 = (s32[2]{0:T(128)S(1)}, s32[2]{0:T(128)}, u32[]{:S(2)}) copy-start(s32[2]{0:T(128)} %constant.71.clone) | copy-start | bytes 28
  1.2 6.9 %copy-start.9 = (s32[16]{0:T(128)S(1)}, s32[16]{0:T(128)}, u32[]{:S(2)}) copy-start(s32[16]{0:T(128)} %param.19) | copy-start | bytes 196
  1.2 7.5 %copy-start = (bf16[1536,512]{1,0:T(8,128)(2,1)S(1)}, bf16[1536,512]{1,0:T(8,128)(2,1)}, u32[]{:S(2)}) copy-start(bf16[1536,512]{1,0:T(8,128)(2,1)} %refs_2_.3) | copy-start | bytes 4718596
  1.2 7.5 %copy-start.1 = (bf16[512,512]{1,0:T(8,128)(2,1)S(1)}, bf16[512,512]{1,0:T(8,128)(2,1)}, u32[]{:S(2)}) copy-start(bf16[512,512]{1,0:T(8,128)(2,1)} %refs_3_.3) | copy-start | bytes 1572868
  2.1 14.0 %collective-permute-start = (bf16[776,128]{1,0:T(8,128)(2,1)S(1)}, bf16[776,128]{1,0:T(8,128)(2,1)S(1)}, u32[]{:S(2)}, u32[]{:S(2)}) collective-permute-start(bf16[776,128]{1,0:T(8,128)(2,1)S(1)} %fusion.1.refs_0_), channel_id=1, source_target_pairs={{0,2},{2,4},{4,6},{6,7},{7,5},{5,3},{3,1},{1,0},{8,10},{10,12},{12... | collective-permute-start | bytes 595976 | tf_op jit(solution)/shard_map/ppermute | solution.py:181
  5.2 12.9 %collective-permute-start.4 = (bf16[776,128]{1,0:T(8,128)(2,1)S(1)}, bf16[776,128]{1,0:T(8,128)(2,1)S(1)}, u32[]{:S(2)}, u32[]{:S(2)}) collective-permute-start(bf16[776,128]{1,0:T(8,128)(2,1)S(1)} %fusion.1.refs_0_), channel_id=1, source_target_pairs={{2,0},{4,2},{6,4},{7,6},{5,7},{3,5},{1,3},{0,1},{10,8},{12,10},{14... | collective-permute-start | bytes 595976 | tf_op jit(solution)/shard_map/ppermute | solution.py:182
  5.2 10.9 %collective-permute-start.1 = (bf16[768,128]{1,0:T(8,128)(2,1)S(1)}, bf16[768,128]{1,0:T(8,128)(2,1)S(1)}, u32[]{:S(2)}, u32[]{:S(2)}) collective-permute-start(bf16[768,128]{1,0:T(8,128)(2,1)S(1)} %get-tuple-element.43.refs_1_), channel_id=1, source_target_pairs={{2,0},{4,2},{6,4},{7,6},{5,7},{3,5},{1,3},{0,1},{10,8},{12,10},{14... | collective-permute-start | bytes 589832 | tf_op jit(solution)/shard_map/ppermute | solution.py:182
  7.2 7.1 %collective-permute-start.5 = (bf16[768,128]{1,0:T(8,128)(2,1)S(1)}, bf16[768,128]{1,0:T(8,128)(2,1)S(1)}, u32[]{:S(2)}, u32[]{:S(2)}) collective-permute-start(bf16[768,128]{1,0:T(8,128)(2,1)S(1)} %get-tuple-element.43.refs_1_), channel_id=1, source_target_pairs={{0,2},{2,4},{4,6},{6,7},{7,5},{5,3},{3,1},{1,0},{8,10},{10,12},{12... | collective-permute-start | bytes 589832 | tf_op jit(solution)/shard_map/ppermute | solution.py:181
  14.3 7.8 %collective-permute-start.9 = (bf16[768,128]{1,0:T(8,128)(2,1)S(1)}, bf16[768,128]{1,0:T(8,128)(2,1)S(1)}, u32[]{:S(2)}, u32[]{:S(2)}) collective-permute-start(bf16[768,128]{1,0:T(8,128)(2,1)S(1)} %collective-permute-done.5.refs_1_), channel_id=1, source_target_pairs={{0,2},{2,4},{4,6},{6,7},{7,5},{5,3},{3,1},{1,0},{8,10},{10,12},{12... | collective-permute-start | bytes 589832 | tf_op jit(solution)/shard_map/ppermute | solution.py:181
  16.1 10.3 %collective-permute-start.2 = (bf16[776,128]{1,0:T(8,128)(2,1)S(1)}, bf16[776,128]{1,0:T(8,128)(2,1)S(1)}, u32[]{:S(2)}, u32[]{:S(2)}) collective-permute-start(bf16[776,128]{1,0:T(8,128)(2,1)S(1)} %collective-permute-done.refs_0_), channel_id=1, source_target_pairs={{0,2},{2,4},{4,6},{6,7},{7,5},{5,3},{3,1},{1,0},{8,10},{10,12},{12... | collective-permute-start | bytes 595976 | tf_op jit(solution)/shard_map/ppermute | solution.py:181
  17.7 7.3 %collective-permute-start.3 = (bf16[768,128]{1,0:T(8,128)(2,1)S(1)}, bf16[768,128]{1,0:T(8,128)(2,1)S(1)}, u32[]{:S(2)}, u32[]{:S(2)}) collective-permute-start(bf16[768,128]{1,0:T(8,128)(2,1)S(1)} %collective-permute-done.1.refs_3_), channel_id=1, source_target_pairs={{2,0},{4,2},{6,4},{7,6},{5,7},{3,5},{1,3},{0,1},{10,8},{12,10},{14... | collective-permute-start | bytes 589832 | tf_op jit(solution)/shard_map/ppermute | solution.py:182
  18.2 10.2 %collective-permute-start.8 = (bf16[776,128]{1,0:T(8,128)(2,1)S(1)}, bf16[776,128]{1,0:T(8,128)(2,1)S(1)}, u32[]{:S(2)}, u32[]{:S(2)}) collective-permute-start(bf16[776,128]{1,0:T(8,128)(2,1)S(1)} %collective-permute-done.4.refs_2_), channel_id=1, source_target_pairs={{2,0},{4,2},{6,4},{7,6},{5,7},{3,5},{1,3},{0,1},{10,8},{12,10},{14... | collective-permute-start | bytes 595976 | tf_op jit(solution)/shard_map/ppermute | solution.py:182
  22.2 14.9 %collective-permute-start.13 = (bf16[768,128]{1,0:T(8,128)(2,1)S(1)}, bf16[768,128]{1,0:T(8,128)(2,1)S(1)}, u32[]{:S(2)}, u32[]{:S(2)}) collective-permute-start(bf16[768,128]{1,0:T(8,128)(2,1)S(1)} %collective-permute-done.9.refs_1_), channel_id=1, source_target_pairs={{0,2},{2,4},{4,6},{6,7},{7,5},{5,3},{3,1},{1,0},{8,10},{10,12},{12... | collective-permute-start | bytes 589832 | tf_op jit(solution)/shard_map/ppermute | solution.py:181
  26.4 7.5 %collective-permute-start.6 = (bf16[776,128]{1,0:T(8,128)(2,1)S(1)}, bf16[776,128]{1,0:T(8,128)(2,1)S(1)}, u32[]{:S(2)}, u32[]{:S(2)}) collective-permute-start(bf16[776,128]{1,0:T(8,128)(2,1)S(1)} %collective-permute-done.2.refs_0_), channel_id=1, source_target_pairs={{0,2},{2,4},{4,6},{6,7},{7,5},{5,3},{3,1},{1,0},{8,10},{10,12},{12... | collective-permute-start | bytes 595976 | tf_op jit(solution)/shard_map/ppermute | solution.py:181
  28.2 5.7 %collective-permute-start.7 = (bf16[768,128]{1,0:T(8,128)(2,1)S(1)}, bf16[768,128]{1,0:T(8,128)(2,1)S(1)}, u32[]{:S(2)}, u32[]{:S(2)}) collective-permute-start(bf16[768,128]{1,0:T(8,128)(2,1)S(1)} %collective-permute-done.3.refs_3_), channel_id=1, source_target_pairs={{2,0},{4,2},{6,4},{7,6},{5,7},{3,5},{1,3},{0,1},{10,8},{12,10},{14... | collective-permute-start | bytes 589832 | tf_op jit(solution)/shard_map/ppermute | solution.py:182
  28.5 8.5 %collective-permute-start.12 = (bf16[776,128]{1,0:T(8,128)(2,1)S(1)}, bf16[776,128]{1,0:T(8,128)(2,1)S(1)}, u32[]{:S(2)}, u32[]{:S(2)}) collective-permute-start(bf16[776,128]{1,0:T(8,128)(2,1)S(1)} %collective-permute-done.8.refs_2_), channel_id=1, source_target_pairs={{2,0},{4,2},{6,4},{7,6},{5,7},{3,5},{1,3},{0,1},{10,8},{12,10},{14... | collective-permute-start | bytes 595976 | tf_op jit(solution)/shard_map/ppermute | solution.py:182
  33.9 5.7 %collective-permute-start.10 = (bf16[776,128]{1,0:T(8,128)(2,1)S(1)}, bf16[776,128]{1,0:T(8,128)(2,1)S(1)}, u32[]{:S(2)}, u32[]{:S(2)}) collective-permute-start(bf16[776,128]{1,0:T(8,128)(2,1)S(1)} %collective-permute-done.6.refs_0_), channel_id=1, source_target_pairs={{0,2},{2,4},{4,6},{6,7},{7,5},{5,3},{3,1},{1,0},{8,10},{10,12},{12... | collective-permute-start | bytes 595976 | tf_op jit(solution)/shard_map/ppermute | solution.py:181
  35.5 5.7 %collective-permute-start.11 = (bf16[768,128]{1,0:T(8,128)(2,1)S(1)}, bf16[768,128]{1,0:T(8,128)(2,1)S(1)}, u32[]{:S(2)}, u32[]{:S(2)}) collective-permute-start(bf16[768,128]{1,0:T(8,128)(2,1)S(1)} %collective-permute-done.7.refs_3_), channel_id=1, source_target_pairs={{2,0},{4,2},{6,4},{7,6},{5,7},{3,5},{1,3},{0,1},{10,8},{12,10},{14... | collective-permute-start | bytes 589832 | tf_op jit(solution)/shard_map/ppermute | solution.py:182
  42.9 2.0 %collective-permute-start.14 = (f32[256,512]{1,0:T(8,128)S(1)}, f32[256,512]{1,0:T(8,128)S(1)}, u32[]{:S(2)}, u32[]{:S(2)}) collective-permute-start(f32[256,512]{1,0:T(8,128)S(1)} %get-tuple-element.35), channel_id=1, source_target_pairs={{0,8},{8,0},{16,24},{24,16},{1,9},{9,1},{17,25},{25,17},{2,10},{10... | collective-permute-start | bytes 1572872 | tf_op jit(solution)/shard_map/ppermute | solution.py:211
  42.9 10.4 %copy-start.2 = (f32[256,512]{1,0:T(8,128)S(1)}, f32[256,512]{1,0:T(8,128)}, u32[]{:S(2)}) copy-start(f32[256,512]{1,0:T(8,128)} %param.20) | copy-start | bytes 1572868
  43.8 2.7 %collective-permute-start.16 = (f32[256,512]{1,0:T(8,128)S(1)}, f32[256,512]{1,0:T(8,128)S(1)}, u32[]{:S(2)}, u32[]{:S(2)}) collective-permute-start(f32[256,512]{1,0:T(8,128)S(1)} %get-tuple-element.38), channel_id=1, source_target_pairs={{0,8},{8,0},{16,24},{24,16},{1,9},{9,1},{17,25},{25,17},{2,10},{10... | collective-permute-start | bytes 1572872 | tf_op jit(solution)/shard_map/ppermute | solution.py:222
  44.9 8.4 %collective-permute-start.15 = (f16[256,512]{1,0:T(8,128)(2,1)S(1)}, f16[256,512]{1,0:T(8,128)(2,1)S(1)}, u32[]{:S(2)}, u32[]{:S(2)}) collective-permute-start(f16[256,512]{1,0:T(8,128)(2,1)S(1)} %multiply_convert_fusion), channel_id=1, source_target_pairs={{0,16},{8,24},{16,0},{24,8},{1,17},{9,25},{17,1},{25,9},{2,18},{10... | collective-permute-start | bytes 786440 | tf_op jit(solution)/shard_map/ppermute | solution.py:212

commit v4 on v3

v4 whole, which is shorter than its diff:
```python
import functools
import math

import jax
import jax.numpy as jnp
from jax import lax
from jax.experimental import pallas as pl
from jax.experimental.pallas import tpu as pltpu
from jax.sharding import PartitionSpec as P

TS = 64
HALF = TS // 2
LANES = 128
SCALE = 16.0
DEAD = 128
MARGIN = 1
VMEM = pl.BlockSpec(memory_space=pltpu.VMEM)
SMEM = pl.BlockSpec(memory_space=pltpu.SMEM)


def ring_order(n):
    return list(range(0, n, 2)) + list(range(n - 1, 0, -2))


def ring_place(d, n):
    return jnp.where(lax.rem(d, 2) == 0, lax.div(d, 2), n - 1 - lax.div(d, 2))


def rows_of(amps):
    tiles, slots, _ = amps.shape
    return amps.reshape(tiles, slots * HALF, 2 * TS)


def marked(ids, count):
    slot = jnp.arange(ids.shape[1], dtype=jnp.int32)[None, :]
    return jnp.where(slot < count, ids, ids + DEAD)


def multiply(ids_ref, amp_refs, ladder_ref, cycle_ref, ladder_slots, slots, rows_ref, out_ref):
    cols = ladder_ref.shape[1]
    for t, amp_ref in enumerate(amp_refs):
        total = jnp.zeros((TS, cols), jnp.float32)
        for q in range(0, slots, 4):
            left, right = [], []
            for s in range(q, min(q + 4, slots)):
                mark = ids_ref[t * slots + s]
                k = pl.multiple_of(lax.rem(mark, DEAD) * TS, TS)
                panel_ref = ladder_ref if s < ladder_slots else cycle_ref
                right.append(panel_ref[pl.ds(k, TS), :])
                tile = amp_ref[s * HALF : (s + 1) * HALF, :]
                tile = jnp.where(mark < DEAD, tile, jnp.zeros_like(tile))
                left.append(jnp.concatenate([tile[:, :TS], tile[:, TS:]], axis=0))
            total += jnp.dot(
                jnp.concatenate(left, axis=1),
                jnp.concatenate(right, axis=0),
                preferred_element_type=jnp.float32,
            )
        for c in range(cols // LANES):
            lanes = slice(c * LANES, (c + 1) * LANES)
            for part in range(2):
                rows_ref[t % 2, c, pl.ds(part, HALF, stride=2), :] = total[
                    part * HALF : (part + 1) * HALF, lanes
                ]
            out_ref[t * TS : (t + 1) * TS, lanes] = rows_ref[t % 2, c]


def arrival(row_tile, place, tiles, n_dev):
    t = lax.rem(row_tile, tiles)
    back = lax.rem(place - ring_place(lax.div(row_tile, tiles), n_dev) + n_dev, n_dev)
    half, cut = n_dev // 2, tiles // 2
    step = jnp.minimum(back, n_dev - back)
    there = jnp.where(back < half, jnp.where(t < cut, t, t + cut), jnp.where(t < cut, t + tiles + cut, t))
    slot = tiles + (step - 1) * 2 * tiles + jnp.where(back == half, t, there)
    return jnp.where(back == 0, t, slot)


def slots_of(group, owned, tiles, n_dev, me_ref, owners_ref):
    place = ring_place(me_ref[1], n_dev)
    return [arrival(owners_ref[group * owned + i], place, tiles, n_dev) for i in range(owned)]


def tile_rows(ref, at):
    return ref.at[pl.ds(pl.multiple_of(at * TS, TS), TS), :]


def pick(part_refs, slots, out_ref):
    for i, slot in enumerate(slots):
        low = 0
        for part_ref in part_refs:
            high = low + part_ref.shape[0] // TS

            @pl.when((slot >= low) & (slot < high))
            def _():
                at = jnp.clip(slot - low, 0, high - low - 1)
                out_ref[i * TS : (i + 1) * TS, :] = tile_rows(part_ref, at)[...]

            low = high


def partner(group):
    return group + 1 - 2 * lax.rem(group, 2)


def tile_kernel(n, ladder_slots, slots, ids_ref, *refs):
    ladder_ref, cycle_ref, out_ref, rows_ref = refs[n:]
    multiply(ids_ref, refs[:n], ladder_ref, cycle_ref, ladder_slots, slots, rows_ref, out_ref)


def last_kernel(n, ladder_slots, slots, n_parts, tiles, n_dev, n_grp, ids_ref, me_ref, owners_ref, *refs):
    amp_refs, (ladder_ref, cycle_ref), part_refs = refs[:n], refs[n : n + 2], refs[n + 2 :][:n_parts]
    new_ref, *out_refs, rows_ref = refs[n + 2 + n_parts :]
    multiply(ids_ref, amp_refs, ladder_ref, cycle_ref, ladder_slots, slots, rows_ref, new_ref)
    owned = out_refs[0].shape[0] // TS
    for k, shift in enumerate(range(2, n_grp, 2)):
        group = lax.rem(me_ref[0] + shift, n_grp)
        for owner, out_ref in zip((group, partner(group)), out_refs[2 * k :]):
            pick(part_refs + (new_ref,), slots_of(owner, owned, tiles, n_dev, me_ref, owners_ref), out_ref)


def own_kernel(n_parts, tiles, n_dev, me_ref, owners_ref, *refs):
    owned = refs[-1].shape[0] // TS
    for owner, out_ref in zip((me_ref[0], partner(me_ref[0])), refs[n_parts:]):
        pick(refs[:n_parts], slots_of(owner, owned, tiles, n_dev, me_ref, owners_ref), out_ref)


def call(kernel, out_shape, n_smem, args, scratch=()):
    held = [*args, *jax.tree.leaves(out_shape)]
    held = sum(math.prod(x.shape) * x.dtype.itemsize for x in held)
    return pl.pallas_call(
        kernel,
        out_shape=out_shape,
        in_specs=[SMEM] * n_smem + [VMEM] * (len(args) - n_smem),
        out_specs=jax.tree.map(lambda _: VMEM, out_shape),
        scratch_shapes=list(scratch),
        compiler_params=pltpu.CompilerParams(vmem_limit_bytes=held + (MARGIN << 20)),
        cost_estimate=pl.CostEstimate(flops=1, bytes_accessed=1, transcendentals=0),
    )(*args)


def per_device(
    ladder_amps,
    ladder_ids,
    ladder_count,
    cycle_amps,
    cycle_ids,
    cycle_count,
    ladder_panel,
    cycle_panel,
    owners,
    base,
):
    n_dev, n_grp = lax.axis_size("dev"), lax.axis_size("grp")
    tiles, ladder_slots, _ = ladder_amps.shape
    slots = ladder_slots + cycle_amps.shape[1]
    order = ring_order(n_dev)
    forward = [(order[i], order[(i + 1) % n_dev]) for i in range(n_dev)]
    backward = [(b, a) for a, b in forward]
    swap = [(g, g ^ 1) for g in range(n_grp)]

    own = jnp.concatenate([rows_of(ladder_amps), rows_of(cycle_amps)], axis=1)
    marks = jnp.concatenate(
        [marked(ladder_ids, ladder_count), marked(cycle_ids, cycle_count)], axis=1
    ).reshape(1, -1)
    note = jnp.pad(marks.astype(jnp.bfloat16), ((0, 7), (0, 2 * TS - marks.size)))
    own = [jnp.concatenate([own[t], note], axis=0) for t in range(tiles)]

    def marks_of(piece, t):
        return piece[slots * HALF, t * slots : (t + 1) * slots].astype(jnp.int32)

    cols = base.shape[1]
    rows_scratch = [pltpu.VMEM((2, cols // LANES, TS, LANES), jnp.float32)]

    def products(amps, ids):
        return call(
            functools.partial(tile_kernel, len(amps), ladder_slots, slots),
            jax.ShapeDtypeStruct((len(amps) * TS, cols), jnp.float32),
            1,
            [ids, *amps, ladder_panel, cycle_panel],
            rows_scratch,
        )

    me = jnp.stack([lax.axis_index("grp"), lax.axis_index("dev")])
    owned = owners.shape[0] // n_grp
    shifts = range(2, n_grp, 2)

    def sums(n):
        return jax.ShapeDtypeStruct((n * TS, cols), jnp.float32)

    cut = tiles // 2
    waves = [
        [(t < cut, t) for t in range(tiles)],
        [(t >= cut, t) for t in (*range(cut, tiles), *range(cut))],
    ]

    def hop(wave, pieces):
        return [
            lax.ppermute(piece, "dev", forward if ahead else backward)
            for (ahead, _), piece in zip(waves[wave], pieces)
        ]

    def marks_in(wave, pieces):
        return jnp.concatenate([marks_of(piece, t) for (_, t), piece in zip(waves[wave], pieces)])

    def products_of(wave, pieces):
        return products(pieces, marks_in(wave, pieces))

    first = hop(0, [own[t] for _, t in waves[0]])
    parts = [products(own, marks.reshape(-1))]
    own, parts = lax.optimization_barrier((own, parts))
    second = hop(1, [own[t] for _, t in waves[1]])
    for step in range(1, n_dev // 2):
        first, parts = lax.optimization_barrier((first, parts))
        landed, first = first, hop(0, first)
        if step < n_dev // 2 - 1:
            parts.append(products_of(0, landed))
            second, parts = lax.optimization_barrier((second, parts))
            landed, second = second, hop(1, second)
            parts.append(products_of(1, landed))
        else:
            parts.append(products_of(0, landed))
            second, parts = lax.optimization_barrier((second, parts))
    pieces = second + first
    new, *leaving = call(
        functools.partial(
            last_kernel, len(pieces), ladder_slots, slots, len(parts), tiles, n_dev, n_grp
        ),
        (sums(len(pieces)),) + (sums(owned),) * (n_grp - 2),
        3,
        [
            jnp.concatenate([marks_in(1, second), marks_in(0, first)]),
            me,
            owners,
            *pieces,
            ladder_panel,
            cycle_panel,
            *parts,
        ],
        rows_scratch,
    )
    parts.append(new)
    total = base
    for k, shift in enumerate(shifts):
        chip = leaving[2 * k] + lax.ppermute(leaving[2 * k + 1], "grp", swap)
        sent = lax.ppermute(
            (chip * SCALE).astype(jnp.float16), "grp", [(g, (g + shift) % n_grp) for g in range(n_grp)]
        )
        total = total + sent.astype(jnp.float32) * (1 / SCALE)
    mine, partners = call(
        functools.partial(own_kernel, len(parts), tiles, n_dev),
        (sums(owned), sums(owned)),
        2,
        [me, owners, *parts],
    )
    return total + (mine + lax.ppermute(partners, "grp", swap))


def solution(mesh):
    placed = (
        P("dev", "grp", None),
        P("dev", "grp"),
        P("dev", "grp"),
        P("dev", "grp", None),
        P("dev", "grp"),
        P("dev", "grp"),
        P("grp", "dev"),
        P("grp", "dev"),
        P(),
        P("grp", "dev"),
    )
    return jax.shard_map(
        per_device, mesh=mesh, in_specs=placed, out_specs=P("grp", "dev"), check_vma=False
    )
```

time: 54.5 us -> 52.4 us (0.961)
  Pallas kernels: 10 us -> 12.2 us
  other arithmetic: 4.02 us -> 1.89 us
  starting transfers between devices: 19 us -> 17.6 us
    pallas_call x6 -> x8, Pallas kernels: 10 us -> 12.2 us  [call(): pl.pallas_call(kernel, out_shape=out_shape, in_specs=[SMEM] * n_smem + [V...]
    ppermute x15, starting transfers between devices: 16.9 us -> 15.5 us  [the longest x14 15.4 us: hop(): lax.ppermute(piece, 'dev', forward if ahead else backward)]
    reduce_sum x1 -> x0, other arithmetic: 1.29 us -> none  [per_device(): jnp.sum(jnp.where(picked[:, :, None], slot_of[None], 0), axis=1).reshape(-1)]
    convert_element_type x6 -> x13, local copies, waits for them, and re-layouts: 0.01 us -> 1.18 us  [marks_of(): return piece[slots * HALF, t * slots:(t + 1) * slots].astype(jnp.int32)]
    reshape x1 -> x0, local copies, waits for them, and re-layouts: 0.76 us -> none  [per_device(): jnp.sum(jnp.where(picked[:, :, None], slot_of[None], 0), axis=1).reshape(-1)]
    broadcast_in_dim x1 -> x0, local copies, waits for them, and re-layouts: 0.74 us -> none  [per_device(): jnp.where(picked[:, :, None], slot_of[None], 0)]
    eq x1 -> x0, other arithmetic: 0.61 us -> none  [per_device(): picked = chosen == jnp.arange(n_grp, dtype=jnp.int32)[None, :]]
    unnamed x23 -> x21, local copies, waits for them, and re-layouts: 1.3 us -> 1.29 us
  transfers between devices with their start and end apart: 17 -> 17, of which waited for: 10 -> 10; matrix products, arithmetic and copies ran while one was open for 8% -> 4% of each run, Pallas kernels for 15% -> 19%
where the time goes in v4:
time: 52.4 us; the launch traced here: 52.2 us
  starting transfers between devices  17.6 us (34%)
  waiting for transfers between devices  17.3 us (33%)
  Pallas kernels  12.2 us (23%)
  local copies, waits for them, and re-layouts  3.01 us (6%)
  other arithmetic  1.89 us (4%)
    ppermute x14, starting transfers between devices, hop(): lax.ppermute(piece, 'dev', forward if ahead else backward)  15.4 us
    pallas_call x8, Pallas kernels, call(): pl.pallas_call(kernel, out_shape=out_shape, in_specs=[SMEM] * n_smem + [V...  12.2 us
    ppermute x14, waiting for transfers between devices, hop(): lax.ppermute(piece, 'dev', forward if ahead else backward)  10.2 us
    ppermute x1, waiting for transfers between devices, per_device(): lax.ppermute((chip * SCALE).astype(jnp.float16), 'grp', [(g, (g + shift)...  6.85 us
    ppermute x1, starting transfers between devices, per_device(): lax.ppermute((chip * SCALE).astype(jnp.float16), 'grp', [(g, (g + shift)...  1.56 us
    unnamed x21, local copies, waits for them, and re-layouts  1.29 us
    convert_element_type x13, local copies, waits for them, and re-layouts, marks_of(): return piece[slots * HALF, t * slots:(t + 1) * slots].astype(jnp.int32)  1.18 us
  transfers between devices with their start and end apart: 17, of which 10 were waited for; matrix products, arithmetic and copies ran while one was open for 4% of the time, Pallas kernels for 19%

profile of v4, /device:TPU:0, one launch (start us, length us, event | category | flops | bytes accessed | tf_op | source)
XLA Modules:
  0.0 52.2 jit_solution(16081492772189043836)
XLA Ops:
  0.0 1.2 %copy.13 = bf16[2,18,4096]{2,1,0:T(8,128)(2,1)S(1)} copy(bf16[2,18,4096]{2,0,1:T(2,128)(2,1)} %param.10) | data formatting | bytes 589824 | tf_op args[0]
  2.1 3.1 %collective-permute-start.2 = (bf16[776,128]{1,0:T(8,128)(2,1)S(1)}, bf16[776,128]{1,0:T(8,128)(2,1)S(1)}, u32[]{:S(2)}, u32[]{:S(2)}) collective-permute-start(bf16[776,128]{1,0:T(8,128)(2,1)S(1)} %get-tuple-element.47.refs_0_), channel_id=1, source_target_pairs={{0,2},{2,4},{4,6},{6,7},{7,5},{5,3},{3,1},{1,0},{8,10},{10,12},{12... | collective-permute-start | bytes 595976 | tf_op jit(solution)/shard_map/ppermute | solution.py:197
  5.3 1.4 %shard_map.100.refs_6_.refs_0_ = f32[128,512]{1,0:T(8,128)S(1)} custom-call(s32[48]{0:T(128)S(1)} %reshape_reshape.3.ids_ref, bf16[776,128]{1,0:T(8,128)(2,1)S(1)} %get-tuple-element.47.refs_0_, bf16[776,128]{1,0:T(8,128)(2,1)S(1)} %get-tuple-element.46.refs_1_, bf16[1536,512]{1,0:T(8,128)(2,1)S(1)} %copy-done, bf16[512,512]{1,0:T(8,128)(2,1)S(1)} %copy-done.1), custom_call_target="tpu_custom_call" | custom-call | flops 1 | bytes 1 | tf_op jit(solution)/shard_map/pallas_call | solution.py:129
  6.7 2.1 %collective-permute-start = (bf16[776,128]{1,0:T(8,128)(2,1)S(1)}, bf16[776,128]{1,0:T(8,128)(2,1)S(1)}, u32[]{:S(2)}, u32[]{:S(2)}) collective-permute-start(bf16[776,128]{1,0:T(8,128)(2,1)S(1)} %get-tuple-element.46.refs_1_), channel_id=1, source_target_pairs={{0,2},{2,4},{4,6},{6,7},{7,5},{5,3},{3,1},{1,0},{8,10},{10,12},{12... | collective-permute-start | bytes 595976 | tf_op jit(solution)/shard_map/ppermute | solution.py:197
  8.8 2.1 %collective-permute-done.2.refs_0_ = bf16[776,128]{1,0:T(8,128)(2,1)S(1)} collective-permute-done((bf16[776,128]{1,0:T(8,128)(2,1)S(1)}, bf16[776,128]{1,0:T(8,128)(2,1)S(1)}, u32[]{:S(2)}, u32[]{:S(2)}) %collective-permute-start.2) | collective-permute-done | bytes 198688 | tf_op jit(solution)/shard_map/ppermute | solution.py:197
  10.9 1.9 %collective-permute-done.3.refs_1_ = bf16[776,128]{1,0:T(8,128)(2,1)S(1)} collective-permute-done((bf16[776,128]{1,0:T(8,128)(2,1)S(1)}, bf16[776,128]{1,0:T(8,128)(2,1)S(1)}, u32[]{:S(2)}, u32[]{:S(2)}) %collective-permute-start.3) | collective-permute-done | bytes 198688 | tf_op jit(solution)/shard_map/ppermute | solution.py:197
  12.8 1.6 %collective-permute-start.6 = (bf16[776,128]{1,0:T(8,128)(2,1)S(1)}, bf16[776,128]{1,0:T(8,128)(2,1)S(1)}, u32[]{:S(2)}, u32[]{:S(2)}) collective-permute-start(bf16[776,128]{1,0:T(8,128)(2,1)S(1)} %collective-permute-done.2.refs_0_), channel_id=1, source_target_pairs={{0,2},{2,4},{4,6},{6,7},{7,5},{5,3},{3,1},{1,0},{8,10},{10,12},{12... | collective-permute-start | bytes 595976 | tf_op jit(solution)/shard_map/ppermute | solution.py:197
  14.6 0.4 collective-permute-start.7
  15.0 1.4 %shard_map.101.refs_7_.refs_1_ = f32[128,512]{1,0:T(8,128)S(1)} custom-call(s32[48]{0:T(128)S(1)} %maximum_convert_fusion.ids_ref, bf16[776,128]{1,0:T(8,128)(2,1)S(1)} %collective-permute-done.2.refs_0_, bf16[776,128]{1,0:T(8,128)(2,1)S(1)} %collective-permute-done.3.refs_1_, bf16[1536,512]{1,0:T(8,128)(2,1)S(1)} %copy-done, bf16[512,512]{1,0:T(8,128)(2,1)S(1)} %copy-done.1), custom_call_target="tpu_custom_call" | custom-call | flops 1 | bytes 1 | tf_op jit(solution)/shard_map/pallas_call | solution.py:129
  16.4 0.8 %collective-permute-done.1.refs_1_ = bf16[776,128]{1,0:T(8,128)(2,1)} collective-permute-done((bf16[776,128]{1,0:T(8,128)(2,1)S(1)}, bf16[776,128]{1,0:T(8,128)(2,1)}, u32[]{:S(2)}, u32[]{:S(2)}) %collective-permute-start.1) | collective-permute-done | bytes 198688 | tf_op jit(solution)/shard_map/ppermute | solution.py:197
  17.3 1.6 %collective-permute-start.4 = (bf16[776,128]{1,0:T(8,128)(2,1)S(1)}, bf16[776,128]{1,0:T(8,128)(2,1)S(1)}, u32[]{:S(2)}, u32[]{:S(2)}) collective-permute-start(bf16[776,128]{1,0:T(8,128)(2,1)S(1)} %collective-permute-done.refs_0_), channel_id=1, source_target_pairs={{0,2},{2,4},{4,6},{6,7},{7,5},{5,3},{3,1},{1,0},{8,10},{10,12},{12... | collective-permute-start | bytes 595976 | tf_op jit(solution)/shard_map/ppermute | solution.py:197
  18.8 0.7 %slice_bitcast_fusion.12 = bf16[24]{0:T(256)(128)(2,1)S(1)} fusion(bf16[776,128]{1,0:T(8,128)(2,1)} %collective-permute-done.1.refs_1_), kind=kLoop, calls=%fused_computation.30 | loop fusion | bytes 96 | tf_op jit(solution)/shard_map/convert_element_type | solution.py:168
  19.6 0.4 collective-permute-start.5
  20.0 1.8 %shard_map.102.refs_8_.refs_2_ = f32[128,512]{1,0:T(8,128)S(1)} custom-call(s32[48]{0:T(128)S(1)} %maximum_convert_fusion.1.ids_ref, bf16[776,128]{1,0:T(8,128)(2,1)S(1)} %collective-permute-done.refs_0_, bf16[776,128]{1,0:T(8,128)(2,1)} %collective-permute-done.1.refs_1_, bf16[1536,512]{1,0:T(8,128)(2,1)S(1)} %copy-done, bf16[512,512]{1,0:T(8,128)(2,1)S(1)} %copy-done.1), custom_call_target="tpu_custom_call" | custom-call | flops 1 | bytes 1 | tf_op jit(solution)/shard_map/pallas_call | solution.py:129
  21.9 1.6 %collective-permute-start.10 = (bf16[776,128]{1,0:T(8,128)(2,1)S(1)}, bf16[776,128]{1,0:T(8,128)(2,1)S(1)}, u32[]{:S(2)}, u32[]{:S(2)}) collective-permute-start(bf16[776,128]{1,0:T(8,128)(2,1)S(1)} %collective-permute-done.6.refs_0_), channel_id=1, source_target_pairs={{0,2},{2,4},{4,6},{6,7},{7,5},{5,3},{3,1},{1,0},{8,10},{10,12},{12... | collective-permute-start | bytes 595976 | tf_op jit(solution)/shard_map/ppermute | solution.py:197
  23.6 0.4 collective-permute-start.11
  24.1 1.4 %shard_map.103.refs_9_.refs_3_ = f32[128,512]{1,0:T(8,128)S(1)} custom-call(s32[48]{0:T(128)S(1)} %maximum_convert_fusion.2.ids_ref, bf16[776,128]{1,0:T(8,128)(2,1)S(1)} %collective-permute-done.6.refs_0_, bf16[776,128]{1,0:T(8,128)(2,1)S(1)} %collective-permute-done.7.refs_1_, bf16[1536,512]{1,0:T(8,128)(2,1)S(1)} %copy-done, bf16[512,512]{1,0:T(8,128)(2,1)S(1)} %copy-done.1), custom_call_target="tpu_custom_call" | custom-call | flops 1 | bytes 1 | tf_op jit(solution)/shard_map/pallas_call | solution.py:129
  25.5 2.1 %collective-permute-done.5.refs_1_ = bf16[776,128]{1,0:T(8,128)(2,1)S(1)} collective-permute-done((bf16[776,128]{1,0:T(8,128)(2,1)}, bf16[776,128]{1,0:T(8,128)(2,1)S(1)}, u32[]{:S(2)}, u32[]{:S(2)}) %collective-permute-start.5) | collective-permute-done | bytes 198688 | tf_op jit(solution)/shard_map/ppermute | solution.py:197
  27.7 1.6 %collective-permute-start.8 = (bf16[776,128]{1,0:T(8,128)(2,1)S(1)}, bf16[776,128]{1,0:T(8,128)(2,1)S(1)}, u32[]{:S(2)}, u32[]{:S(2)}) collective-permute-start(bf16[776,128]{1,0:T(8,128)(2,1)S(1)} %collective-permute-done.4.refs_0_), channel_id=1, source_target_pairs={{0,2},{2,4},{4,6},{6,7},{7,5},{5,3},{3,1},{1,0},{8,10},{10,12},{12... | collective-permute-start | bytes 595976 | tf_op jit(solution)/shard_map/ppermute | solution.py:197
  29.3 0.4 collective-permute-start.9
  29.8 1.4 %shard_map.104.refs_10_.refs_4_ = f32[128,512]{1,0:T(8,128)S(1)} custom-call(s32[48]{0:T(128)S(1)} %maximum_convert_fusion.3.ids_ref, bf16[776,128]{1,0:T(8,128)(2,1)S(1)} %collective-permute-done.4.refs_0_, bf16[776,128]{1,0:T(8,128)(2,1)S(1)} %collective-permute-done.5.refs_1_, bf16[1536,512]{1,0:T(8,128)(2,1)S(1)} %copy-done, bf16[512,512]{1,0:T(8,128)(2,1)S(1)} %copy-done.1), custom_call_target="tpu_custom_call" | custom-call | flops 1 | bytes 1 | tf_op jit(solution)/shard_map/pallas_call | solution.py:129
  31.2 0.7 %collective-permute-done.11.refs_1_ = bf16[776,128]{1,0:T(8,128)(2,1)S(1)} collective-permute-done((bf16[776,128]{1,0:T(8,128)(2,1)S(1)}, bf16[776,128]{1,0:T(8,128)(2,1)S(1)}, u32[]{:S(2)}, u32[]{:S(2)}) %collective-permute-start.11) | collective-permute-done | bytes 198688 | tf_op jit(solution)/shard_map/ppermute | solution.py:197
  31.9 0.4 collective-permute-start.13
  32.5 1.6 %collective-permute-start.12 = (bf16[776,128]{1,0:T(8,128)(2,1)S(1)}, bf16[776,128]{1,0:T(8,128)(2,1)S(1)}, u32[]{:S(2)}, u32[]{:S(2)}) collective-permute-start(bf16[776,128]{1,0:T(8,128)(2,1)S(1)} %collective-permute-done.10.refs_0_), channel_id=1, source_target_pairs={{0,2},{2,4},{4,6},{6,7},{7,5},{5,3},{3,1},{1,0},{8,10},{10,12},{12... | collective-permute-start | bytes 595976 | tf_op jit(solution)/shard_map/ppermute | solution.py:197
  34.1 1.4 %shard_map.105.refs_11_.refs_5_ = f32[128,512]{1,0:T(8,128)S(1)} custom-call(s32[48]{0:T(128)S(1)} %maximum_convert_fusion.4.ids_ref, bf16[776,128]{1,0:T(8,128)(2,1)S(1)} %collective-permute-done.10.refs_0_, bf16[776,128]{1,0:T(8,128)(2,1)S(1)} %collective-permute-done.11.refs_1_, bf16[1536,512]{1,0:T(8,128)(2,1)S(1)} %copy-done, bf16[512,512]{1,0:T(8,128)(2,1)S(1)} %copy-done.1), custom_call_target="tpu_custom_call" | custom-call | flops 1 | bytes 1 | tf_op jit(solution)/shard_map/pallas_call | solution.py:129
  36.0 2.1 %collective-permute-done.13.refs_3_ = bf16[776,128]{1,0:T(8,128)(2,1)S(1)} collective-permute-done((bf16[776,128]{1,0:T(8,128)(2,1)S(1)}, bf16[776,128]{1,0:T(8,128)(2,1)S(1)}, u32[]{:S(2)}, u32[]{:S(2)}) %collective-permute-start.13) | collective-permute-done | bytes 198688 | tf_op jit(solution)/shard_map/ppermute | solution.py:197
  38.2 2.5 %shard_map.106 = (f32[256,512]{1,0:T(8,128)S(1)}, f32[256,512]{1,0:T(8,128)S(1)}, f32[256,512]{1,0:T(8,128)S(1)}) custom-call(s32[96]{0:T(128)S(1)} %maximum_convert_fusion.5.ids_ref, s32[2]{0:T(128)S(1)} %pad_add_fusion.1.me_ref, s32[16]{0:T(128)S(1)} %copy-done.2, bf16[776,128]{1,0:T(8,128)(2,1)S(1)} %collective-permute-done.8.refs_0_, ...), custom_call_target="tpu_custom_call" | custom-call | flops 1 | bytes 1 | tf_op jit(solution)/shard_map/pallas_call | solution.py:129
  40.8 1.1 %shard_map.107 = (f32[256,512]{1,0:T(8,128)S(1)}, f32[256,512]{1,0:T(8,128)S(1)}) custom-call(s32[2]{0:T(128)S(1)} %pad_add_fusion.1.me_ref, s32[16]{0:T(128)S(1)} %copy-done.2, f32[128,512]{1,0:T(8,128)S(1)} %shard_map.100.refs_6_.refs_0_, f32[128,512]{1,0:T(8,128)S(1)} %shard_map.101.refs_7_.refs_1_, f32[128,512]{1,0:T(8,128)S(1)} %shard_map.102.refs_8_.refs_2_, ...), custom_call_target="tpu_custom_call" | custom-call | flops 1 | bytes 1 | tf_op jit(solution)/shard_map/pallas_call | solution.py:129
  41.9 0.5 %collective-permute-start.16 = (f32[256,512]{1,0:T(8,128)S(1)}, f32[256,512]{1,0:T(8,128)S(1)}, u32[]{:S(2)}, u32[]{:S(2)}) collective-permute-start(f32[256,512]{1,0:T(8,128)S(1)} %get-tuple-element.86), channel_id=1, source_target_pairs={{0,8},{8,0},{16,24},{24,16},{1,9},{9,1},{17,25},{25,17},{2,10},{10... | collective-permute-start | bytes 1572872 | tf_op jit(solution)/shard_map/ppermute | solution.py:254
  42.8 1.6 %collective-permute-start.15 = (f16[256,512]{1,0:T(8,128)(2,1)S(1)}, f16[256,512]{1,0:T(8,128)(2,1)S(1)}, u32[]{:S(2)}, u32[]{:S(2)}) collective-permute-start(f16[256,512]{1,0:T(8,128)(2,1)S(1)} %multiply_convert_fusion), channel_id=1, source_target_pairs={{0,16},{8,24},{16,0},{24,8},{1,17},{9,25},{17,1},{25,9},{2,18},{10... | collective-permute-start | bytes 786440 | tf_op jit(solution)/shard_map/ppermute | solution.py:244
  44.4 6.8 %collective-permute-done.15 = f16[256,512]{1,0:T(8,128)(2,1)S(1)} collective-permute-done((f16[256,512]{1,0:T(8,128)(2,1)S(1)}, f16[256,512]{1,0:T(8,128)(2,1)S(1)}, u32[]{:S(2)}, u32[]{:S(2)}) %collective-permute-start.15) | collective-permute-done | bytes 262176 | tf_op jit(solution)/shard_map/ppermute | solution.py:244
  51.3 1.0 %add_add_fusion = f32[256,512]{1,0:T(8,128)} fusion(f32[256,512]{1,0:T(8,128)S(1)} %get-tuple-element.85, f32[256,512]{1,0:T(8,128)S(1)} %collective-permute-done.16, f32[256,512]{1,0:T(8,128)S(1)} %copy-done.3, f16[256,512]{1,0:T(8,128)(2,1)S(1)} %collective-permute-done.15), kind=kLoop, calls=%fused_computation | loop fusion | flops 655360 | bytes 2359296 | tf_op jit(solution)/shard_map/add | solution.py:254
  (63 shorter events, 3.0 us)
Async XLA Ops:
  0.0 1.4 %copy-start.4 = (bf16[2,6,4096]{2,0,1:T(2,128)(2,1)S(1)}, bf16[2,6,4096]{2,0,1:T(2,128)(2,1)}, u32[]{:S(2)}) copy-start(bf16[2,6,4096]{2,0,1:T(2,128)(2,1)} %param.13) | copy-start | bytes 294916
  0.0 1.7 %copy-start.7 = (s32[2,1]{0,1:T(1,128)S(1)}, s32[2,1]{0,1:T(1,128)}, u32[]{:S(2)}) copy-start(s32[2,1]{0,1:T(1,128)} %param.15) | copy-start | bytes 28
  0.0 1.7 %copy-start.5 = (s32[2,6]{1,0:T(2,128)S(1)}, s32[2,6]{1,0:T(2,128)}, u32[]{:S(2)}) copy-start(s32[2,6]{1,0:T(2,128)} %param.14) | copy-start | bytes 148
  0.0 1.8 %copy-start.8 = (s32[2,1]{0,1:T(1,128)S(1)}, s32[2,1]{0,1:T(1,128)}, u32[]{:S(2)}) copy-start(s32[2,1]{0,1:T(1,128)} %param.12) | copy-start | bytes 28
  0.0 1.8 %copy-start.6 = (s32[2,18]{1,0:T(2,128)S(1)}, s32[2,18]{1,0:T(2,128)}, u32[]{:S(2)}) copy-start(s32[2,18]{1,0:T(2,128)} %param.11) | copy-start | bytes 436
  1.4 3.9 %copy-start = (bf16[1536,512]{1,0:T(8,128)(2,1)S(1)}, bf16[1536,512]{1,0:T(8,128)(2,1)}, u32[]{:S(2)}) copy-start(bf16[1536,512]{1,0:T(8,128)(2,1)} %refs_4_.1) | copy-start | bytes 4718596
  1.4 3.9 %copy-start.1 = (bf16[512,512]{1,0:T(8,128)(2,1)S(1)}, bf16[512,512]{1,0:T(8,128)(2,1)}, u32[]{:S(2)}) copy-start(bf16[512,512]{1,0:T(8,128)(2,1)} %refs_5_.1) | copy-start | bytes 1572868
  2.1 8.9 %collective-permute-start.2 = (bf16[776,128]{1,0:T(8,128)(2,1)S(1)}, bf16[776,128]{1,0:T(8,128)(2,1)S(1)}, u32[]{:S(2)}, u32[]{:S(2)}) collective-permute-start(bf16[776,128]{1,0:T(8,128)(2,1)S(1)} %get-tuple-element.47.refs_0_), channel_id=1, source_target_pairs={{0,2},{2,4},{4,6},{6,7},{7,5},{5,3},{3,1},{1,0},{8,10},{10,12},{12... | collective-permute-start | bytes 595976 | tf_op jit(solution)/shard_map/ppermute | solution.py:197
  5.2 7.6 %collective-permute-start.3 = (bf16[776,128]{1,0:T(8,128)(2,1)S(1)}, bf16[776,128]{1,0:T(8,128)(2,1)S(1)}, u32[]{:S(2)}, u32[]{:S(2)}) collective-permute-start(bf16[776,128]{1,0:T(8,128)(2,1)S(1)} %get-tuple-element.46.refs_1_), channel_id=1, source_target_pairs={{2,0},{4,2},{6,4},{7,6},{5,7},{3,5},{1,3},{0,1},{10,8},{12,10},{14... | collective-permute-start | bytes 595976 | tf_op jit(solution)/shard_map/ppermute | solution.py:197
  6.7 9.7 %collective-permute-start = (bf16[776,128]{1,0:T(8,128)(2,1)S(1)}, bf16[776,128]{1,0:T(8,128)(2,1)S(1)}, u32[]{:S(2)}, u32[]{:S(2)}) collective-permute-start(bf16[776,128]{1,0:T(8,128)(2,1)S(1)} %get-tuple-element.46.refs_1_), channel_id=1, source_target_pairs={{0,2},{2,4},{4,6},{6,7},{7,5},{5,3},{3,1},{1,0},{8,10},{10,12},{12... | collective-permute-start | bytes 595976 | tf_op jit(solution)/shard_map/ppermute | solution.py:197
  8.8 8.4 %collective-permute-start.1 = (bf16[776,128]{1,0:T(8,128)(2,1)S(1)}, bf16[776,128]{1,0:T(8,128)(2,1)}, u32[]{:S(2)}, u32[]{:S(2)}) collective-permute-start(bf16[776,128]{1,0:T(8,128)(2,1)S(1)} %get-tuple-element.47.refs_0_), channel_id=1, source_target_pairs={{2,0},{4,2},{6,4},{7,6},{5,7},{3,5},{1,3},{0,1},{10,8},{12,10},{14... | collective-permute-start | bytes 595976 | tf_op jit(solution)/shard_map/ppermute | solution.py:197
  12.8 9.0 %collective-permute-start.6 = (bf16[776,128]{1,0:T(8,128)(2,1)S(1)}, bf16[776,128]{1,0:T(8,128)(2,1)S(1)}, u32[]{:S(2)}, u32[]{:S(2)}) collective-permute-start(bf16[776,128]{1,0:T(8,128)(2,1)S(1)} %collective-permute-done.2.refs_0_), channel_id=1, source_target_pairs={{0,2},{2,4},{4,6},{6,7},{7,5},{5,3},{3,1},{1,0},{8,10},{10,12},{12... | collective-permute-start | bytes 595976 | tf_op jit(solution)/shard_map/ppermute | solution.py:197
  14.6 7.3 %collective-permute-start.7 = (bf16[776,128]{1,0:T(8,128)(2,1)S(1)}, bf16[776,128]{1,0:T(8,128)(2,1)S(1)}, u32[]{:S(2)}, u32[]{:S(2)}) collective-permute-start(bf16[776,128]{1,0:T(8,128)(2,1)S(1)} %collective-permute-done.3.refs_1_), channel_id=1, source_target_pairs={{2,0},{4,2},{6,4},{7,6},{5,7},{3,5},{1,3},{0,1},{10,8},{12,10},{14... | collective-permute-start | bytes 595976 | tf_op jit(solution)/shard_map/ppermute | solution.py:197
  17.3 8.2 %collective-permute-start.4 = (bf16[776,128]{1,0:T(8,128)(2,1)S(1)}, bf16[776,128]{1,0:T(8,128)(2,1)S(1)}, u32[]{:S(2)}, u32[]{:S(2)}) collective-permute-start(bf16[776,128]{1,0:T(8,128)(2,1)S(1)} %collective-permute-done.refs_0_), channel_id=1, source_target_pairs={{0,2},{2,4},{4,6},{6,7},{7,5},{5,3},{3,1},{1,0},{8,10},{10,12},{12... | collective-permute-start | bytes 595976 | tf_op jit(solution)/shard_map/ppermute | solution.py:197
  19.6 8.0 %collective-permute-start.5 = (bf16[776,128]{1,0:T(8,128)(2,1)}, bf16[776,128]{1,0:T(8,128)(2,1)S(1)}, u32[]{:S(2)}, u32[]{:S(2)}) collective-permute-start(bf16[776,128]{1,0:T(8,128)(2,1)} %collective-permute-done.1.refs_1_), channel_id=1, source_target_pairs={{2,0},{4,2},{6,4},{7,6},{5,7},{3,5},{1,3},{0,1},{10,8},{12,10},{14... | collective-permute-start | bytes 595976 | tf_op jit(solution)/shard_map/ppermute | solution.py:197
  21.9 9.3 %collective-permute-start.10 = (bf16[776,128]{1,0:T(8,128)(2,1)S(1)}, bf16[776,128]{1,0:T(8,128)(2,1)S(1)}, u32[]{:S(2)}, u32[]{:S(2)}) collective-permute-start(bf16[776,128]{1,0:T(8,128)(2,1)S(1)} %collective-permute-done.6.refs_0_), channel_id=1, source_target_pairs={{0,2},{2,4},{4,6},{6,7},{7,5},{5,3},{3,1},{1,0},{8,10},{10,12},{12... | collective-permute-start | bytes 595976 | tf_op jit(solution)/shard_map/ppermute | solution.py:197
  23.6 8.2 %collective-permute-start.11 = (bf16[776,128]{1,0:T(8,128)(2,1)S(1)}, bf16[776,128]{1,0:T(8,128)(2,1)S(1)}, u32[]{:S(2)}, u32[]{:S(2)}) collective-permute-start(bf16[776,128]{1,0:T(8,128)(2,1)S(1)} %collective-permute-done.7.refs_1_), channel_id=1, source_target_pairs={{2,0},{4,2},{6,4},{7,6},{5,7},{3,5},{1,3},{0,1},{10,8},{12,10},{14... | collective-permute-start | bytes 595976 | tf_op jit(solution)/shard_map/ppermute | solution.py:197
  27.7 7.7 %collective-permute-start.8 = (bf16[776,128]{1,0:T(8,128)(2,1)S(1)}, bf16[776,128]{1,0:T(8,128)(2,1)S(1)}, u32[]{:S(2)}, u32[]{:S(2)}) collective-permute-start(bf16[776,128]{1,0:T(8,128)(2,1)S(1)} %collective-permute-done.4.refs_0_), channel_id=1, source_target_pairs={{0,2},{2,4},{4,6},{6,7},{7,5},{5,3},{3,1},{1,0},{8,10},{10,12},{12... | collective-permute-start | bytes 595976 | tf_op jit(solution)/shard_map/ppermute | solution.py:197
  29.3 6.5 %collective-permute-start.9 = (bf16[776,128]{1,0:T(8,128)(2,1)S(1)}, bf16[776,128]{1,0:T(8,128)(2,1)S(1)}, u32[]{:S(2)}, u32[]{:S(2)}) collective-permute-start(bf16[776,128]{1,0:T(8,128)(2,1)S(1)} %collective-permute-done.5.refs_1_), channel_id=1, source_target_pairs={{2,0},{4,2},{6,4},{7,6},{5,7},{3,5},{1,3},{0,1},{10,8},{12,10},{14... | collective-permute-start | bytes 595976 | tf_op jit(solution)/shard_map/ppermute | solution.py:197
  31.2 7.1 %copy-start.2 = (s32[16]{0:T(128)S(1)}, s32[16]{0:T(128)}, u32[]{:S(2)}) copy-start(s32[16]{0:T(128)} %owners_ref.3) | copy-start | bytes 196
  31.9 6.1 %collective-permute-start.13 = (bf16[776,128]{1,0:T(8,128)(2,1)S(1)}, bf16[776,128]{1,0:T(8,128)(2,1)S(1)}, u32[]{:S(2)}, u32[]{:S(2)}) collective-permute-start(bf16[776,128]{1,0:T(8,128)(2,1)S(1)} %collective-permute-done.11.refs_1_), channel_id=1, source_target_pairs={{2,0},{4,2},{6,4},{7,6},{5,7},{3,5},{1,3},{0,1},{10,8},{12,10},{14... | collective-permute-start | bytes 595976 | tf_op jit(solution)/shard_map/ppermute | solution.py:197
  32.5 5.7 %collective-permute-start.12 = (bf16[776,128]{1,0:T(8,128)(2,1)S(1)}, bf16[776,128]{1,0:T(8,128)(2,1)S(1)}, u32[]{:S(2)}, u32[]{:S(2)}) collective-permute-start(bf16[776,128]{1,0:T(8,128)(2,1)S(1)} %collective-permute-done.10.refs_0_), channel_id=1, source_target_pairs={{0,2},{2,4},{4,6},{6,7},{7,5},{5,3},{3,1},{1,0},{8,10},{10,12},{12... | collective-permute-start | bytes 595976 | tf_op jit(solution)/shard_map/ppermute | solution.py:197
  40.8 2.0 %collective-permute-start.14 = (f32[256,512]{1,0:T(8,128)S(1)}, f32[256,512]{1,0:T(8,128)S(1)}, u32[]{:S(2)}, u32[]{:S(2)}) collective-permute-start(f32[256,512]{1,0:T(8,128)S(1)} %get-tuple-element.83), channel_id=1, source_target_pairs={{0,8},{8,0},{16,24},{24,16},{1,9},{9,1},{17,25},{25,17},{2,10},{10... | collective-permute-start | bytes 1572872 | tf_op jit(solution)/shard_map/ppermute | solution.py:243
  40.8 10.4 %copy-start.3 = (f32[256,512]{1,0:T(8,128)S(1)}, f32[256,512]{1,0:T(8,128)}, u32[]{:S(2)}) copy-start(f32[256,512]{1,0:T(8,128)} %param.19) | copy-start | bytes 1572868
  41.9 2.5 %collective-permute-start.16 = (f32[256,512]{1,0:T(8,128)S(1)}, f32[256,512]{1,0:T(8,128)S(1)}, u32[]{:S(2)}, u32[]{:S(2)}) collective-permute-start(f32[256,512]{1,0:T(8,128)S(1)} %get-tuple-element.86), channel_id=1, source_target_pairs={{0,8},{8,0},{16,24},{24,16},{1,9},{9,1},{17,25},{25,17},{2,10},{10... | collective-permute-start | bytes 1572872 | tf_op jit(solution)/shard_map/ppermute | solution.py:254
  42.8 8.4 %collective-permute-start.15 = (f16[256,512]{1,0:T(8,128)(2,1)S(1)}, f16[256,512]{1,0:T(8,128)(2,1)S(1)}, u32[]{:S(2)}, u32[]{:S(2)}) collective-permute-start(f16[256,512]{1,0:T(8,128)(2,1)S(1)} %multiply_convert_fusion), channel_id=1, source_target_pairs={{0,16},{8,24},{16,0},{24,8},{1,17},{9,25},{17,1},{25,9},{2,18},{10... | collective-permute-start | bytes 786440 | tf_op jit(solution)/shard_map/ppermute | solution.py:244

commit v5 on v4

--- a/solution.py
+++ b/solution.py
@@ -76,25 +76,25 @@
 
 def slots_of(group, owned, tiles, n_dev, me_ref, owners_ref):
     place = ring_place(me_ref[1], n_dev)
-    return [arrival(owners_ref[group * owned + i], place, tiles, n_dev) for i in range(owned)]
+    slots = [arrival(owners_ref[group * owned + i], place, tiles, n_dev) for i in range(owned)]
+    ranks = [sum((other < slot).astype(jnp.int32) for other in slots) for slot in slots]
+    return list(zip(slots, ranks))
 
 
 def tile_rows(ref, at):
     return ref.at[pl.ds(pl.multiple_of(at * TS, TS), TS), :]
 
 
-def pick(part_refs, slots, out_ref):
-    for i, slot in enumerate(slots):
-        low = 0
-        for part_ref in part_refs:
-            high = low + part_ref.shape[0] // TS
-
-            @pl.when((slot >= low) & (slot < high))
-            def _():
-                at = jnp.clip(slot - low, 0, high - low - 1)
-                out_ref[i * TS : (i + 1) * TS, :] = tile_rows(part_ref, at)[...]
-
-            low = high
+def pick(part_refs, slot, out_ref, at, wanted=True):
+    low = 0
+    for part_ref in part_refs:
+        high = low + part_ref.shape[0] // TS
+
+        @pl.when((slot >= low) & (slot < high) & wanted)
+        def _():
+            tile_rows(out_ref, at)[...] = tile_rows(part_ref, jnp.clip(slot - low, 0, high - low - 1))[...]
+
+        low = high
 
 
 def partner(group):
@@ -106,21 +106,38 @@
     multiply(ids_ref, refs[:n], ladder_ref, cycle_ref, ladder_slots, slots, rows_ref, out_ref)
 
 
-def last_kernel(n, ladder_slots, slots, n_parts, tiles, n_dev, n_grp, ids_ref, me_ref, owners_ref, *refs):
+def leaving_kernel(
+    n, ladder_slots, slots, n_parts, tiles, n_dev, n_grp, owned, ranks, ids_ref, me_ref, owners_ref, *refs
+):
     amp_refs, (ladder_ref, cycle_ref), part_refs = refs[:n], refs[n : n + 2], refs[n + 2 :][:n_parts]
     new_ref, *out_refs, rows_ref = refs[n + 2 + n_parts :]
     multiply(ids_ref, amp_refs, ladder_ref, cycle_ref, ladder_slots, slots, rows_ref, new_ref)
-    owned = out_refs[0].shape[0] // TS
     for k, shift in enumerate(range(2, n_grp, 2)):
         group = lax.rem(me_ref[0] + shift, n_grp)
         for owner, out_ref in zip((group, partner(group)), out_refs[2 * k :]):
-            pick(part_refs + (new_ref,), slots_of(owner, owned, tiles, n_dev, me_ref, owners_ref), out_ref)
-
-
-def own_kernel(n_parts, tiles, n_dev, me_ref, owners_ref, *refs):
-    owned = refs[-1].shape[0] // TS
+            for slot, rank in slots_of(owner, owned, tiles, n_dev, me_ref, owners_ref):
+                wanted = (rank >= ranks.start) & (rank < ranks.stop)
+                at = jnp.clip(rank - ranks.start, 0, len(ranks) - 1)
+                pick(part_refs + (new_ref,), slot, out_ref, at, wanted)
+
+
+def staying_kernel(n_parts, tiles, n_dev, owned, me_ref, owners_ref, *refs):
     for owner, out_ref in zip((me_ref[0], partner(me_ref[0])), refs[n_parts:]):
-        pick(refs[:n_parts], slots_of(owner, owned, tiles, n_dev, me_ref, owners_ref), out_ref)
+        for i, (slot, _) in enumerate(slots_of(owner, owned, tiles, n_dev, me_ref, owners_ref)):
+            pick(refs[:n_parts], slot, out_ref, i)
+
+
+def finish_kernel(tiles, n_dev, owned, me_ref, owners_ref, base_ref, mine_ref, got_ref, *refs):
+    other_refs, out_ref = refs[:-1], refs[-1]
+    for i, (_, rank) in enumerate(slots_of(me_ref[0], owned, tiles, n_dev, me_ref, owners_ref)):
+        rows = slice(i * TS, (i + 1) * TS)
+        total = base_ref[rows, :] + (mine_ref[rows, :] + got_ref[rows, :])
+        for soon_ref, late_ref in zip(other_refs[::2], other_refs[1::2]):
+            n_soon = soon_ref.shape[0] // TS
+            soon = tile_rows(soon_ref, jnp.minimum(rank, n_soon - 1))[...]
+            late = tile_rows(late_ref, jnp.maximum(rank - n_soon, 0))[...]
+            total = total + jnp.where(rank < n_soon, soon, late)
+        out_ref[rows, :] = total
 
 
 def call(kernel, out_shape, n_smem, args, scratch=()):
@@ -157,7 +174,10 @@
     backward = [(b, a) for a, b in forward]
     swap = [(g, g ^ 1) for g in range(n_grp)]
 
-    own = jnp.concatenate([rows_of(ladder_amps), rows_of(cycle_amps)], axis=1)
+    own = rows_of(jnp.concatenate([ladder_amps, cycle_amps], axis=1))
+    own, ladder_ids, ladder_count, cycle_ids, cycle_count = lax.optimization_barrier(
+        (own, ladder_ids, ladder_count, cycle_ids, cycle_count)
+    )
     marks = jnp.concatenate(
         [marked(ladder_ids, ladder_count), marked(cycle_ids, cycle_count)], axis=1
     ).reshape(1, -1)
@@ -204,54 +224,76 @@
     def products_of(wave, pieces):
         return products(pieces, marks_in(wave, pieces))
 
+    def leaving(amps, ids, ranks):
+        new, *rows_for = call(
+            functools.partial(
+                leaving_kernel, len(amps), ladder_slots, slots, len(parts), tiles, n_dev, n_grp, owned, ranks
+            ),
+            (sums(len(amps)),) + (sums(len(ranks)),) * (n_grp - 2),
+            3,
+            [ids, me, owners, *amps, ladder_panel, cycle_panel, *parts],
+            rows_scratch,
+        )
+        return new, rows_for
+
+    def core_sums(rows_for):
+        return [
+            rows_for[2 * k] + lax.ppermute(rows_for[2 * k + 1], "grp", swap) for k in range(len(shifts))
+        ]
+
+    def x_sums(chip):
+        return [
+            lax.ppermute(
+                (rows * SCALE).astype(jnp.float16), "grp", [(g, (g + shift) % n_grp) for g in range(n_grp)]
+            ).astype(jnp.float32)
+            * (1 / SCALE)
+            for shift, rows in zip(shifts, chip)
+        ]
+
+    def landed_after(parts, flying):
+        landed = []
+        for piece in flying:
+            piece, parts = lax.optimization_barrier((piece, parts))
+            landed.append(piece)
+        return landed, parts
+
     first = hop(0, [own[t] for _, t in waves[0]])
     parts = [products(own, marks.reshape(-1))]
     own, parts = lax.optimization_barrier((own, parts))
     second = hop(1, [own[t] for _, t in waves[1]])
     for step in range(1, n_dev // 2):
-        first, parts = lax.optimization_barrier((first, parts))
-        landed, first = first, hop(0, first)
+        landed, parts = landed_after(parts, first)
+        first = hop(0, landed)
         if step < n_dev // 2 - 1:
             parts.append(products_of(0, landed))
-            second, parts = lax.optimization_barrier((second, parts))
-            landed, second = second, hop(1, second)
+            landed, parts = landed_after(parts, second)
+            second = hop(1, landed)
             parts.append(products_of(1, landed))
-        else:
-            parts.append(products_of(0, landed))
-            second, parts = lax.optimization_barrier((second, parts))
-    pieces = second + first
-    new, *leaving = call(
-        functools.partial(
-            last_kernel, len(pieces), ladder_slots, slots, len(parts), tiles, n_dev, n_grp
-        ),
-        (sums(len(pieces)),) + (sums(owned),) * (n_grp - 2),
-        3,
-        [
-            jnp.concatenate([marks_in(1, second), marks_in(0, first)]),
-            me,
-            owners,
-            *pieces,
-            ladder_panel,
-            cycle_panel,
-            *parts,
-        ],
-        rows_scratch,
-    )
+    n_soon = owned - tiles
+    parts.append(products_of(0, landed))
+    second, parts = lax.optimization_barrier((second, parts))
+    parts = [jnp.concatenate(parts, axis=0)]
+    new, rows_for = leaving(second, marks_in(1, second), range(n_soon))
     parts.append(new)
-    total = base
-    for k, shift in enumerate(shifts):
-        chip = leaving[2 * k] + lax.ppermute(leaving[2 * k + 1], "grp", swap)
-        sent = lax.ppermute(
-            (chip * SCALE).astype(jnp.float16), "grp", [(g, (g + shift) % n_grp) for g in range(n_grp)]
-        )
-        total = total + sent.astype(jnp.float32) * (1 / SCALE)
+    soon = x_sums(core_sums(rows_for))
+    new, rows_for = leaving(first, marks_in(0, first), range(n_soon, owned))
+    parts.append(new)
+    late = core_sums(rows_for)
+    late, parts = lax.optimization_barrier((late, parts))
+    late = x_sums(late)
     mine, partners = call(
-        functools.partial(own_kernel, len(parts), tiles, n_dev),
+        functools.partial(staying_kernel, len(parts), tiles, n_dev, owned),
         (sums(owned), sums(owned)),
         2,
         [me, owners, *parts],
     )
-    return total + (mine + lax.ppermute(partners, "grp", swap))
+    got = lax.ppermute(partners, "grp", swap)
+    return call(
+        functools.partial(finish_kernel, tiles, n_dev, owned),
+        jax.ShapeDtypeStruct(base.shape, base.dtype),
+        2,
+        [me, owners, base, mine, got, *(rows for pair in zip(soon, late) for rows in pair)],
+    )
 
 
 def solution(mesh):

time: 52.4 us -> 50 us (0.954)
  waiting for transfers between devices: 17.3 us -> 11.7 us
  Pallas kernels: 12.2 us -> 14.3 us
  starting transfers between devices: 17.6 us -> 18.9 us
  local copies, waits for them, and re-layouts: 3.01 us -> 1.97 us
  other arithmetic: 1.89 us -> 2.61 us
    ppermute x14, waiting for transfers between devices: 10.2 us -> 7.13 us  [hop(): lax.ppermute(piece, 'dev', forward if ahead else backward)]
    ppermute x3 -> x5, waiting for transfers between devices: 7.11 us -> 4.53 us  [the longest x2 4.52 us: x_sums(): lax.ppermute((rows * SCALE).astype(jnp.float16), 'grp', [(g, (g + shift)...]
    pallas_call x8 -> x10, Pallas kernels: 12.2 us -> 14.3 us  [call(): pl.pallas_call(kernel, out_shape=out_shape, in_specs=[SMEM] * n_smem + [V...]
    concatenate x1, other arithmetic: 0.08 us -> 1.57 us  [per_device(): own = rows_of(jnp.concatenate([ladder_amps, cycle_amps], axis=1))]
    ppermute x3 -> x5, starting transfers between devices: 2.18 us -> 3.39 us  [the longest x2 2.96 us: x_sums(): lax.ppermute((rows * SCALE).astype(jnp.float16), 'grp', [(g, (g + shift)...]
    unnamed x21, local copies, waits for them, and re-layouts: 1.29 us -> 0.14 us
    add x1, other arithmetic: 0.98 us -> 0.04 us  [core_sums(): rows_for[2 * k] + lax.ppermute(rows_for[2 * k + 1], 'grp', swap)]
  transfers between devices with their start and end apart: 17 -> 19, of which waited for: 10 -> 9; matrix products, arithmetic and copies ran while one was open for 4% -> 4% of each run, Pallas kernels for 19% -> 26%
where the time goes in v5:
time: 50 us; the launch traced here: 49.8 us
  starting transfers between devices  18.9 us (38%)
  Pallas kernels  14.3 us (29%)
  waiting for transfers between devices  11.7 us (23%)
  other arithmetic  2.61 us (5%)
  local copies, waits for them, and re-layouts  1.97 us (4%)
    ppermute x14, starting transfers between devices, hop(): lax.ppermute(piece, 'dev', forward if ahead else backward)  15.5 us
    pallas_call x10, Pallas kernels, call(): pl.pallas_call(kernel, out_shape=out_shape, in_specs=[SMEM] * n_smem + [V...  14.3 us
    ppermute x14, waiting for transfers between devices, hop(): lax.ppermute(piece, 'dev', forward if ahead else backward)  7.13 us
    ppermute x2, waiting for transfers between devices, x_sums(): lax.ppermute((rows * SCALE).astype(jnp.float16), 'grp', [(g, (g + shift)...  4.52 us
    ppermute x2, starting transfers between devices, x_sums(): lax.ppermute((rows * SCALE).astype(jnp.float16), 'grp', [(g, (g + shift)...  2.96 us
    concatenate x1, other arithmetic, per_device(): own = rows_of(jnp.concatenate([ladder_amps, cycle_amps], axis=1))  1.57 us
    convert_element_type x13, local copies, waits for them, and re-layouts, marks_of(): return piece[slots * HALF, t * slots:(t + 1) * slots].astype(jnp.int32)  1.21 us
  transfers between devices with their start and end apart: 19, of which 9 were waited for; matrix products, arithmetic and copies ran while one was open for 4% of the time, Pallas kernels for 26%

profile of v5, /device:TPU:0, one launch (start us, length us, event | category | flops | bytes accessed | tf_op | source)
XLA Modules:
  0.0 49.8 jit_solution(5083812838032266059)
XLA Ops:
  0.0 1.6 %pad_maximum_fusion = bf16[2,24,4096]{2,0,1:T(2,128)(2,1)S(1)} fusion(bf16[2,6,4096]{2,0,1:T(2,128)(2,1)} %param.13, bf16[2,18,4096]{2,0,1:T(2,128)(2,1)} %param.10), kind=kLoop, calls=%fused_computation.2 | loop fusion | flops 196608 | bytes 786432 | tf_op jit(solution)/shard_map/concatenate | solution.py:177
  1.6 0.2 copy.11
  2.4 3.1 %collective-permute-start = (bf16[776,128]{1,0:T(8,128)(2,1)S(1)}, bf16[776,128]{1,0:T(8,128)(2,1)}, u32[]{:S(2)}, u32[]{:S(2)}) collective-permute-start(bf16[776,128]{1,0:T(8,128)(2,1)S(1)} %get-tuple-element.80.refs_0_), channel_id=1, source_target_pairs={{0,2},{2,4},{4,6},{6,7},{7,5},{5,3},{3,1},{1,0},{8,10},{10,12},{12... | collective-permute-start | bytes 595976 | tf_op jit(solution)/shard_map/ppermute | solution.py:217
  5.6 1.4 %shard_map.100 = f32[128,512]{1,0:T(8,128)S(1)} custom-call(s32[48]{0:T(128)S(1)} %reshape_reshape.3.ids_ref, bf16[776,128]{1,0:T(8,128)(2,1)S(1)} %get-tuple-element.80.refs_0_, bf16[776,128]{1,0:T(8,128)(2,1)S(1)} %get-tuple-element.81.refs_1_, bf16[1536,512]{1,0:T(8,128)(2,1)S(1)} %copy-done, bf16[512,512]{1,0:T(8,128)(2,1)S(1)} %copy-done.1), custom_call_target="tpu_custom_call" | custom-call | flops 1 | bytes 1 | tf_op jit(solution)/shard_map/pallas_call | solution.py:146
  7.0 2.1 %collective-permute-start.3 = (bf16[776,128]{1,0:T(8,128)(2,1)S(1)}, bf16[776,128]{1,0:T(8,128)(2,1)S(1)}, u32[]{:S(2)}, u32[]{:S(2)}) collective-permute-start(bf16[776,128]{1,0:T(8,128)(2,1)S(1)} %get-tuple-element.81.refs_1_), channel_id=1, source_target_pairs={{0,2},{2,4},{4,6},{6,7},{7,5},{5,3},{3,1},{1,0},{8,10},{10,12},{12... | collective-permute-start | bytes 595976 | tf_op jit(solution)/shard_map/ppermute | solution.py:217
  9.1 2.2 %collective-permute-done.refs_0_ = bf16[776,128]{1,0:T(8,128)(2,1)} collective-permute-done((bf16[776,128]{1,0:T(8,128)(2,1)S(1)}, bf16[776,128]{1,0:T(8,128)(2,1)}, u32[]{:S(2)}, u32[]{:S(2)}) %collective-permute-start) | collective-permute-done | bytes 198688 | tf_op jit(solution)/shard_map/ppermute | solution.py:217
  11.3 2.1 %collective-permute-start.1 = (bf16[776,128]{1,0:T(8,128)(2,1)}, bf16[776,128]{1,0:T(8,128)(2,1)S(1)}, u32[]{:S(2)}, u32[]{:S(2)}) collective-permute-start(bf16[776,128]{1,0:T(8,128)(2,1)} %collective-permute-done.refs_0_), channel_id=1, source_target_pairs={{0,2},{2,4},{4,6},{6,7},{7,5},{5,3},{3,1},{1,0},{8,10},{10,12},{12... | collective-permute-start | bytes 595976 | tf_op jit(solution)/shard_map/ppermute | solution.py:217
  13.4 0.7 %slice_bitcast_fusion.15 = bf16[24]{0:T(256)(128)(2,1)S(1)} fusion(bf16[776,128]{1,0:T(8,128)(2,1)} %collective-permute-done.refs_0_), kind=kLoop, calls=%fused_computation.41 | loop fusion | bytes 96 | tf_op jit(solution)/shard_map/convert_element_type | solution.py:188
  14.3 1.8 %shard_map.101 = f32[128,512]{1,0:T(8,128)S(1)} custom-call(s32[48]{0:T(128)S(1)} %maximum_convert_fusion.ids_ref, bf16[776,128]{1,0:T(8,128)(2,1)} %collective-permute-done.refs_0_, bf16[776,128]{1,0:T(8,128)(2,1)S(1)} %collective-permute-done.4.refs_1_, bf16[1536,512]{1,0:T(8,128)(2,1)S(1)} %copy-done, bf16[512,512]{1,0:T(8,128)(2,1)S(1)} %copy-done.1), custom_call_target="tpu_custom_call" | custom-call | flops 1 | bytes 1 | tf_op jit(solution)/shard_map/pallas_call | solution.py:146
  16.1 2.1 %collective-permute-start.7 = (bf16[776,128]{1,0:T(8,128)(2,1)S(1)}, bf16[776,128]{1,0:T(8,128)(2,1)S(1)}, u32[]{:S(2)}, u32[]{:S(2)}) collective-permute-start(bf16[776,128]{1,0:T(8,128)(2,1)S(1)} %collective-permute-done.3.refs_0_), channel_id=1, source_target_pairs={{0,2},{2,4},{4,6},{6,7},{7,5},{5,3},{3,1},{1,0},{8,10},{10,12},{12... | collective-permute-start | bytes 595976 | tf_op jit(solution)/shard_map/ppermute | solution.py:217
  18.3 1.4 %shard_map.102 = f32[128,512]{1,0:T(8,128)S(1)} custom-call(s32[48]{0:T(128)S(1)} %maximum_convert_fusion.1.ids_ref, bf16[776,128]{1,0:T(8,128)(2,1)S(1)} %collective-permute-done.3.refs_0_, bf16[776,128]{1,0:T(8,128)(2,1)S(1)} %collective-permute-done.2.refs_1_, bf16[1536,512]{1,0:T(8,128)(2,1)S(1)} %copy-done, bf16[512,512]{1,0:T(8,128)(2,1)S(1)} %copy-done.1), custom_call_target="tpu_custom_call" | custom-call | flops 1 | bytes 1 | tf_op jit(solution)/shard_map/pallas_call | solution.py:146
  19.7 2.1 %collective-permute-start.5 = (bf16[776,128]{1,0:T(8,128)(2,1)S(1)}, bf16[776,128]{1,0:T(8,128)(2,1)S(1)}, u32[]{:S(2)}, u32[]{:S(2)}) collective-permute-start(bf16[776,128]{1,0:T(8,128)(2,1)S(1)} %collective-permute-done.1.refs_0_), channel_id=1, source_target_pairs={{0,2},{2,4},{4,6},{6,7},{7,5},{5,3},{3,1},{1,0},{8,10},{10,12},{12... | collective-permute-start | bytes 595976 | tf_op jit(solution)/shard_map/ppermute | solution.py:217
  21.9 0.3 collective-permute-done.8.refs_1_
  22.3 1.4 %shard_map.103 = f32[128,512]{1,0:T(8,128)S(1)} custom-call(s32[48]{0:T(128)S(1)} %maximum_convert_fusion.2.ids_ref, bf16[776,128]{1,0:T(8,128)(2,1)S(1)} %collective-permute-done.1.refs_0_, bf16[776,128]{1,0:T(8,128)(2,1)S(1)} %collective-permute-done.8.refs_1_, bf16[1536,512]{1,0:T(8,128)(2,1)S(1)} %copy-done, bf16[512,512]{1,0:T(8,128)(2,1)S(1)} %copy-done.1), custom_call_target="tpu_custom_call" | custom-call | flops 1 | bytes 1 | tf_op jit(solution)/shard_map/pallas_call | solution.py:146
  23.7 0.3 collective-permute-done.7.refs_0_
  24.0 2.4 %collective-permute-done.6.refs_1_ = bf16[776,128]{1,0:T(8,128)(2,1)S(1)} collective-permute-done((bf16[776,128]{1,0:T(8,128)(2,1)S(1)}, bf16[776,128]{1,0:T(8,128)(2,1)S(1)}, u32[]{:S(2)}, u32[]{:S(2)}) %collective-permute-start.6) | collective-permute-done | bytes 198688 | tf_op jit(solution)/shard_map/ppermute | solution.py:217
  26.6 2.0 %collective-permute-start.12 = (bf16[776,128]{1,0:T(8,128)(2,1)S(1)}, bf16[776,128]{1,0:T(8,128)(2,1)S(1)}, u32[]{:S(2)}, u32[]{:S(2)}) collective-permute-start(bf16[776,128]{1,0:T(8,128)(2,1)S(1)} %collective-permute-done.7.refs_0_), channel_id=1, source_target_pairs={{0,2},{2,4},{4,6},{6,7},{7,5},{5,3},{3,1},{1,0},{8,10},{10,12},{12... | collective-permute-start | bytes 595976 | tf_op jit(solution)/shard_map/ppermute | solution.py:217
  28.6 1.4 %shard_map.104 = f32[128,512]{1,0:T(8,128)S(1)} custom-call(s32[48]{0:T(128)S(1)} %maximum_convert_fusion.3.ids_ref, bf16[776,128]{1,0:T(8,128)(2,1)S(1)} %collective-permute-done.7.refs_0_, bf16[776,128]{1,0:T(8,128)(2,1)S(1)} %collective-permute-done.6.refs_1_, bf16[1536,512]{1,0:T(8,128)(2,1)S(1)} %copy-done, bf16[512,512]{1,0:T(8,128)(2,1)S(1)} %copy-done.1), custom_call_target="tpu_custom_call" | custom-call | flops 1 | bytes 1 | tf_op jit(solution)/shard_map/pallas_call | solution.py:146
  30.0 0.7 %collective-permute-done.10.refs_1_ = bf16[776,128]{1,0:T(8,128)(2,1)S(1)} collective-permute-done((bf16[776,128]{1,0:T(8,128)(2,1)S(1)}, bf16[776,128]{1,0:T(8,128)(2,1)S(1)}, u32[]{:S(2)}, u32[]{:S(2)}) %collective-permute-start.10) | collective-permute-done | bytes 198688 | tf_op jit(solution)/shard_map/ppermute | solution.py:217
  30.9 2.0 %collective-permute-start.9 = (bf16[776,128]{1,0:T(8,128)(2,1)S(1)}, bf16[776,128]{1,0:T(8,128)(2,1)S(1)}, u32[]{:S(2)}, u32[]{:S(2)}) collective-permute-start(bf16[776,128]{1,0:T(8,128)(2,1)S(1)} %collective-permute-done.5.refs_0_), channel_id=1, source_target_pairs={{0,2},{2,4},{4,6},{6,7},{7,5},{5,3},{3,1},{1,0},{8,10},{10,12},{12... | collective-permute-start | bytes 595976 | tf_op jit(solution)/shard_map/ppermute | solution.py:217
  32.9 1.4 %shard_map.105 = f32[128,512]{1,0:T(8,128)S(1)} custom-call(s32[48]{0:T(128)S(1)} %maximum_convert_fusion.5.ids_ref, bf16[776,128]{1,0:T(8,128)(2,1)S(1)} %collective-permute-done.5.refs_0_, bf16[776,128]{1,0:T(8,128)(2,1)S(1)} %collective-permute-done.10.refs_1_, bf16[1536,512]{1,0:T(8,128)(2,1)S(1)} %copy-done, bf16[512,512]{1,0:T(8,128)(2,1)S(1)} %copy-done.1), custom_call_target="tpu_custom_call" | custom-call | flops 1 | bytes 1 | tf_op jit(solution)/shard_map/pallas_call | solution.py:146
  34.3 0.7 %collective-permute-done.13.refs_1_ = bf16[776,128]{1,0:T(8,128)(2,1)S(1)} collective-permute-done((bf16[776,128]{1,0:T(8,128)(2,1)S(1)}, bf16[776,128]{1,0:T(8,128)(2,1)S(1)}, u32[]{:S(2)}, u32[]{:S(2)}) %collective-permute-start.13) | collective-permute-done | bytes 198688 | tf_op jit(solution)/shard_map/ppermute | solution.py:217
  35.3 1.6 %shard_map.106 = (f32[128,512]{1,0:T(8,128)S(1)}, f32[128,512]{1,0:T(8,128)S(1)}, f32[128,512]{1,0:T(8,128)S(1)}) custom-call(s32[48]{0:T(128)S(1)} %maximum_convert_fusion.6.ids_ref, s32[2]{0:T(128)S(1)} %pad_add_fusion.1.me_ref, s32[16]{0:T(128)S(1)} %copy-done.3, bf16[776,128]{1,0:T(8,128)(2,1)S(1)} %collective-permute-done.12.refs_0_, ...), custom_call_target="tpu_custom_call" | custom-call | flops 1 | bytes 1 | tf_op jit(solution)/shard_map/pallas_call | solution.py:146
  37.0 0.5 collective-permute-done.11.refs_1_
  37.6 1.7 %shard_map.107 = (f32[128,512]{1,0:T(8,128)S(1)}, f32[128,512]{1,0:T(8,128)S(1)}, f32[128,512]{1,0:T(8,128)S(1)}) custom-call(s32[48]{0:T(128)S(1)} %maximum_convert_fusion.4.ids_ref, s32[2]{0:T(128)S(1)} %pad_add_fusion.1.me_ref, s32[16]{0:T(128)S(1)} %copy-done.3, bf16[776,128]{1,0:T(8,128)(2,1)S(1)} %collective-permute-done.9.refs_0_, ...), custom_call_target="tpu_custom_call" | custom-call | flops 1 | bytes 1 | tf_op jit(solution)/shard_map/pallas_call | solution.py:146
  39.4 1.6 %collective-permute-start.17 = (f16[128,512]{1,0:T(8,128)(2,1)S(1)}, f16[128,512]{1,0:T(8,128)(2,1)S(1)}, u32[]{:S(2)}, u32[]{:S(2)}) collective-permute-start(f16[128,512]{1,0:T(8,128)(2,1)S(1)} %multiply_convert_fusion.1), channel_id=1, source_target_pairs={{0,16},{8,24},{16,0},{24,8},{1,17},{9,25},{17,1},{25,9},{2,18},{10... | collective-permute-start | bytes 393224 | tf_op jit(solution)/shard_map/ppermute | solution.py:246
  41.1 0.9 %shard_map.108 = (f32[256,512]{1,0:T(8,128)S(1)}, f32[256,512]{1,0:T(8,128)S(1)}) custom-call(s32[2]{0:T(128)S(1)} %pad_add_fusion.1.me_ref, s32[16]{0:T(128)S(1)} %copy-done.3, f32[768,512]{1,0:T(8,128)S(1)} %constant_dynamic-update-slice_fusion.refs_4_.refs_0_, f32[128,512]{1,0:T(8,128)S(1)} %get-tuple-element.134.refs_5_.refs_1_, ...), custom_call_target="tpu_custom_call" | custom-call | flops 1 | bytes 1 | tf_op jit(solution)/shard_map/pallas_call | solution.py:146
  42.0 0.3 collective-permute-start.15
  42.2 1.4 %collective-permute-start.18 = (f16[128,512]{1,0:T(8,128)(2,1)S(1)}, f16[128,512]{1,0:T(8,128)(2,1)S(1)}, u32[]{:S(2)}, u32[]{:S(2)}) collective-permute-start(f16[128,512]{1,0:T(8,128)(2,1)S(1)} %multiply_convert_fusion), channel_id=1, source_target_pairs={{0,16},{8,24},{16,0},{24,8},{1,17},{9,25},{17,1},{25,9},{2,18},{10... | collective-permute-start | bytes 393224 | tf_op jit(solution)/shard_map/ppermute | solution.py:246
  43.6 1.9 %collective-permute-done.17 = f16[128,512]{1,0:T(8,128)(2,1)S(1)} collective-permute-done((f16[128,512]{1,0:T(8,128)(2,1)S(1)}, f16[128,512]{1,0:T(8,128)(2,1)S(1)}, u32[]{:S(2)}, u32[]{:S(2)}) %collective-permute-start.17) | collective-permute-done | bytes 131104 | tf_op jit(solution)/shard_map/ppermute | solution.py:246
  45.5 2.7 %collective-permute-done.18 = f16[128,512]{1,0:T(8,128)(2,1)S(1)} collective-permute-done((f16[128,512]{1,0:T(8,128)(2,1)S(1)}, f16[128,512]{1,0:T(8,128)(2,1)S(1)}, u32[]{:S(2)}, u32[]{:S(2)}) %collective-permute-start.18) | collective-permute-done | bytes 131104 | tf_op jit(solution)/shard_map/ppermute | solution.py:246
  48.3 1.5 %shard_map.109 = f32[256,512]{1,0:T(8,128)} custom-call(s32[2]{0:T(128)S(1)} %pad_add_fusion.1.me_ref, s32[16]{0:T(128)S(1)} %copy-done.3, f32[256,512]{1,0:T(8,128)S(1)} %copy-done.2, f32[256,512]{1,0:T(8,128)S(1)} %get-tuple-element.136.mine_ref, f32[256,512]{1,0:T(8,128)S(1)} %collective-permute-done.15.got_ref, ...), custom_call_target="tpu_custom_call" | custom-call | flops 1 | bytes 1 | tf_op jit(solution)/shard_map/pallas_call | solution.py:146
  (74 shorter events, 2.4 us)
Async XLA Ops:
  0.0 2.0 %copy-start.4 = (s32[2,18]{1,0:T(2,128)S(1)}, s32[2,18]{1,0:T(2,128)}, u32[]{:S(2)}) copy-start(s32[2,18]{1,0:T(2,128)} %param.11) | copy-start | bytes 436
  0.0 2.0 %copy-start.6 = (s32[2,1]{0,1:T(1,128)S(1)}, s32[2,1]{0,1:T(1,128)}, u32[]{:S(2)}) copy-start(s32[2,1]{0,1:T(1,128)} %param.12) | copy-start | bytes 28
  0.0 2.1 %copy-start.5 = (s32[2,6]{1,0:T(2,128)S(1)}, s32[2,6]{1,0:T(2,128)}, u32[]{:S(2)}) copy-start(s32[2,6]{1,0:T(2,128)} %param.14) | copy-start | bytes 148
  0.0 2.1 %copy-start.7 = (s32[2,1]{0,1:T(1,128)S(1)}, s32[2,1]{0,1:T(1,128)}, u32[]{:S(2)}) copy-start(s32[2,1]{0,1:T(1,128)} %param.15) | copy-start | bytes 28
  1.6 4.0 %copy-start = (bf16[1536,512]{1,0:T(8,128)(2,1)S(1)}, bf16[1536,512]{1,0:T(8,128)(2,1)}, u32[]{:S(2)}) copy-start(bf16[1536,512]{1,0:T(8,128)(2,1)} %refs_2_.15) | copy-start | bytes 4718596
  1.6 4.0 %copy-start.1 = (bf16[512,512]{1,0:T(8,128)(2,1)S(1)}, bf16[512,512]{1,0:T(8,128)(2,1)}, u32[]{:S(2)}) copy-start(bf16[512,512]{1,0:T(8,128)(2,1)} %refs_3_.15) | copy-start | bytes 1572868
  2.4 8.9 %collective-permute-start = (bf16[776,128]{1,0:T(8,128)(2,1)S(1)}, bf16[776,128]{1,0:T(8,128)(2,1)}, u32[]{:S(2)}, u32[]{:S(2)}) collective-permute-start(bf16[776,128]{1,0:T(8,128)(2,1)S(1)} %get-tuple-element.80.refs_0_), channel_id=1, source_target_pairs={{0,2},{2,4},{4,6},{6,7},{7,5},{5,3},{3,1},{1,0},{8,10},{10,12},{12... | collective-permute-start | bytes 595976 | tf_op jit(solution)/shard_map/ppermute | solution.py:217
  5.5 8.6 %collective-permute-start.4 = (bf16[776,128]{1,0:T(8,128)(2,1)S(1)}, bf16[776,128]{1,0:T(8,128)(2,1)S(1)}, u32[]{:S(2)}, u32[]{:S(2)}) collective-permute-start(bf16[776,128]{1,0:T(8,128)(2,1)S(1)} %get-tuple-element.81.refs_1_), channel_id=1, source_target_pairs={{2,0},{4,2},{6,4},{7,6},{5,7},{3,5},{1,3},{0,1},{10,8},{12,10},{14... | collective-permute-start | bytes 595976 | tf_op jit(solution)/shard_map/ppermute | solution.py:217
  7.0 9.1 %collective-permute-start.3 = (bf16[776,128]{1,0:T(8,128)(2,1)S(1)}, bf16[776,128]{1,0:T(8,128)(2,1)S(1)}, u32[]{:S(2)}, u32[]{:S(2)}) collective-permute-start(bf16[776,128]{1,0:T(8,128)(2,1)S(1)} %get-tuple-element.81.refs_1_), channel_id=1, source_target_pairs={{0,2},{2,4},{4,6},{6,7},{7,5},{5,3},{3,1},{1,0},{8,10},{10,12},{12... | collective-permute-start | bytes 595976 | tf_op jit(solution)/shard_map/ppermute | solution.py:217
  9.1 9.2 %collective-permute-start.2 = (bf16[776,128]{1,0:T(8,128)(2,1)S(1)}, bf16[776,128]{1,0:T(8,128)(2,1)S(1)}, u32[]{:S(2)}, u32[]{:S(2)}) collective-permute-start(bf16[776,128]{1,0:T(8,128)(2,1)S(1)} %get-tuple-element.80.refs_0_), channel_id=1, source_target_pairs={{2,0},{4,2},{6,4},{7,6},{5,7},{3,5},{1,3},{0,1},{10,8},{12,10},{14... | collective-permute-start | bytes 595976 | tf_op jit(solution)/shard_map/ppermute | solution.py:217
  11.3 8.4 %collective-permute-start.1 = (bf16[776,128]{1,0:T(8,128)(2,1)}, bf16[776,128]{1,0:T(8,128)(2,1)S(1)}, u32[]{:S(2)}, u32[]{:S(2)}) collective-permute-start(bf16[776,128]{1,0:T(8,128)(2,1)} %collective-permute-done.refs_0_), channel_id=1, source_target_pairs={{0,2},{2,4},{4,6},{6,7},{7,5},{5,3},{3,1},{1,0},{8,10},{10,12},{12... | collective-permute-start | bytes 595976 | tf_op jit(solution)/shard_map/ppermute | solution.py:217
  14.3 7.9 %collective-permute-start.8 = (bf16[776,128]{1,0:T(8,128)(2,1)S(1)}, bf16[776,128]{1,0:T(8,128)(2,1)S(1)}, u32[]{:S(2)}, u32[]{:S(2)}) collective-permute-start(bf16[776,128]{1,0:T(8,128)(2,1)S(1)} %collective-permute-done.4.refs_1_), channel_id=1, source_target_pairs={{2,0},{4,2},{6,4},{7,6},{5,7},{3,5},{1,3},{0,1},{10,8},{12,10},{14... | collective-permute-start | bytes 595976 | tf_op jit(solution)/shard_map/ppermute | solution.py:217
  16.1 7.9 %collective-permute-start.7 = (bf16[776,128]{1,0:T(8,128)(2,1)S(1)}, bf16[776,128]{1,0:T(8,128)(2,1)S(1)}, u32[]{:S(2)}, u32[]{:S(2)}) collective-permute-start(bf16[776,128]{1,0:T(8,128)(2,1)S(1)} %collective-permute-done.3.refs_0_), channel_id=1, source_target_pairs={{0,2},{2,4},{4,6},{6,7},{7,5},{5,3},{3,1},{1,0},{8,10},{10,12},{12... | collective-permute-start | bytes 595976 | tf_op jit(solution)/shard_map/ppermute | solution.py:217
  18.3 8.1 %collective-permute-start.6 = (bf16[776,128]{1,0:T(8,128)(2,1)S(1)}, bf16[776,128]{1,0:T(8,128)(2,1)S(1)}, u32[]{:S(2)}, u32[]{:S(2)}) collective-permute-start(bf16[776,128]{1,0:T(8,128)(2,1)S(1)} %collective-permute-done.2.refs_1_), channel_id=1, source_target_pairs={{2,0},{4,2},{6,4},{7,6},{5,7},{3,5},{1,3},{0,1},{10,8},{12,10},{14... | collective-permute-start | bytes 595976 | tf_op jit(solution)/shard_map/ppermute | solution.py:217
  19.7 10.3 %collective-permute-start.5 = (bf16[776,128]{1,0:T(8,128)(2,1)S(1)}, bf16[776,128]{1,0:T(8,128)(2,1)S(1)}, u32[]{:S(2)}, u32[]{:S(2)}) collective-permute-start(bf16[776,128]{1,0:T(8,128)(2,1)S(1)} %collective-permute-done.1.refs_0_), channel_id=1, source_target_pairs={{0,2},{2,4},{4,6},{6,7},{7,5},{5,3},{3,1},{1,0},{8,10},{10,12},{12... | collective-permute-start | bytes 595976 | tf_op jit(solution)/shard_map/ppermute | solution.py:217
  22.3 8.4 %collective-permute-start.10 = (bf16[776,128]{1,0:T(8,128)(2,1)S(1)}, bf16[776,128]{1,0:T(8,128)(2,1)S(1)}, u32[]{:S(2)}, u32[]{:S(2)}) collective-permute-start(bf16[776,128]{1,0:T(8,128)(2,1)S(1)} %collective-permute-done.8.refs_1_), channel_id=1, source_target_pairs={{2,0},{4,2},{6,4},{7,6},{5,7},{3,5},{1,3},{0,1},{10,8},{12,10},{14... | collective-permute-start | bytes 595976 | tf_op jit(solution)/shard_map/ppermute | solution.py:217
  26.4 8.5 %collective-permute-start.13 = (bf16[776,128]{1,0:T(8,128)(2,1)S(1)}, bf16[776,128]{1,0:T(8,128)(2,1)S(1)}, u32[]{:S(2)}, u32[]{:S(2)}) collective-permute-start(bf16[776,128]{1,0:T(8,128)(2,1)S(1)} %collective-permute-done.6.refs_1_), channel_id=1, source_target_pairs={{2,0},{4,2},{6,4},{7,6},{5,7},{3,5},{1,3},{0,1},{10,8},{12,10},{14... | collective-permute-start | bytes 595976 | tf_op jit(solution)/shard_map/ppermute | solution.py:217
  26.6 8.4 %collective-permute-start.12 = (bf16[776,128]{1,0:T(8,128)(2,1)S(1)}, bf16[776,128]{1,0:T(8,128)(2,1)S(1)}, u32[]{:S(2)}, u32[]{:S(2)}) collective-permute-start(bf16[776,128]{1,0:T(8,128)(2,1)S(1)} %collective-permute-done.7.refs_0_), channel_id=1, source_target_pairs={{0,2},{2,4},{4,6},{6,7},{7,5},{5,3},{3,1},{1,0},{8,10},{10,12},{12... | collective-permute-start | bytes 595976 | tf_op jit(solution)/shard_map/ppermute | solution.py:217
  30.8 6.7 %collective-permute-start.11 = (bf16[776,128]{1,0:T(8,128)(2,1)S(1)}, bf16[776,128]{1,0:T(8,128)(2,1)S(1)}, u32[]{:S(2)}, u32[]{:S(2)}) collective-permute-start(bf16[776,128]{1,0:T(8,128)(2,1)S(1)} %collective-permute-done.10.refs_1_), channel_id=1, source_target_pairs={{2,0},{4,2},{6,4},{7,6},{5,7},{3,5},{1,3},{0,1},{10,8},{12,10},{14... | collective-permute-start | bytes 595976 | tf_op jit(solution)/shard_map/ppermute | solution.py:217
  30.9 6.7 %collective-permute-start.9 = (bf16[776,128]{1,0:T(8,128)(2,1)S(1)}, bf16[776,128]{1,0:T(8,128)(2,1)S(1)}, u32[]{:S(2)}, u32[]{:S(2)}) collective-permute-start(bf16[776,128]{1,0:T(8,128)(2,1)S(1)} %collective-permute-done.5.refs_0_), channel_id=1, source_target_pairs={{0,2},{2,4},{4,6},{6,7},{7,5},{5,3},{3,1},{1,0},{8,10},{10,12},{12... | collective-permute-start | bytes 595976 | tf_op jit(solution)/shard_map/ppermute | solution.py:217
  34.3 1.0 %copy-start.3 = (s32[16]{0:T(128)S(1)}, s32[16]{0:T(128)}, u32[]{:S(2)}) copy-start(s32[16]{0:T(128)} %owners_ref.7) | copy-start | bytes 196
  36.9 2.5 %collective-permute-start.16 = (f32[128,512]{1,0:T(8,128)S(1)}, f32[128,512]{1,0:T(8,128)S(1)}, u32[]{:S(2)}, u32[]{:S(2)}) collective-permute-start(f32[128,512]{1,0:T(8,128)S(1)} %get-tuple-element.139), channel_id=1, source_target_pairs={{0,8},{8,0},{16,24},{24,16},{1,9},{9,1},{17,25},{25,17},{2,10},{10... | collective-permute-start | bytes 786440 | tf_op jit(solution)/shard_map/ppermute | solution.py:241
  39.3 1.7 %collective-permute-start.14 = (f32[128,512]{1,0:T(8,128)S(1)}, f32[128,512]{1,0:T(8,128)S(1)}, u32[]{:S(2)}, u32[]{:S(2)}) collective-permute-start(f32[128,512]{1,0:T(8,128)S(1)} %get-tuple-element.131), channel_id=1, source_target_pairs={{0,8},{8,0},{16,24},{24,16},{1,9},{9,1},{17,25},{25,17},{2,10},{10... | collective-permute-start | bytes 786440 | tf_op jit(solution)/shard_map/ppermute | solution.py:241
  39.4 6.1 %collective-permute-start.17 = (f16[128,512]{1,0:T(8,128)(2,1)S(1)}, f16[128,512]{1,0:T(8,128)(2,1)S(1)}, u32[]{:S(2)}, u32[]{:S(2)}) collective-permute-start(f16[128,512]{1,0:T(8,128)(2,1)S(1)} %multiply_convert_fusion.1), channel_id=1, source_target_pairs={{0,16},{8,24},{16,0},{24,8},{1,17},{9,25},{17,1},{25,9},{2,18},{10... | collective-permute-start | bytes 393224 | tf_op jit(solution)/shard_map/ppermute | solution.py:246
  41.0 7.2 %copy-start.2 = (f32[256,512]{1,0:T(8,128)S(1)}, f32[256,512]{1,0:T(8,128)}, u32[]{:S(2)}) copy-start(f32[256,512]{1,0:T(8,128)} %base_ref.1) | copy-start | bytes 1572868
  42.0 6.3 %collective-permute-start.15 = (f32[256,512]{1,0:T(8,128)S(1)}, f32[256,512]{1,0:T(8,128)S(1)}, u32[]{:S(2)}, u32[]{:S(2)}) collective-permute-start(f32[256,512]{1,0:T(8,128)S(1)} %get-tuple-element.137), channel_id=1, source_target_pairs={{0,8},{8,0},{16,24},{24,16},{1,9},{9,1},{17,25},{25,17},{2,10},{10... | collective-permute-start | bytes 1572872 | tf_op jit(solution)/shard_map/ppermute | solution.py:290
  42.2 6.0 %collective-permute-start.18 = (f16[128,512]{1,0:T(8,128)(2,1)S(1)}, f16[128,512]{1,0:T(8,128)(2,1)S(1)}, u32[]{:S(2)}, u32[]{:S(2)}) collective-permute-start(f16[128,512]{1,0:T(8,128)(2,1)S(1)} %multiply_convert_fusion), channel_id=1, source_target_pairs={{0,16},{8,24},{16,0},{24,8},{1,17},{9,25},{17,1},{25,9},{2,18},{10... | collective-permute-start | bytes 393224 | tf_op jit(solution)/shard_map/ppermute | solution.py:246

commit v6 on v5

--- a/solution.py
+++ b/solution.py
@@ -74,8 +74,8 @@
     return jnp.where(back == 0, t, slot)
 
 
-def slots_of(group, owned, tiles, n_dev, me_ref, owners_ref):
-    place = ring_place(me_ref[1], n_dev)
+def slots_of(group, owned, tiles, n_dev, owners_ref):
+    place = ring_place(lax.axis_index("dev"), n_dev)
     slots = [arrival(owners_ref[group * owned + i], place, tiles, n_dev) for i in range(owned)]
     ranks = [sum((other < slot).astype(jnp.int32) for other in slots) for slot in slots]
     return list(zip(slots, ranks))
@@ -85,14 +85,14 @@
     return ref.at[pl.ds(pl.multiple_of(at * TS, TS), TS), :]
 
 
-def pick(part_refs, slot, out_ref, at, wanted=True):
+def pick(part_refs, slot, out_ref, at):
     low = 0
     for part_ref in part_refs:
         high = low + part_ref.shape[0] // TS
 
-        @pl.when((slot >= low) & (slot < high) & wanted)
+        @pl.when((slot >= low) & (slot < high))
         def _():
-            tile_rows(out_ref, at)[...] = tile_rows(part_ref, jnp.clip(slot - low, 0, high - low - 1))[...]
+            out_ref[at * TS : (at + 1) * TS, :] = tile_rows(part_ref, jnp.clip(slot - low, 0, high - low - 1))[...]
 
         low = high
 
@@ -107,37 +107,28 @@
 
 
 def leaving_kernel(
-    n, ladder_slots, slots, n_parts, tiles, n_dev, n_grp, owned, ranks, ids_ref, me_ref, owners_ref, *refs
+    n, ladder_slots, slots, n_parts, tiles, n_dev, n_grp, owned, ranks, ids_ref, owners_ref, *refs
 ):
     amp_refs, (ladder_ref, cycle_ref), part_refs = refs[:n], refs[n : n + 2], refs[n + 2 :][:n_parts]
     new_ref, *out_refs, rows_ref = refs[n + 2 + n_parts :]
     multiply(ids_ref, amp_refs, ladder_ref, cycle_ref, ladder_slots, slots, rows_ref, new_ref)
     for k, shift in enumerate(range(2, n_grp, 2)):
-        group = lax.rem(me_ref[0] + shift, n_grp)
+        group = lax.rem(lax.axis_index("grp") + shift, n_grp)
         for owner, out_ref in zip((group, partner(group)), out_refs[2 * k :]):
-            for slot, rank in slots_of(owner, owned, tiles, n_dev, me_ref, owners_ref):
-                wanted = (rank >= ranks.start) & (rank < ranks.stop)
-                at = jnp.clip(rank - ranks.start, 0, len(ranks) - 1)
-                pick(part_refs + (new_ref,), slot, out_ref, at, wanted)
-
-
-def staying_kernel(n_parts, tiles, n_dev, owned, me_ref, owners_ref, *refs):
-    for owner, out_ref in zip((me_ref[0], partner(me_ref[0])), refs[n_parts:]):
-        for i, (slot, _) in enumerate(slots_of(owner, owned, tiles, n_dev, me_ref, owners_ref)):
-            pick(refs[:n_parts], slot, out_ref, i)
-
-
-def finish_kernel(tiles, n_dev, owned, me_ref, owners_ref, base_ref, mine_ref, got_ref, *refs):
-    other_refs, out_ref = refs[:-1], refs[-1]
-    for i, (_, rank) in enumerate(slots_of(me_ref[0], owned, tiles, n_dev, me_ref, owners_ref)):
-        rows = slice(i * TS, (i + 1) * TS)
-        total = base_ref[rows, :] + (mine_ref[rows, :] + got_ref[rows, :])
-        for soon_ref, late_ref in zip(other_refs[::2], other_refs[1::2]):
-            n_soon = soon_ref.shape[0] // TS
-            soon = tile_rows(soon_ref, jnp.minimum(rank, n_soon - 1))[...]
-            late = tile_rows(late_ref, jnp.maximum(rank - n_soon, 0))[...]
-            total = total + jnp.where(rank < n_soon, soon, late)
-        out_ref[rows, :] = total
+            found = slots_of(owner, owned, tiles, n_dev, owners_ref)
+            for at, wanted in enumerate(ranks):
+                slot = sum(jnp.where(rank == wanted, slot, 0) for slot, rank in found)
+                pick(part_refs + (new_ref,), slot, out_ref, at)
+
+
+def staying_kernel(n_parts, tiles, n_dev, owned, owners_ref, *refs):
+    part_refs, (mine_ref, partners_ref, rank_ref) = refs[:n_parts], refs[n_parts:]
+    group = lax.axis_index("grp")
+    for i, (slot, _) in enumerate(slots_of(partner(group), owned, tiles, n_dev, owners_ref)):
+        pick(part_refs, slot, partners_ref, i)
+    for i, (slot, rank) in enumerate(slots_of(group, owned, tiles, n_dev, owners_ref)):
+        pick(part_refs, slot, mine_ref, i)
+        rank_ref[i * TS : (i + 1) * TS, :] = jnp.full((TS, rank_ref.shape[1]), rank, jnp.int32)
 
 
 def call(kernel, out_shape, n_smem, args, scratch=()):
@@ -180,7 +171,8 @@
     )
     marks = jnp.concatenate(
         [marked(ladder_ids, ladder_count), marked(cycle_ids, cycle_count)], axis=1
-    ).reshape(1, -1)
+    )
+    marks = jnp.concatenate([marks[t : t + 1] for t in range(tiles)], axis=1)
     note = jnp.pad(marks.astype(jnp.bfloat16), ((0, 7), (0, 2 * TS - marks.size)))
     own = [jnp.concatenate([own[t], note], axis=0) for t in range(tiles)]
 
@@ -199,7 +191,6 @@
             rows_scratch,
         )
 
-    me = jnp.stack([lax.axis_index("grp"), lax.axis_index("dev")])
     owned = owners.shape[0] // n_grp
     shifts = range(2, n_grp, 2)
 
@@ -230,8 +221,8 @@
                 leaving_kernel, len(amps), ladder_slots, slots, len(parts), tiles, n_dev, n_grp, owned, ranks
             ),
             (sums(len(amps)),) + (sums(len(ranks)),) * (n_grp - 2),
-            3,
-            [ids, me, owners, *amps, ladder_panel, cycle_panel, *parts],
+            2,
+            [ids, owners, *amps, ladder_panel, cycle_panel, *parts],
             rows_scratch,
         )
         return new, rows_for
@@ -241,12 +232,11 @@
             rows_for[2 * k] + lax.ppermute(rows_for[2 * k + 1], "grp", swap) for k in range(len(shifts))
         ]
 
-    def x_sums(chip):
+    def sent(chip):
         return [
             lax.ppermute(
                 (rows * SCALE).astype(jnp.float16), "grp", [(g, (g + shift) % n_grp) for g in range(n_grp)]
-            ).astype(jnp.float32)
-            * (1 / SCALE)
+            )
             for shift, rows in zip(shifts, chip)
         ]
 
@@ -258,7 +248,7 @@
         return landed, parts
 
     first = hop(0, [own[t] for _, t in waves[0]])
-    parts = [products(own, marks.reshape(-1))]
+    parts = [products(own, marks_in(0, own))]
     own, parts = lax.optimization_barrier((own, parts))
     second = hop(1, [own[t] for _, t in waves[1]])
     for step in range(1, n_dev // 2):
@@ -271,29 +261,32 @@
             parts.append(products_of(1, landed))
     n_soon = owned - tiles
     parts.append(products_of(0, landed))
+    parts = [jnp.concatenate(parts, axis=0)]
     second, parts = lax.optimization_barrier((second, parts))
-    parts = [jnp.concatenate(parts, axis=0)]
     new, rows_for = leaving(second, marks_in(1, second), range(n_soon))
     parts.append(new)
-    soon = x_sums(core_sums(rows_for))
+    soon = sent(core_sums(rows_for))
     new, rows_for = leaving(first, marks_in(0, first), range(n_soon, owned))
     parts.append(new)
     late = core_sums(rows_for)
     late, parts = lax.optimization_barrier((late, parts))
-    late = x_sums(late)
-    mine, partners = call(
+    late = sent(late)
+    mine, partners, rank = call(
         functools.partial(staying_kernel, len(parts), tiles, n_dev, owned),
-        (sums(owned), sums(owned)),
-        2,
-        [me, owners, *parts],
-    )
-    got = lax.ppermute(partners, "grp", swap)
-    return call(
-        functools.partial(finish_kernel, tiles, n_dev, owned),
-        jax.ShapeDtypeStruct(base.shape, base.dtype),
-        2,
-        [me, owners, base, mine, got, *(rows for pair in zip(soon, late) for rows in pair)],
-    )
+        (sums(owned), sums(owned), jax.ShapeDtypeStruct((owned * TS, cols), jnp.int32)),
+        1,
+        [owners, *parts],
+    )
+    total = base + (mine + lax.ppermute(partners, "grp", swap))
+    rank = rank.reshape(owned, TS, cols)
+    for rows in zip(soon, late):
+        rows = [part.reshape(1, -1, TS, cols)[:, k] for part in rows for k in range(part.shape[0] // TS)]
+        chosen = rows[0]
+        for k in range(1, owned):
+            chosen = jnp.where(rank == k, rows[k], chosen)
+        chosen = chosen.astype(jnp.float32) * (1 / SCALE)
+        total = total + chosen.reshape(base.shape)
+    return total
 
 
 def solution(mesh):

time: 50 us -> 49.4 us (0.988)
  Pallas kernels: 14.3 us -> 12.3 us
  other arithmetic: 2.61 us -> 3.74 us
  waiting for transfers between devices: 11.7 us -> 12.8 us
  local copies, waits for them, and re-layouts: 1.97 us -> 1.17 us
    pallas_call x10 -> x9, Pallas kernels: 14.3 us -> 12.3 us  [call(): pl.pallas_call(kernel, out_shape=out_shape, in_specs=[SMEM] * n_smem + [V...]
    ppermute x14, waiting for transfers between devices: 7.13 us -> 8.35 us  [hop(): lax.ppermute(piece, 'dev', forward if ahead else backward)]
    add x0 -> x1, other arithmetic: none -> 1.08 us  [per_device(): total = total + chosen.reshape(base.shape)]
    convert_element_type x13 -> x14, local copies, waits for them, and re-layouts: 1.21 us -> 0.53 us  [marks_of(): return piece[slots * HALF, t * slots:(t + 1) * slots].astype(jnp.int32)]
  transfers between devices with their start and end apart: 19 -> 19, of which waited for: 9 -> 10; matrix products, arithmetic and copies ran while one was open for 4% -> 3% of each run, Pallas kernels for 26% -> 25%
where the time goes in v6:
time: 49.4 us; the launch traced here: 49.2 us
  starting transfers between devices  18.9 us (38%)
  waiting for transfers between devices  12.8 us (26%)
  Pallas kernels  12.3 us (25%)
  other arithmetic  3.74 us (8%)
  local copies, waits for them, and re-layouts  1.17 us (2%)
    ppermute x14, starting transfers between devices, hop(): lax.ppermute(piece, 'dev', forward if ahead else backward)  15.6 us
    pallas_call x9, Pallas kernels, call(): pl.pallas_call(kernel, out_shape=out_shape, in_specs=[SMEM] * n_smem + [V...  12.3 us
    ppermute x14, waiting for transfers between devices, hop(): lax.ppermute(piece, 'dev', forward if ahead else backward)  8.35 us
    ppermute x2, waiting for transfers between devices, sent(): lax.ppermute((rows * SCALE).astype(jnp.float16), 'grp', [(g, (g + shift)...  4.49 us
    ppermute x2, starting transfers between devices, sent(): lax.ppermute((rows * SCALE).astype(jnp.float16), 'grp', [(g, (g + shift)...  2.95 us
    concatenate x1, other arithmetic, per_device(): own = rows_of(jnp.concatenate([ladder_amps, cycle_amps], axis=1))  1.57 us
    add x1, other arithmetic, per_device(): total = total + chosen.reshape(base.shape)  1.08 us
  transfers between devices with their start and end apart: 19, of which 10 were waited for; matrix products, arithmetic and copies ran while one was open for 3% of the time, Pallas kernels for 25%

profile of v6, /device:TPU:0, one launch (start us, length us, event | category | flops | bytes accessed | tf_op | source)
XLA Modules:
  0.0 49.2 jit_solution(11981562973201912686)
XLA Ops:
  0.0 1.6 %pad_maximum_fusion = bf16[2,24,4096]{2,0,1:T(2,128)(2,1)S(1)} fusion(bf16[2,6,4096]{2,0,1:T(2,128)(2,1)} %param.13, bf16[2,18,4096]{2,0,1:T(2,128)(2,1)} %param.10), kind=kLoop, calls=%fused_computation.4 | loop fusion | flops 196608 | bytes 786432 | tf_op jit(solution)/shard_map/concatenate | solution.py:168
  2.4 3.1 %collective-permute-start = (bf16[776,128]{1,0:T(8,128)(2,1)S(1)}, bf16[776,128]{1,0:T(8,128)(2,1)S(1)}, u32[]{:S(2)}, u32[]{:S(2)}) collective-permute-start(bf16[776,128]{1,0:T(8,128)(2,1)S(1)} %get-tuple-element.76.refs_0_), channel_id=1, source_target_pairs={{0,2},{2,4},{4,6},{6,7},{7,5},{5,3},{3,1},{1,0},{8,10},{10,12},{12... | collective-permute-start | bytes 595976 | tf_op jit(solution)/shard_map/ppermute | solution.py:208
  5.6 1.4 %shard_map.100 = f32[128,512]{1,0:T(8,128)S(1)} custom-call(s32[48]{0:T(128)S(1)} %maximum_convert_fusion.ids_ref, bf16[776,128]{1,0:T(8,128)(2,1)S(1)} %get-tuple-element.76.refs_0_, bf16[776,128]{1,0:T(8,128)(2,1)S(1)} %get-tuple-element.77.refs_1_, bf16[1536,512]{1,0:T(8,128)(2,1)S(1)} %copy-done, bf16[512,512]{1,0:T(8,128)(2,1)S(1)} %copy-done.1), custom_call_target="tpu_custom_call" | custom-call | flops 1 | bytes 1 | tf_op jit(solution)/shard_map/pallas_call | solution.py:137
  7.0 2.1 %collective-permute-start.3 = (bf16[776,128]{1,0:T(8,128)(2,1)S(1)}, bf16[776,128]{1,0:T(8,128)(2,1)S(1)}, u32[]{:S(2)}, u32[]{:S(2)}) collective-permute-start(bf16[776,128]{1,0:T(8,128)(2,1)S(1)} %get-tuple-element.77.refs_1_), channel_id=1, source_target_pairs={{0,2},{2,4},{4,6},{6,7},{7,5},{5,3},{3,1},{1,0},{8,10},{10,12},{12... | collective-permute-start | bytes 595976 | tf_op jit(solution)/shard_map/ppermute | solution.py:208
  9.1 2.2 %collective-permute-done.refs_0_ = bf16[776,128]{1,0:T(8,128)(2,1)S(1)} collective-permute-done((bf16[776,128]{1,0:T(8,128)(2,1)S(1)}, bf16[776,128]{1,0:T(8,128)(2,1)S(1)}, u32[]{:S(2)}, u32[]{:S(2)}) %collective-permute-start) | collective-permute-done | bytes 198688 | tf_op jit(solution)/shard_map/ppermute | solution.py:208
  11.2 2.1 %collective-permute-start.1 = (bf16[776,128]{1,0:T(8,128)(2,1)S(1)}, bf16[776,128]{1,0:T(8,128)(2,1)S(1)}, u32[]{:S(2)}, u32[]{:S(2)}) collective-permute-start(bf16[776,128]{1,0:T(8,128)(2,1)S(1)} %collective-permute-done.refs_0_), channel_id=1, source_target_pairs={{0,2},{2,4},{4,6},{6,7},{7,5},{5,3},{3,1},{1,0},{8,10},{10,12},{12... | collective-permute-start | bytes 595976 | tf_op jit(solution)/shard_map/ppermute | solution.py:208
  13.5 1.4 %shard_map.101 = f32[128,512]{1,0:T(8,128)S(1)} custom-call(s32[48]{0:T(128)S(1)} %maximum_convert_fusion.1.ids_ref, bf16[776,128]{1,0:T(8,128)(2,1)S(1)} %collective-permute-done.refs_0_, bf16[776,128]{1,0:T(8,128)(2,1)S(1)} %collective-permute-done.4.refs_1_, bf16[1536,512]{1,0:T(8,128)(2,1)S(1)} %copy-done, bf16[512,512]{1,0:T(8,128)(2,1)S(1)} %copy-done.1), custom_call_target="tpu_custom_call" | custom-call | flops 1 | bytes 1 | tf_op jit(solution)/shard_map/pallas_call | solution.py:137
  14.9 0.6 %collective-permute-done.3.refs_0_ = bf16[776,128]{1,0:T(8,128)(2,1)S(1)} collective-permute-done((bf16[776,128]{1,0:T(8,128)(2,1)S(1)}, bf16[776,128]{1,0:T(8,128)(2,1)S(1)}, u32[]{:S(2)}, u32[]{:S(2)}) %collective-permute-start.3) | collective-permute-done | bytes 198688 | tf_op jit(solution)/shard_map/ppermute | solution.py:208
  15.5 2.1 %collective-permute-start.7 = (bf16[776,128]{1,0:T(8,128)(2,1)S(1)}, bf16[776,128]{1,0:T(8,128)(2,1)S(1)}, u32[]{:S(2)}, u32[]{:S(2)}) collective-permute-start(bf16[776,128]{1,0:T(8,128)(2,1)S(1)} %collective-permute-done.3.refs_0_), channel_id=1, source_target_pairs={{0,2},{2,4},{4,6},{6,7},{7,5},{5,3},{3,1},{1,0},{8,10},{10,12},{12... | collective-permute-start | bytes 595976 | tf_op jit(solution)/shard_map/ppermute | solution.py:208
  17.8 1.4 %shard_map.102 = f32[128,512]{1,0:T(8,128)S(1)} custom-call(s32[48]{0:T(128)S(1)} %maximum_convert_fusion.2.ids_ref, bf16[776,128]{1,0:T(8,128)(2,1)S(1)} %collective-permute-done.3.refs_0_, bf16[776,128]{1,0:T(8,128)(2,1)S(1)} %collective-permute-done.2.refs_1_, bf16[1536,512]{1,0:T(8,128)(2,1)S(1)} %copy-done, bf16[512,512]{1,0:T(8,128)(2,1)S(1)} %copy-done.1), custom_call_target="tpu_custom_call" | custom-call | flops 1 | bytes 1 | tf_op jit(solution)/shard_map/pallas_call | solution.py:137
  19.1 0.6 %collective-permute-done.1.refs_0_ = bf16[776,128]{1,0:T(8,128)(2,1)S(1)} collective-permute-done((bf16[776,128]{1,0:T(8,128)(2,1)S(1)}, bf16[776,128]{1,0:T(8,128)(2,1)S(1)}, u32[]{:S(2)}, u32[]{:S(2)}) %collective-permute-start.1) | collective-permute-done | bytes 198688 | tf_op jit(solution)/shard_map/ppermute | solution.py:208
  19.7 2.1 %collective-permute-start.5 = (bf16[776,128]{1,0:T(8,128)(2,1)S(1)}, bf16[776,128]{1,0:T(8,128)(2,1)S(1)}, u32[]{:S(2)}, u32[]{:S(2)}) collective-permute-start(bf16[776,128]{1,0:T(8,128)(2,1)S(1)} %collective-permute-done.1.refs_0_), channel_id=1, source_target_pairs={{0,2},{2,4},{4,6},{6,7},{7,5},{5,3},{3,1},{1,0},{8,10},{10,12},{12... | collective-permute-start | bytes 595976 | tf_op jit(solution)/shard_map/ppermute | solution.py:208
  22.0 1.4 %shard_map.103 = f32[128,512]{1,0:T(8,128)S(1)} custom-call(s32[48]{0:T(128)S(1)} %maximum_convert_fusion.3.ids_ref, bf16[776,128]{1,0:T(8,128)(2,1)S(1)} %collective-permute-done.1.refs_0_, bf16[776,128]{1,0:T(8,128)(2,1)S(1)} %collective-permute-done.8.refs_1_, bf16[1536,512]{1,0:T(8,128)(2,1)S(1)} %copy-done, bf16[512,512]{1,0:T(8,128)(2,1)S(1)} %copy-done.1), custom_call_target="tpu_custom_call" | custom-call | flops 1 | bytes 1 | tf_op jit(solution)/shard_map/pallas_call | solution.py:137
  23.4 0.6 %collective-permute-done.7.refs_0_ = bf16[776,128]{1,0:T(8,128)(2,1)S(1)} collective-permute-done((bf16[776,128]{1,0:T(8,128)(2,1)S(1)}, bf16[776,128]{1,0:T(8,128)(2,1)S(1)}, u32[]{:S(2)}, u32[]{:S(2)}) %collective-permute-start.7) | collective-permute-done | bytes 198688 | tf_op jit(solution)/shard_map/ppermute | solution.py:208
  24.0 1.9 %collective-permute-done.6.refs_1_ = bf16[776,128]{1,0:T(8,128)(2,1)S(1)} collective-permute-done((bf16[776,128]{1,0:T(8,128)(2,1)S(1)}, bf16[776,128]{1,0:T(8,128)(2,1)S(1)}, u32[]{:S(2)}, u32[]{:S(2)}) %collective-permute-start.6) | collective-permute-done | bytes 198688 | tf_op jit(solution)/shard_map/ppermute | solution.py:208
  25.9 0.2 collective-permute-start.13
  26.3 1.8 %collective-permute-start.12 = (bf16[776,128]{1,0:T(8,128)(2,1)S(1)}, bf16[776,128]{1,0:T(8,128)(2,1)S(1)}, u32[]{:S(2)}, u32[]{:S(2)}) collective-permute-start(bf16[776,128]{1,0:T(8,128)(2,1)S(1)} %collective-permute-done.7.refs_0_), channel_id=1, source_target_pairs={{0,2},{2,4},{4,6},{6,7},{7,5},{5,3},{3,1},{1,0},{8,10},{10,12},{12... | collective-permute-start | bytes 595976 | tf_op jit(solution)/shard_map/ppermute | solution.py:208
  28.1 1.4 %shard_map.104 = f32[128,512]{1,0:T(8,128)S(1)} custom-call(s32[48]{0:T(128)S(1)} %maximum_convert_fusion.4.ids_ref, bf16[776,128]{1,0:T(8,128)(2,1)S(1)} %collective-permute-done.7.refs_0_, bf16[776,128]{1,0:T(8,128)(2,1)S(1)} %collective-permute-done.6.refs_1_, bf16[1536,512]{1,0:T(8,128)(2,1)S(1)} %copy-done, bf16[512,512]{1,0:T(8,128)(2,1)S(1)} %copy-done.1), custom_call_target="tpu_custom_call" | custom-call | flops 1 | bytes 1 | tf_op jit(solution)/shard_map/pallas_call | solution.py:137
  29.5 0.7 %collective-permute-done.10.refs_1_ = bf16[776,128]{1,0:T(8,128)(2,1)S(1)} collective-permute-done((bf16[776,128]{1,0:T(8,128)(2,1)S(1)}, bf16[776,128]{1,0:T(8,128)(2,1)S(1)}, u32[]{:S(2)}, u32[]{:S(2)}) %collective-permute-start.10) | collective-permute-done | bytes 198688 | tf_op jit(solution)/shard_map/ppermute | solution.py:208
  30.5 1.8 %collective-permute-start.9 = (bf16[776,128]{1,0:T(8,128)(2,1)S(1)}, bf16[776,128]{1,0:T(8,128)(2,1)S(1)}, u32[]{:S(2)}, u32[]{:S(2)}) collective-permute-start(bf16[776,128]{1,0:T(8,128)(2,1)S(1)} %collective-permute-done.5.refs_0_), channel_id=1, source_target_pairs={{0,2},{2,4},{4,6},{6,7},{7,5},{5,3},{3,1},{1,0},{8,10},{10,12},{12... | collective-permute-start | bytes 595976 | tf_op jit(solution)/shard_map/ppermute | solution.py:208
  32.3 1.4 %shard_map.105 = f32[128,512]{1,0:T(8,128)S(1)} custom-call(s32[48]{0:T(128)S(1)} %maximum_convert_fusion.6.ids_ref, bf16[776,128]{1,0:T(8,128)(2,1)S(1)} %collective-permute-done.5.refs_0_, bf16[776,128]{1,0:T(8,128)(2,1)S(1)} %collective-permute-done.10.refs_1_, bf16[1536,512]{1,0:T(8,128)(2,1)S(1)} %copy-done, bf16[512,512]{1,0:T(8,128)(2,1)S(1)} %copy-done.1), custom_call_target="tpu_custom_call" | custom-call | flops 1 | bytes 1 | tf_op jit(solution)/shard_map/pallas_call | solution.py:137
  33.9 0.5 %collective-permute-done.13.refs_1_ = bf16[776,128]{1,0:T(8,128)(2,1)S(1)} collective-permute-done((bf16[776,128]{1,0:T(8,128)(2,1)S(1)}, bf16[776,128]{1,0:T(8,128)(2,1)S(1)}, u32[]{:S(2)}, u32[]{:S(2)}) %collective-permute-start.13) | collective-permute-done | bytes 198688 | tf_op jit(solution)/shard_map/ppermute | solution.py:208
  34.6 1.5 %shard_map.106 = (f32[128,512]{1,0:T(8,128)S(1)}, f32[128,512]{1,0:T(8,128)S(1)}, f32[128,512]{1,0:T(8,128)S(1)}) custom-call(s32[48]{0:T(128)S(1)} %maximum_convert_fusion.7.ids_ref, s32[16]{0:T(128)S(1)} %copy-done.2, bf16[776,128]{1,0:T(8,128)(2,1)S(1)} %collective-permute-done.12.refs_0_, bf16[776,128]{1,0:T(8,128)(2,1)S(1)} %collective-permute-done.13.refs_1_, ...), custom_call_target="tpu_custom_call" | custom-call | flops 1 | bytes 1 | tf_op jit(solution)/shard_map/pallas_call | solution.py:137
  36.2 1.3 %collective-permute-done.11.refs_1_ = bf16[776,128]{1,0:T(8,128)(2,1)S(1)} collective-permute-done((bf16[776,128]{1,0:T(8,128)(2,1)S(1)}, bf16[776,128]{1,0:T(8,128)(2,1)S(1)}, u32[]{:S(2)}, u32[]{:S(2)}) %collective-permute-start.11) | collective-permute-done | bytes 198688 | tf_op jit(solution)/shard_map/ppermute | solution.py:208
  37.6 1.6 %shard_map.107 = (f32[128,512]{1,0:T(8,128)S(1)}, f32[128,512]{1,0:T(8,128)S(1)}, f32[128,512]{1,0:T(8,128)S(1)}) custom-call(s32[48]{0:T(128)S(1)} %maximum_convert_fusion.5.ids_ref, s32[16]{0:T(128)S(1)} %copy-done.2, bf16[776,128]{1,0:T(8,128)(2,1)S(1)} %collective-permute-done.9.refs_0_, bf16[776,128]{1,0:T(8,128)(2,1)S(1)} %collective-permute-done.11.refs_1_, ...), custom_call_target="tpu_custom_call" | custom-call | flops 1 | bytes 1 | tf_op jit(solution)/shard_map/pallas_call | solution.py:137
  39.3 1.6 %collective-permute-start.18 = (f16[128,512]{1,0:T(8,128)(2,1)S(1)}, f16[128,512]{1,0:T(8,128)(2,1)S(1)}, u32[]{:S(2)}, u32[]{:S(2)}) collective-permute-start(f16[128,512]{1,0:T(8,128)(2,1)S(1)} %multiply_convert_fusion), channel_id=1, source_target_pairs={{0,16},{8,24},{16,0},{24,8},{1,17},{9,25},{17,1},{25,9},{2,18},{10... | collective-permute-start | bytes 393224 | tf_op jit(solution)/shard_map/ppermute | solution.py:237
  41.0 0.9 %shard_map.108 = (f32[256,512]{1,0:T(8,128)S(1)}, f32[256,512]{1,0:T(8,128)S(1)}, s32[256,512]{1,0:T(8,128)S(1)}) custom-call(s32[16]{0:T(128)S(1)} %copy-done.2, f32[768,512]{1,0:T(8,128)S(1)} %constant_dynamic-update-slice_fusion.refs_4_.refs_0_, f32[128,512]{1,0:T(8,128)S(1)} %get-tuple-element.125.refs_5_.refs_1_, f32[128,512]{1,0:T(8,128)S(1)} %get-tuple-element.126.refs_2_), custom_call_target="tpu_custom_call" | custom-call | flops 1 | bytes 1 | tf_op jit(solution)/shard_map/pallas_call | solution.py:137
  41.9 0.3 collective-permute-start.15
  42.2 1.4 %collective-permute-start.16 = (f16[128,512]{1,0:T(8,128)(2,1)S(1)}, f16[128,512]{1,0:T(8,128)(2,1)S(1)}, u32[]{:S(2)}, u32[]{:S(2)}) collective-permute-start(f16[128,512]{1,0:T(8,128)(2,1)S(1)} %multiply_convert_fusion.1), channel_id=1, source_target_pairs={{0,16},{8,24},{16,0},{24,8},{1,17},{9,25},{17,1},{25,9},{2,18},{10... | collective-permute-start | bytes 393224 | tf_op jit(solution)/shard_map/ppermute | solution.py:237
  43.6 1.8 %collective-permute-done.18 = f16[128,512]{1,0:T(8,128)(2,1)S(1)} collective-permute-done((f16[128,512]{1,0:T(8,128)(2,1)S(1)}, f16[128,512]{1,0:T(8,128)(2,1)S(1)}, u32[]{:S(2)}, u32[]{:S(2)}) %collective-permute-start.18) | collective-permute-done | bytes 131104 | tf_op jit(solution)/shard_map/ppermute | solution.py:237
  45.4 2.7 %collective-permute-done.16 = f16[128,512]{1,0:T(8,128)(2,1)S(1)} collective-permute-done((f16[128,512]{1,0:T(8,128)(2,1)S(1)}, f16[128,512]{1,0:T(8,128)(2,1)S(1)}, u32[]{:S(2)}, u32[]{:S(2)}) %collective-permute-start.16) | collective-permute-done | bytes 131104 | tf_op jit(solution)/shard_map/ppermute | solution.py:237
  48.1 1.1 %multiply_add_fusion = f32[256,512]{1,0:T(8,128)} fusion(f32[256,512]{1,0:T(8,128)S(1)} %copy-done.3, f32[256,512]{1,0:T(8,128)S(1)} %get-tuple-element.127, f32[256,512]{1,0:T(8,128)S(1)} %collective-permute-done.15, s32[256,512]{1,0:T(8,128)S(1)} %get-tuple-element.129, f16[64,512]{1,0:T(8,128)(2,1)S(1)} %get-tuple-element.138, ...), kind=kLoop, calls=%fused_computation | loop fusion | flops 1441792 | bytes 2883584 | tf_op jit(solution)/shard_map/add | solution.py:288
  (74 shorter events, 2.7 us)
Async XLA Ops:
  0.0 2.0 %copy-start.4 = (s32[2,18]{1,0:T(2,128)S(1)}, s32[2,18]{1,0:T(2,128)}, u32[]{:S(2)}) copy-start(s32[2,18]{1,0:T(2,128)} %param.11) | copy-start | bytes 436
  0.0 2.0 %copy-start.6 = (s32[2,1]{0,1:T(1,128)S(1)}, s32[2,1]{0,1:T(1,128)}, u32[]{:S(2)}) copy-start(s32[2,1]{0,1:T(1,128)} %param.12) | copy-start | bytes 28
  0.0 2.1 %copy-start.5 = (s32[2,6]{1,0:T(2,128)S(1)}, s32[2,6]{1,0:T(2,128)}, u32[]{:S(2)}) copy-start(s32[2,6]{1,0:T(2,128)} %param.14) | copy-start | bytes 148
  0.0 2.1 %copy-start.7 = (s32[2,1]{0,1:T(1,128)S(1)}, s32[2,1]{0,1:T(1,128)}, u32[]{:S(2)}) copy-start(s32[2,1]{0,1:T(1,128)} %param.15) | copy-start | bytes 28
  1.6 4.0 %copy-start = (bf16[1536,512]{1,0:T(8,128)(2,1)S(1)}, bf16[1536,512]{1,0:T(8,128)(2,1)}, u32[]{:S(2)}) copy-start(bf16[1536,512]{1,0:T(8,128)(2,1)} %refs_2_.15) | copy-start | bytes 4718596
  1.6 4.0 %copy-start.1 = (bf16[512,512]{1,0:T(8,128)(2,1)S(1)}, bf16[512,512]{1,0:T(8,128)(2,1)}, u32[]{:S(2)}) copy-start(bf16[512,512]{1,0:T(8,128)(2,1)} %refs_3_.15) | copy-start | bytes 1572868
  2.4 8.8 %collective-permute-start = (bf16[776,128]{1,0:T(8,128)(2,1)S(1)}, bf16[776,128]{1,0:T(8,128)(2,1)S(1)}, u32[]{:S(2)}, u32[]{:S(2)}) collective-permute-start(bf16[776,128]{1,0:T(8,128)(2,1)S(1)} %get-tuple-element.76.refs_0_), channel_id=1, source_target_pairs={{0,2},{2,4},{4,6},{6,7},{7,5},{5,3},{3,1},{1,0},{8,10},{10,12},{12... | collective-permute-start | bytes 595976 | tf_op jit(solution)/shard_map/ppermute | solution.py:208
  5.5 7.8 %collective-permute-start.4 = (bf16[776,128]{1,0:T(8,128)(2,1)S(1)}, bf16[776,128]{1,0:T(8,128)(2,1)S(1)}, u32[]{:S(2)}, u32[]{:S(2)}) collective-permute-start(bf16[776,128]{1,0:T(8,128)(2,1)S(1)} %get-tuple-element.77.refs_1_), channel_id=1, source_target_pairs={{2,0},{4,2},{6,4},{7,6},{5,7},{3,5},{1,3},{0,1},{10,8},{12,10},{14... | collective-permute-start | bytes 595976 | tf_op jit(solution)/shard_map/ppermute | solution.py:208
  7.0 8.5 %collective-permute-start.3 = (bf16[776,128]{1,0:T(8,128)(2,1)S(1)}, bf16[776,128]{1,0:T(8,128)(2,1)S(1)}, u32[]{:S(2)}, u32[]{:S(2)}) collective-permute-start(bf16[776,128]{1,0:T(8,128)(2,1)S(1)} %get-tuple-element.77.refs_1_), channel_id=1, source_target_pairs={{0,2},{2,4},{4,6},{6,7},{7,5},{5,3},{3,1},{1,0},{8,10},{10,12},{12... | collective-permute-start | bytes 595976 | tf_op jit(solution)/shard_map/ppermute | solution.py:208
  9.0 8.6 %collective-permute-start.2 = (bf16[776,128]{1,0:T(8,128)(2,1)S(1)}, bf16[776,128]{1,0:T(8,128)(2,1)S(1)}, u32[]{:S(2)}, u32[]{:S(2)}) collective-permute-start(bf16[776,128]{1,0:T(8,128)(2,1)S(1)} %get-tuple-element.76.refs_0_), channel_id=1, source_target_pairs={{2,0},{4,2},{6,4},{7,6},{5,7},{3,5},{1,3},{0,1},{10,8},{12,10},{14... | collective-permute-start | bytes 595976 | tf_op jit(solution)/shard_map/ppermute | solution.py:208
  11.2 8.5 %collective-permute-start.1 = (bf16[776,128]{1,0:T(8,128)(2,1)S(1)}, bf16[776,128]{1,0:T(8,128)(2,1)S(1)}, u32[]{:S(2)}, u32[]{:S(2)}) collective-permute-start(bf16[776,128]{1,0:T(8,128)(2,1)S(1)} %collective-permute-done.refs_0_), channel_id=1, source_target_pairs={{0,2},{2,4},{4,6},{6,7},{7,5},{5,3},{3,1},{1,0},{8,10},{10,12},{12... | collective-permute-start | bytes 595976 | tf_op jit(solution)/shard_map/ppermute | solution.py:208
  13.5 8.4 %collective-permute-start.8 = (bf16[776,128]{1,0:T(8,128)(2,1)S(1)}, bf16[776,128]{1,0:T(8,128)(2,1)S(1)}, u32[]{:S(2)}, u32[]{:S(2)}) collective-permute-start(bf16[776,128]{1,0:T(8,128)(2,1)S(1)} %collective-permute-done.4.refs_1_), channel_id=1, source_target_pairs={{2,0},{4,2},{6,4},{7,6},{5,7},{3,5},{1,3},{0,1},{10,8},{12,10},{14... | collective-permute-start | bytes 595976 | tf_op jit(solution)/shard_map/ppermute | solution.py:208
  15.5 8.5 %collective-permute-start.7 = (bf16[776,128]{1,0:T(8,128)(2,1)S(1)}, bf16[776,128]{1,0:T(8,128)(2,1)S(1)}, u32[]{:S(2)}, u32[]{:S(2)}) collective-permute-start(bf16[776,128]{1,0:T(8,128)(2,1)S(1)} %collective-permute-done.3.refs_0_), channel_id=1, source_target_pairs={{0,2},{2,4},{4,6},{6,7},{7,5},{5,3},{3,1},{1,0},{8,10},{10,12},{12... | collective-permute-start | bytes 595976 | tf_op jit(solution)/shard_map/ppermute | solution.py:208
  17.8 8.1 %collective-permute-start.6 = (bf16[776,128]{1,0:T(8,128)(2,1)S(1)}, bf16[776,128]{1,0:T(8,128)(2,1)S(1)}, u32[]{:S(2)}, u32[]{:S(2)}) collective-permute-start(bf16[776,128]{1,0:T(8,128)(2,1)S(1)} %collective-permute-done.2.refs_1_), channel_id=1, source_target_pairs={{2,0},{4,2},{6,4},{7,6},{5,7},{3,5},{1,3},{0,1},{10,8},{12,10},{14... | collective-permute-start | bytes 595976 | tf_op jit(solution)/shard_map/ppermute | solution.py:208
  19.7 9.7 %collective-permute-start.5 = (bf16[776,128]{1,0:T(8,128)(2,1)S(1)}, bf16[776,128]{1,0:T(8,128)(2,1)S(1)}, u32[]{:S(2)}, u32[]{:S(2)}) collective-permute-start(bf16[776,128]{1,0:T(8,128)(2,1)S(1)} %collective-permute-done.1.refs_0_), channel_id=1, source_target_pairs={{0,2},{2,4},{4,6},{6,7},{7,5},{5,3},{3,1},{1,0},{8,10},{10,12},{12... | collective-permute-start | bytes 595976 | tf_op jit(solution)/shard_map/ppermute | solution.py:208
  22.0 8.1 %collective-permute-start.10 = (bf16[776,128]{1,0:T(8,128)(2,1)S(1)}, bf16[776,128]{1,0:T(8,128)(2,1)S(1)}, u32[]{:S(2)}, u32[]{:S(2)}) collective-permute-start(bf16[776,128]{1,0:T(8,128)(2,1)S(1)} %collective-permute-done.8.refs_1_), channel_id=1, source_target_pairs={{2,0},{4,2},{6,4},{7,6},{5,7},{3,5},{1,3},{0,1},{10,8},{12,10},{14... | collective-permute-start | bytes 595976 | tf_op jit(solution)/shard_map/ppermute | solution.py:208
  25.9 8.5 %collective-permute-start.13 = (bf16[776,128]{1,0:T(8,128)(2,1)S(1)}, bf16[776,128]{1,0:T(8,128)(2,1)S(1)}, u32[]{:S(2)}, u32[]{:S(2)}) collective-permute-start(bf16[776,128]{1,0:T(8,128)(2,1)S(1)} %collective-permute-done.6.refs_1_), channel_id=1, source_target_pairs={{2,0},{4,2},{6,4},{7,6},{5,7},{3,5},{1,3},{0,1},{10,8},{12,10},{14... | collective-permute-start | bytes 595976 | tf_op jit(solution)/shard_map/ppermute | solution.py:208
  26.3 8.1 %collective-permute-start.12 = (bf16[776,128]{1,0:T(8,128)(2,1)S(1)}, bf16[776,128]{1,0:T(8,128)(2,1)S(1)}, u32[]{:S(2)}, u32[]{:S(2)}) collective-permute-start(bf16[776,128]{1,0:T(8,128)(2,1)S(1)} %collective-permute-done.7.refs_0_), channel_id=1, source_target_pairs={{0,2},{2,4},{4,6},{6,7},{7,5},{5,3},{3,1},{1,0},{8,10},{10,12},{12... | collective-permute-start | bytes 595976 | tf_op jit(solution)/shard_map/ppermute | solution.py:208
  30.2 7.2 %collective-permute-start.11 = (bf16[776,128]{1,0:T(8,128)(2,1)S(1)}, bf16[776,128]{1,0:T(8,128)(2,1)S(1)}, u32[]{:S(2)}, u32[]{:S(2)}) collective-permute-start(bf16[776,128]{1,0:T(8,128)(2,1)S(1)} %collective-permute-done.10.refs_1_), channel_id=1, source_target_pairs={{2,0},{4,2},{6,4},{7,6},{5,7},{3,5},{1,3},{0,1},{10,8},{12,10},{14... | collective-permute-start | bytes 595976 | tf_op jit(solution)/shard_map/ppermute | solution.py:208
  30.5 7.0 %collective-permute-start.9 = (bf16[776,128]{1,0:T(8,128)(2,1)S(1)}, bf16[776,128]{1,0:T(8,128)(2,1)S(1)}, u32[]{:S(2)}, u32[]{:S(2)}) collective-permute-start(bf16[776,128]{1,0:T(8,128)(2,1)S(1)} %collective-permute-done.5.refs_0_), channel_id=1, source_target_pairs={{0,2},{2,4},{4,6},{6,7},{7,5},{5,3},{3,1},{1,0},{8,10},{10,12},{12... | collective-permute-start | bytes 595976 | tf_op jit(solution)/shard_map/ppermute | solution.py:208
  33.7 0.9 %copy-start.2 = (s32[16]{0:T(128)S(1)}, s32[16]{0:T(128)}, u32[]{:S(2)}) copy-start(s32[16]{0:T(128)} %owners_ref.5) | copy-start | bytes 196
  36.1 3.2 %collective-permute-start.17 = (f32[128,512]{1,0:T(8,128)S(1)}, f32[128,512]{1,0:T(8,128)S(1)}, u32[]{:S(2)}, u32[]{:S(2)}) collective-permute-start(f32[128,512]{1,0:T(8,128)S(1)} %get-tuple-element.132), channel_id=1, source_target_pairs={{0,8},{8,0},{16,24},{24,16},{1,9},{9,1},{17,25},{25,17},{2,10},{10... | collective-permute-start | bytes 786440 | tf_op jit(solution)/shard_map/ppermute | solution.py:232
  39.2 1.7 %collective-permute-start.14 = (f32[128,512]{1,0:T(8,128)S(1)}, f32[128,512]{1,0:T(8,128)S(1)}, u32[]{:S(2)}, u32[]{:S(2)}) collective-permute-start(f32[128,512]{1,0:T(8,128)S(1)} %get-tuple-element.122), channel_id=1, source_target_pairs={{0,8},{8,0},{16,24},{24,16},{1,9},{9,1},{17,25},{25,17},{2,10},{10... | collective-permute-start | bytes 786440 | tf_op jit(solution)/shard_map/ppermute | solution.py:232
  39.3 6.0 %collective-permute-start.18 = (f16[128,512]{1,0:T(8,128)(2,1)S(1)}, f16[128,512]{1,0:T(8,128)(2,1)S(1)}, u32[]{:S(2)}, u32[]{:S(2)}) collective-permute-start(f16[128,512]{1,0:T(8,128)(2,1)S(1)} %multiply_convert_fusion), channel_id=1, source_target_pairs={{0,16},{8,24},{16,0},{24,8},{1,17},{9,25},{17,1},{25,9},{2,18},{10... | collective-permute-start | bytes 393224 | tf_op jit(solution)/shard_map/ppermute | solution.py:237
  40.9 7.2 %copy-start.3 = (f32[256,512]{1,0:T(8,128)S(1)}, f32[256,512]{1,0:T(8,128)}, u32[]{:S(2)}) copy-start(f32[256,512]{1,0:T(8,128)} %param.19) | copy-start | bytes 1572868
  41.9 6.2 %collective-permute-start.15 = (f32[256,512]{1,0:T(8,128)S(1)}, f32[256,512]{1,0:T(8,128)S(1)}, u32[]{:S(2)}, u32[]{:S(2)}) collective-permute-start(f32[256,512]{1,0:T(8,128)S(1)} %get-tuple-element.128), channel_id=1, source_target_pairs={{0,8},{8,0},{16,24},{24,16},{1,9},{9,1},{17,25},{25,17},{2,10},{10... | collective-permute-start | bytes 1572872 | tf_op jit(solution)/shard_map/ppermute | solution.py:280
  42.2 5.9 %collective-permute-start.16 = (f16[128,512]{1,0:T(8,128)(2,1)S(1)}, f16[128,512]{1,0:T(8,128)(2,1)S(1)}, u32[]{:S(2)}, u32[]{:S(2)}) collective-permute-start(f16[128,512]{1,0:T(8,128)(2,1)S(1)} %multiply_convert_fusion.1), channel_id=1, source_target_pairs={{0,16},{8,24},{16,0},{24,8},{1,17},{9,25},{17,1},{25,9},{2,18},{10... | collective-permute-start | bytes 393224 | tf_op jit(solution)/shard_map/ppermute | solution.py:237

commit v7 on v6

--- a/solution.py
+++ b/solution.py
@@ -18,12 +18,20 @@
 SMEM = pl.BlockSpec(memory_space=pltpu.SMEM)
 
 
+def remainder(x, n):
+    return lax.rem(x, n) if n & (n - 1) else x & (n - 1)
+
+
+def quotient(x, n):
+    return lax.div(x, n) if n & (n - 1) else x >> (n.bit_length() - 1)
+
+
 def ring_order(n):
     return list(range(0, n, 2)) + list(range(n - 1, 0, -2))
 
 
 def ring_place(d, n):
-    return jnp.where(lax.rem(d, 2) == 0, lax.div(d, 2), n - 1 - lax.div(d, 2))
+    return jnp.where(remainder(d, 2) == 0, quotient(d, 2), n - 1 - quotient(d, 2))
 
 
 def rows_of(amps):
@@ -44,7 +52,7 @@
             left, right = [], []
             for s in range(q, min(q + 4, slots)):
                 mark = ids_ref[t * slots + s]
-                k = pl.multiple_of(lax.rem(mark, DEAD) * TS, TS)
+                k = pl.multiple_of(remainder(mark, DEAD) * TS, TS)
                 panel_ref = ladder_ref if s < ladder_slots else cycle_ref
                 right.append(panel_ref[pl.ds(k, TS), :])
                 tile = amp_ref[s * HALF : (s + 1) * HALF, :]
@@ -65,8 +73,8 @@
 
 
 def arrival(row_tile, place, tiles, n_dev):
-    t = lax.rem(row_tile, tiles)
-    back = lax.rem(place - ring_place(lax.div(row_tile, tiles), n_dev) + n_dev, n_dev)
+    t = remainder(row_tile, tiles)
+    back = remainder(place - ring_place(quotient(row_tile, tiles), n_dev) + n_dev, n_dev)
     half, cut = n_dev // 2, tiles // 2
     step = jnp.minimum(back, n_dev - back)
     there = jnp.where(back < half, jnp.where(t < cut, t, t + cut), jnp.where(t < cut, t + tiles + cut, t))
@@ -98,7 +106,7 @@
 
 
 def partner(group):
-    return group + 1 - 2 * lax.rem(group, 2)
+    return group + 1 - 2 * remainder(group, 2)
 
 
 def tile_kernel(n, ladder_slots, slots, ids_ref, *refs):
@@ -113,7 +121,7 @@
     new_ref, *out_refs, rows_ref = refs[n + 2 + n_parts :]
     multiply(ids_ref, amp_refs, ladder_ref, cycle_ref, ladder_slots, slots, rows_ref, new_ref)
     for k, shift in enumerate(range(2, n_grp, 2)):
-        group = lax.rem(lax.axis_index("grp") + shift, n_grp)
+        group = remainder(lax.axis_index("grp") + shift, n_grp)
         for owner, out_ref in zip((group, partner(group)), out_refs[2 * k :]):
             found = slots_of(owner, owned, tiles, n_dev, owners_ref)
             for at, wanted in enumerate(ranks):
@@ -169,9 +177,10 @@
     own, ladder_ids, ladder_count, cycle_ids, cycle_count = lax.optimization_barrier(
         (own, ladder_ids, ladder_count, cycle_ids, cycle_count)
     )
-    marks = jnp.concatenate(
-        [marked(ladder_ids, ladder_count), marked(cycle_ids, cycle_count)], axis=1
-    )
+    slot = jnp.arange(slots, dtype=jnp.int32)[None, :]
+    ids = jnp.concatenate([ladder_ids, cycle_ids], axis=1)
+    live = jnp.where(slot < ladder_slots, slot < ladder_count, slot - ladder_slots < cycle_count)
+    marks = jnp.where(live, ids, ids + DEAD)
     marks = jnp.concatenate([marks[t : t + 1] for t in range(tiles)], axis=1)
     note = jnp.pad(marks.astype(jnp.bfloat16), ((0, 7), (0, 2 * TS - marks.size)))
     own = [jnp.concatenate([own[t], note], axis=0) for t in range(tiles)]

time: 49.4 us -> 49.2 us (level)
  no operation moved by 1% of the time
where the time goes in v7:
time: 49.2 us; the launch traced here: 49.1 us
  starting transfers between devices  18.9 us (38%)
  waiting for transfers between devices  12.9 us (26%)
  Pallas kernels  12.2 us (25%)
  other arithmetic  3.59 us (7%)
  local copies, waits for them, and re-layouts  1.17 us (2%)
    ppermute x14, starting transfers between devices, hop(): lax.ppermute(piece, 'dev', forward if ahead else backward)  15.6 us
    pallas_call x9, Pallas kernels, call(): pl.pallas_call(kernel, out_shape=out_shape, in_specs=[SMEM] * n_smem + [V...  12.2 us
    ppermute x14, waiting for transfers between devices, hop(): lax.ppermute(piece, 'dev', forward if ahead else backward)  8.35 us
    ppermute x2, waiting for transfers between devices, sent(): lax.ppermute((rows * SCALE).astype(jnp.float16), 'grp', [(g, (g + shift)...  4.53 us
    ppermute x2, starting transfers between devices, sent(): lax.ppermute((rows * SCALE).astype(jnp.float16), 'grp', [(g, (g + shift)...  2.95 us
    concatenate x1, other arithmetic, per_device(): own = rows_of(jnp.concatenate([ladder_amps, cycle_amps], axis=1))  1.56 us
    add x1, other arithmetic, per_device(): total = total + chosen.reshape(base.shape)  1.08 us
  transfers between devices with their start and end apart: 19, of which 10 were waited for; matrix products, arithmetic and copies ran while one was open for 3% of the time, Pallas kernels for 25%

profile of v7, /device:TPU:0, one launch (start us, length us, event | category | flops | bytes accessed | tf_op | source)
XLA Modules:
  0.0 49.1 jit_solution(12041063768729670557)
XLA Ops:
  0.0 1.6 %pad_maximum_fusion = bf16[2,24,4096]{2,0,1:T(2,128)(2,1)S(1)} fusion(bf16[2,6,4096]{2,0,1:T(2,128)(2,1)} %param.13, bf16[2,18,4096]{2,0,1:T(2,128)(2,1)} %param.10), kind=kLoop, calls=%fused_computation.4 | loop fusion | flops 196608 | bytes 786432 | tf_op jit(solution)/shard_map/concatenate | solution.py:176
  2.3 3.1 %collective-permute-start = (bf16[776,128]{1,0:T(8,128)(2,1)S(1)}, bf16[776,128]{1,0:T(8,128)(2,1)S(1)}, u32[]{:S(2)}, u32[]{:S(2)}) collective-permute-start(bf16[776,128]{1,0:T(8,128)(2,1)S(1)} %get-tuple-element.76.refs_0_), channel_id=1, source_target_pairs={{0,2},{2,4},{4,6},{6,7},{7,5},{5,3},{3,1},{1,0},{8,10},{10,12},{12... | collective-permute-start | bytes 595976 | tf_op jit(solution)/shard_map/ppermute | solution.py:217
  5.5 1.4 %shard_map.100 = f32[128,512]{1,0:T(8,128)S(1)} custom-call(s32[48]{0:T(128)S(1)} %maximum_convert_fusion.ids_ref, bf16[776,128]{1,0:T(8,128)(2,1)S(1)} %get-tuple-element.76.refs_0_, bf16[776,128]{1,0:T(8,128)(2,1)S(1)} %get-tuple-element.77.refs_1_, bf16[1536,512]{1,0:T(8,128)(2,1)S(1)} %copy-done, bf16[512,512]{1,0:T(8,128)(2,1)S(1)} %copy-done.1), custom_call_target="tpu_custom_call" | custom-call | flops 1 | bytes 1 | tf_op jit(solution)/shard_map/pallas_call | solution.py:145
  6.9 2.1 %collective-permute-start.3 = (bf16[776,128]{1,0:T(8,128)(2,1)S(1)}, bf16[776,128]{1,0:T(8,128)(2,1)S(1)}, u32[]{:S(2)}, u32[]{:S(2)}) collective-permute-start(bf16[776,128]{1,0:T(8,128)(2,1)S(1)} %get-tuple-element.77.refs_1_), channel_id=1, source_target_pairs={{0,2},{2,4},{4,6},{6,7},{7,5},{5,3},{3,1},{1,0},{8,10},{10,12},{12... | collective-permute-start | bytes 595976 | tf_op jit(solution)/shard_map/ppermute | solution.py:217
  8.9 2.2 %collective-permute-done.refs_0_ = bf16[776,128]{1,0:T(8,128)(2,1)S(1)} collective-permute-done((bf16[776,128]{1,0:T(8,128)(2,1)S(1)}, bf16[776,128]{1,0:T(8,128)(2,1)S(1)}, u32[]{:S(2)}, u32[]{:S(2)}) %collective-permute-start) | collective-permute-done | bytes 198688 | tf_op jit(solution)/shard_map/ppermute | solution.py:217
  11.1 2.1 %collective-permute-start.1 = (bf16[776,128]{1,0:T(8,128)(2,1)S(1)}, bf16[776,128]{1,0:T(8,128)(2,1)S(1)}, u32[]{:S(2)}, u32[]{:S(2)}) collective-permute-start(bf16[776,128]{1,0:T(8,128)(2,1)S(1)} %collective-permute-done.refs_0_), channel_id=1, source_target_pairs={{0,2},{2,4},{4,6},{6,7},{7,5},{5,3},{3,1},{1,0},{8,10},{10,12},{12... | collective-permute-start | bytes 595976 | tf_op jit(solution)/shard_map/ppermute | solution.py:217
  13.4 1.4 %shard_map.101 = f32[128,512]{1,0:T(8,128)S(1)} custom-call(s32[48]{0:T(128)S(1)} %maximum_convert_fusion.1.ids_ref, bf16[776,128]{1,0:T(8,128)(2,1)S(1)} %collective-permute-done.refs_0_, bf16[776,128]{1,0:T(8,128)(2,1)S(1)} %collective-permute-done.4.refs_1_, bf16[1536,512]{1,0:T(8,128)(2,1)S(1)} %copy-done, bf16[512,512]{1,0:T(8,128)(2,1)S(1)} %copy-done.1), custom_call_target="tpu_custom_call" | custom-call | flops 1 | bytes 1 | tf_op jit(solution)/shard_map/pallas_call | solution.py:145
  14.8 0.6 %collective-permute-done.3.refs_0_ = bf16[776,128]{1,0:T(8,128)(2,1)S(1)} collective-permute-done((bf16[776,128]{1,0:T(8,128)(2,1)S(1)}, bf16[776,128]{1,0:T(8,128)(2,1)S(1)}, u32[]{:S(2)}, u32[]{:S(2)}) %collective-permute-start.3) | collective-permute-done | bytes 198688 | tf_op jit(solution)/shard_map/ppermute | solution.py:217
  15.4 2.1 %collective-permute-start.7 = (bf16[776,128]{1,0:T(8,128)(2,1)S(1)}, bf16[776,128]{1,0:T(8,128)(2,1)S(1)}, u32[]{:S(2)}, u32[]{:S(2)}) collective-permute-start(bf16[776,128]{1,0:T(8,128)(2,1)S(1)} %collective-permute-done.3.refs_0_), channel_id=1, source_target_pairs={{0,2},{2,4},{4,6},{6,7},{7,5},{5,3},{3,1},{1,0},{8,10},{10,12},{12... | collective-permute-start | bytes 595976 | tf_op jit(solution)/shard_map/ppermute | solution.py:217
  17.6 1.4 %shard_map.102 = f32[128,512]{1,0:T(8,128)S(1)} custom-call(s32[48]{0:T(128)S(1)} %maximum_convert_fusion.2.ids_ref, bf16[776,128]{1,0:T(8,128)(2,1)S(1)} %collective-permute-done.3.refs_0_, bf16[776,128]{1,0:T(8,128)(2,1)S(1)} %collective-permute-done.2.refs_1_, bf16[1536,512]{1,0:T(8,128)(2,1)S(1)} %copy-done, bf16[512,512]{1,0:T(8,128)(2,1)S(1)} %copy-done.1), custom_call_target="tpu_custom_call" | custom-call | flops 1 | bytes 1 | tf_op jit(solution)/shard_map/pallas_call | solution.py:145
  19.0 0.6 %collective-permute-done.1.refs_0_ = bf16[776,128]{1,0:T(8,128)(2,1)S(1)} collective-permute-done((bf16[776,128]{1,0:T(8,128)(2,1)S(1)}, bf16[776,128]{1,0:T(8,128)(2,1)S(1)}, u32[]{:S(2)}, u32[]{:S(2)}) %collective-permute-start.1) | collective-permute-done | bytes 198688 | tf_op jit(solution)/shard_map/ppermute | solution.py:217
  19.6 2.1 %collective-permute-start.5 = (bf16[776,128]{1,0:T(8,128)(2,1)S(1)}, bf16[776,128]{1,0:T(8,128)(2,1)S(1)}, u32[]{:S(2)}, u32[]{:S(2)}) collective-permute-start(bf16[776,128]{1,0:T(8,128)(2,1)S(1)} %collective-permute-done.1.refs_0_), channel_id=1, source_target_pairs={{0,2},{2,4},{4,6},{6,7},{7,5},{5,3},{3,1},{1,0},{8,10},{10,12},{12... | collective-permute-start | bytes 595976 | tf_op jit(solution)/shard_map/ppermute | solution.py:217
  21.9 1.4 %shard_map.103 = f32[128,512]{1,0:T(8,128)S(1)} custom-call(s32[48]{0:T(128)S(1)} %maximum_convert_fusion.3.ids_ref, bf16[776,128]{1,0:T(8,128)(2,1)S(1)} %collective-permute-done.1.refs_0_, bf16[776,128]{1,0:T(8,128)(2,1)S(1)} %collective-permute-done.8.refs_1_, bf16[1536,512]{1,0:T(8,128)(2,1)S(1)} %copy-done, bf16[512,512]{1,0:T(8,128)(2,1)S(1)} %copy-done.1), custom_call_target="tpu_custom_call" | custom-call | flops 1 | bytes 1 | tf_op jit(solution)/shard_map/pallas_call | solution.py:145
  23.3 0.6 %collective-permute-done.7.refs_0_ = bf16[776,128]{1,0:T(8,128)(2,1)S(1)} collective-permute-done((bf16[776,128]{1,0:T(8,128)(2,1)S(1)}, bf16[776,128]{1,0:T(8,128)(2,1)S(1)}, u32[]{:S(2)}, u32[]{:S(2)}) %collective-permute-start.7) | collective-permute-done | bytes 198688 | tf_op jit(solution)/shard_map/ppermute | solution.py:217
  23.9 1.9 %collective-permute-done.6.refs_1_ = bf16[776,128]{1,0:T(8,128)(2,1)S(1)} collective-permute-done((bf16[776,128]{1,0:T(8,128)(2,1)S(1)}, bf16[776,128]{1,0:T(8,128)(2,1)S(1)}, u32[]{:S(2)}, u32[]{:S(2)}) %collective-permute-start.6) | collective-permute-done | bytes 198688 | tf_op jit(solution)/shard_map/ppermute | solution.py:217
  25.8 0.2 collective-permute-start.13
  26.2 1.8 %collective-permute-start.12 = (bf16[776,128]{1,0:T(8,128)(2,1)S(1)}, bf16[776,128]{1,0:T(8,128)(2,1)S(1)}, u32[]{:S(2)}, u32[]{:S(2)}) collective-permute-start(bf16[776,128]{1,0:T(8,128)(2,1)S(1)} %collective-permute-done.7.refs_0_), channel_id=1, source_target_pairs={{0,2},{2,4},{4,6},{6,7},{7,5},{5,3},{3,1},{1,0},{8,10},{10,12},{12... | collective-permute-start | bytes 595976 | tf_op jit(solution)/shard_map/ppermute | solution.py:217
  28.0 1.4 %shard_map.104 = f32[128,512]{1,0:T(8,128)S(1)} custom-call(s32[48]{0:T(128)S(1)} %maximum_convert_fusion.4.ids_ref, bf16[776,128]{1,0:T(8,128)(2,1)S(1)} %collective-permute-done.7.refs_0_, bf16[776,128]{1,0:T(8,128)(2,1)S(1)} %collective-permute-done.6.refs_1_, bf16[1536,512]{1,0:T(8,128)(2,1)S(1)} %copy-done, bf16[512,512]{1,0:T(8,128)(2,1)S(1)} %copy-done.1), custom_call_target="tpu_custom_call" | custom-call | flops 1 | bytes 1 | tf_op jit(solution)/shard_map/pallas_call | solution.py:145
  29.3 0.7 %collective-permute-done.10.refs_1_ = bf16[776,128]{1,0:T(8,128)(2,1)S(1)} collective-permute-done((bf16[776,128]{1,0:T(8,128)(2,1)S(1)}, bf16[776,128]{1,0:T(8,128)(2,1)S(1)}, u32[]{:S(2)}, u32[]{:S(2)}) %collective-permute-start.10) | collective-permute-done | bytes 198688 | tf_op jit(solution)/shard_map/ppermute | solution.py:217
  30.4 1.8 %collective-permute-start.9 = (bf16[776,128]{1,0:T(8,128)(2,1)S(1)}, bf16[776,128]{1,0:T(8,128)(2,1)S(1)}, u32[]{:S(2)}, u32[]{:S(2)}) collective-permute-start(bf16[776,128]{1,0:T(8,128)(2,1)S(1)} %collective-permute-done.5.refs_0_), channel_id=1, source_target_pairs={{0,2},{2,4},{4,6},{6,7},{7,5},{5,3},{3,1},{1,0},{8,10},{10,12},{12... | collective-permute-start | bytes 595976 | tf_op jit(solution)/shard_map/ppermute | solution.py:217
  32.2 1.4 %shard_map.105 = f32[128,512]{1,0:T(8,128)S(1)} custom-call(s32[48]{0:T(128)S(1)} %maximum_convert_fusion.6.ids_ref, bf16[776,128]{1,0:T(8,128)(2,1)S(1)} %collective-permute-done.5.refs_0_, bf16[776,128]{1,0:T(8,128)(2,1)S(1)} %collective-permute-done.10.refs_1_, bf16[1536,512]{1,0:T(8,128)(2,1)S(1)} %copy-done, bf16[512,512]{1,0:T(8,128)(2,1)S(1)} %copy-done.1), custom_call_target="tpu_custom_call" | custom-call | flops 1 | bytes 1 | tf_op jit(solution)/shard_map/pallas_call | solution.py:145
  33.8 0.5 %collective-permute-done.13.refs_1_ = bf16[776,128]{1,0:T(8,128)(2,1)S(1)} collective-permute-done((bf16[776,128]{1,0:T(8,128)(2,1)S(1)}, bf16[776,128]{1,0:T(8,128)(2,1)S(1)}, u32[]{:S(2)}, u32[]{:S(2)}) %collective-permute-start.13) | collective-permute-done | bytes 198688 | tf_op jit(solution)/shard_map/ppermute | solution.py:217
  34.4 1.5 %shard_map.106 = (f32[128,512]{1,0:T(8,128)S(1)}, f32[128,512]{1,0:T(8,128)S(1)}, f32[128,512]{1,0:T(8,128)S(1)}) custom-call(s32[48]{0:T(128)S(1)} %maximum_convert_fusion.7.ids_ref, s32[16]{0:T(128)S(1)} %copy-done.2, bf16[776,128]{1,0:T(8,128)(2,1)S(1)} %collective-permute-done.12.refs_0_, bf16[776,128]{1,0:T(8,128)(2,1)S(1)} %collective-permute-done.13.refs_1_, ...), custom_call_target="tpu_custom_call" | custom-call | flops 1 | bytes 1 | tf_op jit(solution)/shard_map/pallas_call | solution.py:145
  36.0 1.3 %collective-permute-done.11.refs_1_ = bf16[776,128]{1,0:T(8,128)(2,1)S(1)} collective-permute-done((bf16[776,128]{1,0:T(8,128)(2,1)S(1)}, bf16[776,128]{1,0:T(8,128)(2,1)S(1)}, u32[]{:S(2)}, u32[]{:S(2)}) %collective-permute-start.11) | collective-permute-done | bytes 198688 | tf_op jit(solution)/shard_map/ppermute | solution.py:217
  37.5 1.5 %shard_map.107 = (f32[128,512]{1,0:T(8,128)S(1)}, f32[128,512]{1,0:T(8,128)S(1)}, f32[128,512]{1,0:T(8,128)S(1)}) custom-call(s32[48]{0:T(128)S(1)} %maximum_convert_fusion.5.ids_ref, s32[16]{0:T(128)S(1)} %copy-done.2, bf16[776,128]{1,0:T(8,128)(2,1)S(1)} %collective-permute-done.9.refs_0_, bf16[776,128]{1,0:T(8,128)(2,1)S(1)} %collective-permute-done.11.refs_1_, ...), custom_call_target="tpu_custom_call" | custom-call | flops 1 | bytes 1 | tf_op jit(solution)/shard_map/pallas_call | solution.py:145
  39.2 1.6 %collective-permute-start.18 = (f16[128,512]{1,0:T(8,128)(2,1)S(1)}, f16[128,512]{1,0:T(8,128)(2,1)S(1)}, u32[]{:S(2)}, u32[]{:S(2)}) collective-permute-start(f16[128,512]{1,0:T(8,128)(2,1)S(1)} %multiply_convert_fusion), channel_id=1, source_target_pairs={{0,16},{8,24},{16,0},{24,8},{1,17},{9,25},{17,1},{25,9},{2,18},{10... | collective-permute-start | bytes 393224 | tf_op jit(solution)/shard_map/ppermute | solution.py:246
  40.8 0.9 %shard_map.108 = (f32[256,512]{1,0:T(8,128)S(1)}, f32[256,512]{1,0:T(8,128)S(1)}, s32[256,512]{1,0:T(8,128)S(1)}) custom-call(s32[16]{0:T(128)S(1)} %copy-done.2, f32[768,512]{1,0:T(8,128)S(1)} %constant_dynamic-update-slice_fusion.refs_4_.refs_0_, f32[128,512]{1,0:T(8,128)S(1)} %get-tuple-element.125.refs_5_.refs_1_, f32[128,512]{1,0:T(8,128)S(1)} %get-tuple-element.126.refs_2_), custom_call_target="tpu_custom_call" | custom-call | flops 1 | bytes 1 | tf_op jit(solution)/shard_map/pallas_call | solution.py:145
  41.7 0.3 collective-permute-start.15
  42.0 1.4 %collective-permute-start.16 = (f16[128,512]{1,0:T(8,128)(2,1)S(1)}, f16[128,512]{1,0:T(8,128)(2,1)S(1)}, u32[]{:S(2)}, u32[]{:S(2)}) collective-permute-start(f16[128,512]{1,0:T(8,128)(2,1)S(1)} %multiply_convert_fusion.1), channel_id=1, source_target_pairs={{0,16},{8,24},{16,0},{24,8},{1,17},{9,25},{17,1},{25,9},{2,18},{10... | collective-permute-start | bytes 393224 | tf_op jit(solution)/shard_map/ppermute | solution.py:246
  43.4 1.9 %collective-permute-done.18 = f16[128,512]{1,0:T(8,128)(2,1)S(1)} collective-permute-done((f16[128,512]{1,0:T(8,128)(2,1)S(1)}, f16[128,512]{1,0:T(8,128)(2,1)S(1)}, u32[]{:S(2)}, u32[]{:S(2)}) %collective-permute-start.18) | collective-permute-done | bytes 131104 | tf_op jit(solution)/shard_map/ppermute | solution.py:246
  45.3 2.7 %collective-permute-done.16 = f16[128,512]{1,0:T(8,128)(2,1)S(1)} collective-permute-done((f16[128,512]{1,0:T(8,128)(2,1)S(1)}, f16[128,512]{1,0:T(8,128)(2,1)S(1)}, u32[]{:S(2)}, u32[]{:S(2)}) %collective-permute-start.16) | collective-permute-done | bytes 131104 | tf_op jit(solution)/shard_map/ppermute | solution.py:246
  48.0 1.1 %multiply_add_fusion = f32[256,512]{1,0:T(8,128)} fusion(f32[256,512]{1,0:T(8,128)S(1)} %copy-done.3, f32[256,512]{1,0:T(8,128)S(1)} %get-tuple-element.127, f32[256,512]{1,0:T(8,128)S(1)} %collective-permute-done.15, s32[256,512]{1,0:T(8,128)S(1)} %get-tuple-element.129, f16[64,512]{1,0:T(8,128)(2,1)S(1)} %get-tuple-element.138, ...), kind=kLoop, calls=%fused_computation | loop fusion | flops 1441792 | bytes 2883584 | tf_op jit(solution)/shard_map/add | solution.py:297
  (74 shorter events, 2.5 us)
Async XLA Ops:
  0.0 2.0 %copy-start.5 = (s32[2,18]{1,0:T(2,128)S(1)}, s32[2,18]{1,0:T(2,128)}, u32[]{:S(2)}) copy-start(s32[2,18]{1,0:T(2,128)} %param.11) | copy-start | bytes 436
  0.0 2.0 %copy-start.6 = (s32[2,1]{0,1:T(1,128)S(1)}, s32[2,1]{0,1:T(1,128)}, u32[]{:S(2)}) copy-start(s32[2,1]{0,1:T(1,128)} %param.12) | copy-start | bytes 28
  0.0 2.0 %copy-start.4 = (s32[2,6]{1,0:T(2,128)S(1)}, s32[2,6]{1,0:T(2,128)}, u32[]{:S(2)}) copy-start(s32[2,6]{1,0:T(2,128)} %param.14) | copy-start | bytes 148
  0.0 2.1 %copy-start.7 = (s32[2,1]{0,1:T(1,128)S(1)}, s32[2,1]{0,1:T(1,128)}, u32[]{:S(2)}) copy-start(s32[2,1]{0,1:T(1,128)} %param.15) | copy-start | bytes 28
  1.6 3.9 %copy-start = (bf16[1536,512]{1,0:T(8,128)(2,1)S(1)}, bf16[1536,512]{1,0:T(8,128)(2,1)}, u32[]{:S(2)}) copy-start(bf16[1536,512]{1,0:T(8,128)(2,1)} %refs_2_.15) | copy-start | bytes 4718596
  1.6 3.9 %copy-start.1 = (bf16[512,512]{1,0:T(8,128)(2,1)S(1)}, bf16[512,512]{1,0:T(8,128)(2,1)}, u32[]{:S(2)}) copy-start(bf16[512,512]{1,0:T(8,128)(2,1)} %refs_3_.15) | copy-start | bytes 1572868
  2.3 8.8 %collective-permute-start = (bf16[776,128]{1,0:T(8,128)(2,1)S(1)}, bf16[776,128]{1,0:T(8,128)(2,1)S(1)}, u32[]{:S(2)}, u32[]{:S(2)}) collective-permute-start(bf16[776,128]{1,0:T(8,128)(2,1)S(1)} %get-tuple-element.76.refs_0_), channel_id=1, source_target_pairs={{0,2},{2,4},{4,6},{6,7},{7,5},{5,3},{3,1},{1,0},{8,10},{10,12},{12... | collective-permute-start | bytes 595976 | tf_op jit(solution)/shard_map/ppermute | solution.py:217
  5.4 7.8 %collective-permute-start.4 = (bf16[776,128]{1,0:T(8,128)(2,1)S(1)}, bf16[776,128]{1,0:T(8,128)(2,1)S(1)}, u32[]{:S(2)}, u32[]{:S(2)}) collective-permute-start(bf16[776,128]{1,0:T(8,128)(2,1)S(1)} %get-tuple-element.77.refs_1_), channel_id=1, source_target_pairs={{2,0},{4,2},{6,4},{7,6},{5,7},{3,5},{1,3},{0,1},{10,8},{12,10},{14... | collective-permute-start | bytes 595976 | tf_op jit(solution)/shard_map/ppermute | solution.py:217
  6.9 8.5 %collective-permute-start.3 = (bf16[776,128]{1,0:T(8,128)(2,1)S(1)}, bf16[776,128]{1,0:T(8,128)(2,1)S(1)}, u32[]{:S(2)}, u32[]{:S(2)}) collective-permute-start(bf16[776,128]{1,0:T(8,128)(2,1)S(1)} %get-tuple-element.77.refs_1_), channel_id=1, source_target_pairs={{0,2},{2,4},{4,6},{6,7},{7,5},{5,3},{3,1},{1,0},{8,10},{10,12},{12... | collective-permute-start | bytes 595976 | tf_op jit(solution)/shard_map/ppermute | solution.py:217
  8.9 8.6 %collective-permute-start.2 = (bf16[776,128]{1,0:T(8,128)(2,1)S(1)}, bf16[776,128]{1,0:T(8,128)(2,1)S(1)}, u32[]{:S(2)}, u32[]{:S(2)}) collective-permute-start(bf16[776,128]{1,0:T(8,128)(2,1)S(1)} %get-tuple-element.76.refs_0_), channel_id=1, source_target_pairs={{2,0},{4,2},{6,4},{7,6},{5,7},{3,5},{1,3},{0,1},{10,8},{12,10},{14... | collective-permute-start | bytes 595976 | tf_op jit(solution)/shard_map/ppermute | solution.py:217
  11.1 8.5 %collective-permute-start.1 = (bf16[776,128]{1,0:T(8,128)(2,1)S(1)}, bf16[776,128]{1,0:T(8,128)(2,1)S(1)}, u32[]{:S(2)}, u32[]{:S(2)}) collective-permute-start(bf16[776,128]{1,0:T(8,128)(2,1)S(1)} %collective-permute-done.refs_0_), channel_id=1, source_target_pairs={{0,2},{2,4},{4,6},{6,7},{7,5},{5,3},{3,1},{1,0},{8,10},{10,12},{12... | collective-permute-start | bytes 595976 | tf_op jit(solution)/shard_map/ppermute | solution.py:217
  13.4 8.4 %collective-permute-start.8 = (bf16[776,128]{1,0:T(8,128)(2,1)S(1)}, bf16[776,128]{1,0:T(8,128)(2,1)S(1)}, u32[]{:S(2)}, u32[]{:S(2)}) collective-permute-start(bf16[776,128]{1,0:T(8,128)(2,1)S(1)} %collective-permute-done.4.refs_1_), channel_id=1, source_target_pairs={{2,0},{4,2},{6,4},{7,6},{5,7},{3,5},{1,3},{0,1},{10,8},{12,10},{14... | collective-permute-start | bytes 595976 | tf_op jit(solution)/shard_map/ppermute | solution.py:217
  15.4 8.5 %collective-permute-start.7 = (bf16[776,128]{1,0:T(8,128)(2,1)S(1)}, bf16[776,128]{1,0:T(8,128)(2,1)S(1)}, u32[]{:S(2)}, u32[]{:S(2)}) collective-permute-start(bf16[776,128]{1,0:T(8,128)(2,1)S(1)} %collective-permute-done.3.refs_0_), channel_id=1, source_target_pairs={{0,2},{2,4},{4,6},{6,7},{7,5},{5,3},{3,1},{1,0},{8,10},{10,12},{12... | collective-permute-start | bytes 595976 | tf_op jit(solution)/shard_map/ppermute | solution.py:217
  17.6 8.1 %collective-permute-start.6 = (bf16[776,128]{1,0:T(8,128)(2,1)S(1)}, bf16[776,128]{1,0:T(8,128)(2,1)S(1)}, u32[]{:S(2)}, u32[]{:S(2)}) collective-permute-start(bf16[776,128]{1,0:T(8,128)(2,1)S(1)} %collective-permute-done.2.refs_1_), channel_id=1, source_target_pairs={{2,0},{4,2},{6,4},{7,6},{5,7},{3,5},{1,3},{0,1},{10,8},{12,10},{14... | collective-permute-start | bytes 595976 | tf_op jit(solution)/shard_map/ppermute | solution.py:217
  19.6 9.7 %collective-permute-start.5 = (bf16[776,128]{1,0:T(8,128)(2,1)S(1)}, bf16[776,128]{1,0:T(8,128)(2,1)S(1)}, u32[]{:S(2)}, u32[]{:S(2)}) collective-permute-start(bf16[776,128]{1,0:T(8,128)(2,1)S(1)} %collective-permute-done.1.refs_0_), channel_id=1, source_target_pairs={{0,2},{2,4},{4,6},{6,7},{7,5},{5,3},{3,1},{1,0},{8,10},{10,12},{12... | collective-permute-start | bytes 595976 | tf_op jit(solution)/shard_map/ppermute | solution.py:217
  21.9 8.1 %collective-permute-start.10 = (bf16[776,128]{1,0:T(8,128)(2,1)S(1)}, bf16[776,128]{1,0:T(8,128)(2,1)S(1)}, u32[]{:S(2)}, u32[]{:S(2)}) collective-permute-start(bf16[776,128]{1,0:T(8,128)(2,1)S(1)} %collective-permute-done.8.refs_1_), channel_id=1, source_target_pairs={{2,0},{4,2},{6,4},{7,6},{5,7},{3,5},{1,3},{0,1},{10,8},{12,10},{14... | collective-permute-start | bytes 595976 | tf_op jit(solution)/shard_map/ppermute | solution.py:217
  25.8 8.5 %collective-permute-start.13 = (bf16[776,128]{1,0:T(8,128)(2,1)S(1)}, bf16[776,128]{1,0:T(8,128)(2,1)S(1)}, u32[]{:S(2)}, u32[]{:S(2)}) collective-permute-start(bf16[776,128]{1,0:T(8,128)(2,1)S(1)} %collective-permute-done.6.refs_1_), channel_id=1, source_target_pairs={{2,0},{4,2},{6,4},{7,6},{5,7},{3,5},{1,3},{0,1},{10,8},{12,10},{14... | collective-permute-start | bytes 595976 | tf_op jit(solution)/shard_map/ppermute | solution.py:217
  26.2 8.1 %collective-permute-start.12 = (bf16[776,128]{1,0:T(8,128)(2,1)S(1)}, bf16[776,128]{1,0:T(8,128)(2,1)S(1)}, u32[]{:S(2)}, u32[]{:S(2)}) collective-permute-start(bf16[776,128]{1,0:T(8,128)(2,1)S(1)} %collective-permute-done.7.refs_0_), channel_id=1, source_target_pairs={{0,2},{2,4},{4,6},{6,7},{7,5},{5,3},{3,1},{1,0},{8,10},{10,12},{12... | collective-permute-start | bytes 595976 | tf_op jit(solution)/shard_map/ppermute | solution.py:217
  30.1 7.2 %collective-permute-start.11 = (bf16[776,128]{1,0:T(8,128)(2,1)S(1)}, bf16[776,128]{1,0:T(8,128)(2,1)S(1)}, u32[]{:S(2)}, u32[]{:S(2)}) collective-permute-start(bf16[776,128]{1,0:T(8,128)(2,1)S(1)} %collective-permute-done.10.refs_1_), channel_id=1, source_target_pairs={{2,0},{4,2},{6,4},{7,6},{5,7},{3,5},{1,3},{0,1},{10,8},{12,10},{14... | collective-permute-start | bytes 595976 | tf_op jit(solution)/shard_map/ppermute | solution.py:217
  30.4 7.0 %collective-permute-start.9 = (bf16[776,128]{1,0:T(8,128)(2,1)S(1)}, bf16[776,128]{1,0:T(8,128)(2,1)S(1)}, u32[]{:S(2)}, u32[]{:S(2)}) collective-permute-start(bf16[776,128]{1,0:T(8,128)(2,1)S(1)} %collective-permute-done.5.refs_0_), channel_id=1, source_target_pairs={{0,2},{2,4},{4,6},{6,7},{7,5},{5,3},{3,1},{1,0},{8,10},{10,12},{12... | collective-permute-start | bytes 595976 | tf_op jit(solution)/shard_map/ppermute | solution.py:217
  33.6 0.9 %copy-start.2 = (s32[16]{0:T(128)S(1)}, s32[16]{0:T(128)}, u32[]{:S(2)}) copy-start(s32[16]{0:T(128)} %owners_ref.5) | copy-start | bytes 196
  36.0 3.2 %collective-permute-start.17 = (f32[128,512]{1,0:T(8,128)S(1)}, f32[128,512]{1,0:T(8,128)S(1)}, u32[]{:S(2)}, u32[]{:S(2)}) collective-permute-start(f32[128,512]{1,0:T(8,128)S(1)} %get-tuple-element.132), channel_id=1, source_target_pairs={{0,8},{8,0},{16,24},{24,16},{1,9},{9,1},{17,25},{25,17},{2,10},{10... | collective-permute-start | bytes 786440 | tf_op jit(solution)/shard_map/ppermute | solution.py:241
  39.0 1.7 %collective-permute-start.14 = (f32[128,512]{1,0:T(8,128)S(1)}, f32[128,512]{1,0:T(8,128)S(1)}, u32[]{:S(2)}, u32[]{:S(2)}) collective-permute-start(f32[128,512]{1,0:T(8,128)S(1)} %get-tuple-element.122), channel_id=1, source_target_pairs={{0,8},{8,0},{16,24},{24,16},{1,9},{9,1},{17,25},{25,17},{2,10},{10... | collective-permute-start | bytes 786440 | tf_op jit(solution)/shard_map/ppermute | solution.py:241
  39.2 6.1 %collective-permute-start.18 = (f16[128,512]{1,0:T(8,128)(2,1)S(1)}, f16[128,512]{1,0:T(8,128)(2,1)S(1)}, u32[]{:S(2)}, u32[]{:S(2)}) collective-permute-start(f16[128,512]{1,0:T(8,128)(2,1)S(1)} %multiply_convert_fusion), channel_id=1, source_target_pairs={{0,16},{8,24},{16,0},{24,8},{1,17},{9,25},{17,1},{25,9},{2,18},{10... | collective-permute-start | bytes 393224 | tf_op jit(solution)/shard_map/ppermute | solution.py:246
  40.8 7.2 %copy-start.3 = (f32[256,512]{1,0:T(8,128)S(1)}, f32[256,512]{1,0:T(8,128)}, u32[]{:S(2)}) copy-start(f32[256,512]{1,0:T(8,128)} %param.19) | copy-start | bytes 1572868
  41.7 6.3 %collective-permute-start.15 = (f32[256,512]{1,0:T(8,128)S(1)}, f32[256,512]{1,0:T(8,128)S(1)}, u32[]{:S(2)}, u32[]{:S(2)}) collective-permute-start(f32[256,512]{1,0:T(8,128)S(1)} %get-tuple-element.128), channel_id=1, source_target_pairs={{0,8},{8,0},{16,24},{24,16},{1,9},{9,1},{17,25},{25,17},{2,10},{10... | collective-permute-start | bytes 1572872 | tf_op jit(solution)/shard_map/ppermute | solution.py:289
  42.0 6.0 %collective-permute-start.16 = (f16[128,512]{1,0:T(8,128)(2,1)S(1)}, f16[128,512]{1,0:T(8,128)(2,1)S(1)}, u32[]{:S(2)}, u32[]{:S(2)}) collective-permute-start(f16[128,512]{1,0:T(8,128)(2,1)S(1)} %multiply_convert_fusion.1), channel_id=1, source_target_pairs={{0,16},{8,24},{16,0},{24,8},{1,17},{9,25},{17,1},{25,9},{2,18},{10... | collective-permute-start | bytes 393224 | tf_op jit(solution)/shard_map/ppermute | solution.py:246

commit v8 on v7

--- a/solution.py
+++ b/solution.py
@@ -258,7 +258,6 @@
 
     first = hop(0, [own[t] for _, t in waves[0]])
     parts = [products(own, marks_in(0, own))]
-    own, parts = lax.optimization_barrier((own, parts))
     second = hop(1, [own[t] for _, t in waves[1]])
     for step in range(1, n_dev // 2):
         landed, parts = landed_after(parts, first)

time: 49.2 us -> 49.2 us (level)
  no operation moved by 1% of the time
where the time goes in v8:
time: 49.2 us; the launch traced here: 49.1 us
  starting transfers between devices  18.9 us (38%)
  waiting for transfers between devices  12.9 us (26%)
  Pallas kernels  12.2 us (25%)
  other arithmetic  3.59 us (7%)
  local copies, waits for them, and re-layouts  1.17 us (2%)
    ppermute x14, starting transfers between devices, hop(): lax.ppermute(piece, 'dev', forward if ahead else backward)  15.5 us
    pallas_call x9, Pallas kernels, call(): pl.pallas_call(kernel, out_shape=out_shape, in_specs=[SMEM] * n_smem + [V...  12.2 us
    ppermute x14, waiting for transfers between devices, hop(): lax.ppermute(piece, 'dev', forward if ahead else backward)  8.4 us
    ppermute x2, waiting for transfers between devices, sent(): lax.ppermute((rows * SCALE).astype(jnp.float16), 'grp', [(g, (g + shift)...  4.53 us
    ppermute x2, starting transfers between devices, sent(): lax.ppermute((rows * SCALE).astype(jnp.float16), 'grp', [(g, (g + shift)...  2.95 us
    concatenate x1, other arithmetic, per_device(): own = rows_of(jnp.concatenate([ladder_amps, cycle_amps], axis=1))  1.56 us
    add x1, other arithmetic, per_device(): total = total + chosen.reshape(base.shape)  1.08 us
  transfers between devices with their start and end apart: 19, of which 10 were waited for; matrix products, arithmetic and copies ran while one was open for 3% of the time, Pallas kernels for 25%

profile of v8, /device:TPU:0, one launch (start us, length us, event | category | flops | bytes accessed | tf_op | source)
XLA Modules:
  0.0 49.1 jit_solution(2185586477870076797)
XLA Ops:
  0.0 1.6 %pad_maximum_fusion = bf16[2,24,4096]{2,0,1:T(2,128)(2,1)S(1)} fusion(bf16[2,6,4096]{2,0,1:T(2,128)(2,1)} %param.13, bf16[2,18,4096]{2,0,1:T(2,128)(2,1)} %param.10), kind=kLoop, calls=%fused_computation.4 | loop fusion | flops 196608 | bytes 786432 | tf_op jit(solution)/shard_map/concatenate | solution.py:176
  1.6 0.2 copy.11
  2.3 3.1 %collective-permute-start = (bf16[776,128]{1,0:T(8,128)(2,1)S(1)}, bf16[776,128]{1,0:T(8,128)(2,1)S(1)}, u32[]{:S(2)}, u32[]{:S(2)}) collective-permute-start(bf16[776,128]{1,0:T(8,128)(2,1)S(1)} %get-tuple-element.133.refs_0_), channel_id=1, source_target_pairs={{0,2},{2,4},{4,6},{6,7},{7,5},{5,3},{3,1},{1,0},{8,10},{10,12},{12... | collective-permute-start | bytes 595976 | tf_op jit(solution)/shard_map/ppermute | solution.py:217
  5.4 2.0 %collective-permute-start.3 = (bf16[776,128]{1,0:T(8,128)(2,1)S(1)}, bf16[776,128]{1,0:T(8,128)(2,1)S(1)}, u32[]{:S(2)}, u32[]{:S(2)}) collective-permute-start(bf16[776,128]{1,0:T(8,128)(2,1)S(1)} %get-tuple-element.134.refs_1_), channel_id=1, source_target_pairs={{0,2},{2,4},{4,6},{6,7},{7,5},{5,3},{3,1},{1,0},{8,10},{10,12},{12... | collective-permute-start | bytes 595976 | tf_op jit(solution)/shard_map/ppermute | solution.py:217
  7.5 1.4 %shard_map.100 = f32[128,512]{1,0:T(8,128)S(1)} custom-call(s32[48]{0:T(128)S(1)} %maximum_convert_fusion.ids_ref, bf16[776,128]{1,0:T(8,128)(2,1)S(1)} %get-tuple-element.133.refs_0_, bf16[776,128]{1,0:T(8,128)(2,1)S(1)} %get-tuple-element.134.refs_1_, bf16[1536,512]{1,0:T(8,128)(2,1)S(1)} %copy-done, bf16[512,512]{1,0:T(8,128)(2,1)S(1)} %copy-done.1), custom_call_target="tpu_custom_call" | custom-call | flops 1 | bytes 1 | tf_op jit(solution)/shard_map/pallas_call | solution.py:145
  8.9 2.2 %collective-permute-done.refs_0_ = bf16[776,128]{1,0:T(8,128)(2,1)S(1)} collective-permute-done((bf16[776,128]{1,0:T(8,128)(2,1)S(1)}, bf16[776,128]{1,0:T(8,128)(2,1)S(1)}, u32[]{:S(2)}, u32[]{:S(2)}) %collective-permute-start) | collective-permute-done | bytes 198688 | tf_op jit(solution)/shard_map/ppermute | solution.py:217
  11.1 2.1 %collective-permute-start.1 = (bf16[776,128]{1,0:T(8,128)(2,1)S(1)}, bf16[776,128]{1,0:T(8,128)(2,1)S(1)}, u32[]{:S(2)}, u32[]{:S(2)}) collective-permute-start(bf16[776,128]{1,0:T(8,128)(2,1)S(1)} %collective-permute-done.refs_0_), channel_id=1, source_target_pairs={{0,2},{2,4},{4,6},{6,7},{7,5},{5,3},{3,1},{1,0},{8,10},{10,12},{12... | collective-permute-start | bytes 595976 | tf_op jit(solution)/shard_map/ppermute | solution.py:217
  13.4 1.4 %shard_map.101 = f32[128,512]{1,0:T(8,128)S(1)} custom-call(s32[48]{0:T(128)S(1)} %maximum_convert_fusion.1.ids_ref, bf16[776,128]{1,0:T(8,128)(2,1)S(1)} %collective-permute-done.refs_0_, bf16[776,128]{1,0:T(8,128)(2,1)S(1)} %collective-permute-done.4.refs_1_, bf16[1536,512]{1,0:T(8,128)(2,1)S(1)} %copy-done, bf16[512,512]{1,0:T(8,128)(2,1)S(1)} %copy-done.1), custom_call_target="tpu_custom_call" | custom-call | flops 1 | bytes 1 | tf_op jit(solution)/shard_map/pallas_call | solution.py:145
  14.8 0.6 %collective-permute-done.3.refs_0_ = bf16[776,128]{1,0:T(8,128)(2,1)S(1)} collective-permute-done((bf16[776,128]{1,0:T(8,128)(2,1)S(1)}, bf16[776,128]{1,0:T(8,128)(2,1)S(1)}, u32[]{:S(2)}, u32[]{:S(2)}) %collective-permute-start.3) | collective-permute-done | bytes 198688 | tf_op jit(solution)/shard_map/ppermute | solution.py:217
  15.4 2.1 %collective-permute-start.7 = (bf16[776,128]{1,0:T(8,128)(2,1)S(1)}, bf16[776,128]{1,0:T(8,128)(2,1)S(1)}, u32[]{:S(2)}, u32[]{:S(2)}) collective-permute-start(bf16[776,128]{1,0:T(8,128)(2,1)S(1)} %collective-permute-done.3.refs_0_), channel_id=1, source_target_pairs={{0,2},{2,4},{4,6},{6,7},{7,5},{5,3},{3,1},{1,0},{8,10},{10,12},{12... | collective-permute-start | bytes 595976 | tf_op jit(solution)/shard_map/ppermute | solution.py:217
  17.6 1.4 %shard_map.102 = f32[128,512]{1,0:T(8,128)S(1)} custom-call(s32[48]{0:T(128)S(1)} %maximum_convert_fusion.2.ids_ref, bf16[776,128]{1,0:T(8,128)(2,1)S(1)} %collective-permute-done.3.refs_0_, bf16[776,128]{1,0:T(8,128)(2,1)S(1)} %collective-permute-done.2.refs_1_, bf16[1536,512]{1,0:T(8,128)(2,1)S(1)} %copy-done, bf16[512,512]{1,0:T(8,128)(2,1)S(1)} %copy-done.1), custom_call_target="tpu_custom_call" | custom-call | flops 1 | bytes 1 | tf_op jit(solution)/shard_map/pallas_call | solution.py:145
  19.0 0.6 %collective-permute-done.1.refs_0_ = bf16[776,128]{1,0:T(8,128)(2,1)S(1)} collective-permute-done((bf16[776,128]{1,0:T(8,128)(2,1)S(1)}, bf16[776,128]{1,0:T(8,128)(2,1)S(1)}, u32[]{:S(2)}, u32[]{:S(2)}) %collective-permute-start.1) | collective-permute-done | bytes 198688 | tf_op jit(solution)/shard_map/ppermute | solution.py:217
  19.6 2.1 %collective-permute-start.5 = (bf16[776,128]{1,0:T(8,128)(2,1)S(1)}, bf16[776,128]{1,0:T(8,128)(2,1)S(1)}, u32[]{:S(2)}, u32[]{:S(2)}) collective-permute-start(bf16[776,128]{1,0:T(8,128)(2,1)S(1)} %collective-permute-done.1.refs_0_), channel_id=1, source_target_pairs={{0,2},{2,4},{4,6},{6,7},{7,5},{5,3},{3,1},{1,0},{8,10},{10,12},{12... | collective-permute-start | bytes 595976 | tf_op jit(solution)/shard_map/ppermute | solution.py:217
  21.9 1.4 %shard_map.103 = f32[128,512]{1,0:T(8,128)S(1)} custom-call(s32[48]{0:T(128)S(1)} %maximum_convert_fusion.3.ids_ref, bf16[776,128]{1,0:T(8,128)(2,1)S(1)} %collective-permute-done.1.refs_0_, bf16[776,128]{1,0:T(8,128)(2,1)S(1)} %collective-permute-done.8.refs_1_, bf16[1536,512]{1,0:T(8,128)(2,1)S(1)} %copy-done, bf16[512,512]{1,0:T(8,128)(2,1)S(1)} %copy-done.1), custom_call_target="tpu_custom_call" | custom-call | flops 1 | bytes 1 | tf_op jit(solution)/shard_map/pallas_call | solution.py:145
  23.3 0.6 %collective-permute-done.7.refs_0_ = bf16[776,128]{1,0:T(8,128)(2,1)S(1)} collective-permute-done((bf16[776,128]{1,0:T(8,128)(2,1)S(1)}, bf16[776,128]{1,0:T(8,128)(2,1)S(1)}, u32[]{:S(2)}, u32[]{:S(2)}) %collective-permute-start.7) | collective-permute-done | bytes 198688 | tf_op jit(solution)/shard_map/ppermute | solution.py:217
  23.9 2.2 %collective-permute-done.6.refs_1_ = bf16[776,128]{1,0:T(8,128)(2,1)S(1)} collective-permute-done((bf16[776,128]{1,0:T(8,128)(2,1)S(1)}, bf16[776,128]{1,0:T(8,128)(2,1)S(1)}, u32[]{:S(2)}, u32[]{:S(2)}) %collective-permute-start.6) | collective-permute-done | bytes 198688 | tf_op jit(solution)/shard_map/ppermute | solution.py:217
  26.2 2.0 %collective-permute-start.12 = (bf16[776,128]{1,0:T(8,128)(2,1)S(1)}, bf16[776,128]{1,0:T(8,128)(2,1)S(1)}, u32[]{:S(2)}, u32[]{:S(2)}) collective-permute-start(bf16[776,128]{1,0:T(8,128)(2,1)S(1)} %collective-permute-done.7.refs_0_), channel_id=1, source_target_pairs={{0,2},{2,4},{4,6},{6,7},{7,5},{5,3},{3,1},{1,0},{8,10},{10,12},{12... | collective-permute-start | bytes 595976 | tf_op jit(solution)/shard_map/ppermute | solution.py:217
  28.2 1.4 %shard_map.104 = f32[128,512]{1,0:T(8,128)S(1)} custom-call(s32[48]{0:T(128)S(1)} %maximum_convert_fusion.4.ids_ref, bf16[776,128]{1,0:T(8,128)(2,1)S(1)} %collective-permute-done.7.refs_0_, bf16[776,128]{1,0:T(8,128)(2,1)S(1)} %collective-permute-done.6.refs_1_, bf16[1536,512]{1,0:T(8,128)(2,1)S(1)} %copy-done, bf16[512,512]{1,0:T(8,128)(2,1)S(1)} %copy-done.1), custom_call_target="tpu_custom_call" | custom-call | flops 1 | bytes 1 | tf_op jit(solution)/shard_map/pallas_call | solution.py:145
  29.6 0.7 %collective-permute-done.10.refs_1_ = bf16[776,128]{1,0:T(8,128)(2,1)S(1)} collective-permute-done((bf16[776,128]{1,0:T(8,128)(2,1)S(1)}, bf16[776,128]{1,0:T(8,128)(2,1)S(1)}, u32[]{:S(2)}, u32[]{:S(2)}) %collective-permute-start.10) | collective-permute-done | bytes 198688 | tf_op jit(solution)/shard_map/ppermute | solution.py:217
  30.4 2.0 %collective-permute-start.9 = (bf16[776,128]{1,0:T(8,128)(2,1)S(1)}, bf16[776,128]{1,0:T(8,128)(2,1)S(1)}, u32[]{:S(2)}, u32[]{:S(2)}) collective-permute-start(bf16[776,128]{1,0:T(8,128)(2,1)S(1)} %collective-permute-done.5.refs_0_), channel_id=1, source_target_pairs={{0,2},{2,4},{4,6},{6,7},{7,5},{5,3},{3,1},{1,0},{8,10},{10,12},{12... | collective-permute-start | bytes 595976 | tf_op jit(solution)/shard_map/ppermute | solution.py:217
  32.5 1.4 %shard_map.105 = f32[128,512]{1,0:T(8,128)S(1)} custom-call(s32[48]{0:T(128)S(1)} %maximum_convert_fusion.6.ids_ref, bf16[776,128]{1,0:T(8,128)(2,1)S(1)} %collective-permute-done.5.refs_0_, bf16[776,128]{1,0:T(8,128)(2,1)S(1)} %collective-permute-done.10.refs_1_, bf16[1536,512]{1,0:T(8,128)(2,1)S(1)} %copy-done, bf16[512,512]{1,0:T(8,128)(2,1)S(1)} %copy-done.1), custom_call_target="tpu_custom_call" | custom-call | flops 1 | bytes 1 | tf_op jit(solution)/shard_map/pallas_call | solution.py:145
  34.0 0.5 %collective-permute-done.13.refs_1_ = bf16[776,128]{1,0:T(8,128)(2,1)S(1)} collective-permute-done((bf16[776,128]{1,0:T(8,128)(2,1)S(1)}, bf16[776,128]{1,0:T(8,128)(2,1)S(1)}, u32[]{:S(2)}, u32[]{:S(2)}) %collective-permute-start.13) | collective-permute-done | bytes 198688 | tf_op jit(solution)/shard_map/ppermute | solution.py:217
  34.7 1.5 %shard_map.106 = (f32[128,512]{1,0:T(8,128)S(1)}, f32[128,512]{1,0:T(8,128)S(1)}, f32[128,512]{1,0:T(8,128)S(1)}) custom-call(s32[48]{0:T(128)S(1)} %maximum_convert_fusion.7.ids_ref, s32[16]{0:T(128)S(1)} %copy-done.2, bf16[776,128]{1,0:T(8,128)(2,1)S(1)} %collective-permute-done.12.refs_0_, bf16[776,128]{1,0:T(8,128)(2,1)S(1)} %collective-permute-done.13.refs_1_, ...), custom_call_target="tpu_custom_call" | custom-call | flops 1 | bytes 1 | tf_op jit(solution)/shard_map/pallas_call | solution.py:145
  36.3 1.0 %collective-permute-done.11.refs_1_ = bf16[776,128]{1,0:T(8,128)(2,1)S(1)} collective-permute-done((bf16[776,128]{1,0:T(8,128)(2,1)S(1)}, bf16[776,128]{1,0:T(8,128)(2,1)S(1)}, u32[]{:S(2)}, u32[]{:S(2)}) %collective-permute-start.11) | collective-permute-done | bytes 198688 | tf_op jit(solution)/shard_map/ppermute | solution.py:217
  37.5 1.5 %shard_map.107 = (f32[128,512]{1,0:T(8,128)S(1)}, f32[128,512]{1,0:T(8,128)S(1)}, f32[128,512]{1,0:T(8,128)S(1)}) custom-call(s32[48]{0:T(128)S(1)} %maximum_convert_fusion.5.ids_ref, s32[16]{0:T(128)S(1)} %copy-done.2, bf16[776,128]{1,0:T(8,128)(2,1)S(1)} %collective-permute-done.9.refs_0_, bf16[776,128]{1,0:T(8,128)(2,1)S(1)} %collective-permute-done.11.refs_1_, ...), custom_call_target="tpu_custom_call" | custom-call | flops 1 | bytes 1 | tf_op jit(solution)/shard_map/pallas_call | solution.py:145
  39.2 1.6 %collective-permute-start.18 = (f16[128,512]{1,0:T(8,128)(2,1)S(1)}, f16[128,512]{1,0:T(8,128)(2,1)S(1)}, u32[]{:S(2)}, u32[]{:S(2)}) collective-permute-start(f16[128,512]{1,0:T(8,128)(2,1)S(1)} %multiply_convert_fusion), channel_id=1, source_target_pairs={{0,16},{8,24},{16,0},{24,8},{1,17},{9,25},{17,1},{25,9},{2,18},{10... | collective-permute-start | bytes 393224 | tf_op jit(solution)/shard_map/ppermute | solution.py:246
  40.8 0.9 %shard_map.108 = (f32[256,512]{1,0:T(8,128)S(1)}, f32[256,512]{1,0:T(8,128)S(1)}, s32[256,512]{1,0:T(8,128)S(1)}) custom-call(s32[16]{0:T(128)S(1)} %copy-done.2, f32[768,512]{1,0:T(8,128)S(1)} %constant_dynamic-update-slice_fusion.refs_4_.refs_0_, f32[128,512]{1,0:T(8,128)S(1)} %get-tuple-element.119.refs_5_.refs_1_, f32[128,512]{1,0:T(8,128)S(1)} %get-tuple-element.120.refs_2_), custom_call_target="tpu_custom_call" | custom-call | flops 1 | bytes 1 | tf_op jit(solution)/shard_map/pallas_call | solution.py:145
  41.7 0.3 collective-permute-start.15
  42.0 1.4 %collective-permute-start.16 = (f16[128,512]{1,0:T(8,128)(2,1)S(1)}, f16[128,512]{1,0:T(8,128)(2,1)S(1)}, u32[]{:S(2)}, u32[]{:S(2)}) collective-permute-start(f16[128,512]{1,0:T(8,128)(2,1)S(1)} %multiply_convert_fusion.1), channel_id=1, source_target_pairs={{0,16},{8,24},{16,0},{24,8},{1,17},{9,25},{17,1},{25,9},{2,18},{10... | collective-permute-start | bytes 393224 | tf_op jit(solution)/shard_map/ppermute | solution.py:246
  43.4 1.9 %collective-permute-done.18 = f16[128,512]{1,0:T(8,128)(2,1)S(1)} collective-permute-done((f16[128,512]{1,0:T(8,128)(2,1)S(1)}, f16[128,512]{1,0:T(8,128)(2,1)S(1)}, u32[]{:S(2)}, u32[]{:S(2)}) %collective-permute-start.18) | collective-permute-done | bytes 131104 | tf_op jit(solution)/shard_map/ppermute | solution.py:246
  45.3 2.7 %collective-permute-done.16 = f16[128,512]{1,0:T(8,128)(2,1)S(1)} collective-permute-done((f16[128,512]{1,0:T(8,128)(2,1)S(1)}, f16[128,512]{1,0:T(8,128)(2,1)S(1)}, u32[]{:S(2)}, u32[]{:S(2)}) %collective-permute-start.16) | collective-permute-done | bytes 131104 | tf_op jit(solution)/shard_map/ppermute | solution.py:246
  48.0 1.1 %multiply_add_fusion = f32[256,512]{1,0:T(8,128)} fusion(f32[256,512]{1,0:T(8,128)S(1)} %copy-done.3, f32[256,512]{1,0:T(8,128)S(1)} %get-tuple-element.121, f32[256,512]{1,0:T(8,128)S(1)} %collective-permute-done.15, s32[256,512]{1,0:T(8,128)S(1)} %get-tuple-element.123, f16[64,512]{1,0:T(8,128)(2,1)S(1)} %get-tuple-element.132, ...), kind=kLoop, calls=%fused_computation | loop fusion | flops 1441792 | bytes 2883584 | tf_op jit(solution)/shard_map/add | solution.py:296
  (74 shorter events, 2.2 us)
Async XLA Ops:
  0.0 2.0 %copy-start.5 = (s32[2,18]{1,0:T(2,128)S(1)}, s32[2,18]{1,0:T(2,128)}, u32[]{:S(2)}) copy-start(s32[2,18]{1,0:T(2,128)} %param.11) | copy-start | bytes 436
  0.0 2.0 %copy-start.6 = (s32[2,1]{0,1:T(1,128)S(1)}, s32[2,1]{0,1:T(1,128)}, u32[]{:S(2)}) copy-start(s32[2,1]{0,1:T(1,128)} %param.12) | copy-start | bytes 28
  0.0 2.0 %copy-start.4 = (s32[2,6]{1,0:T(2,128)S(1)}, s32[2,6]{1,0:T(2,128)}, u32[]{:S(2)}) copy-start(s32[2,6]{1,0:T(2,128)} %param.14) | copy-start | bytes 148
  0.0 2.1 %copy-start.7 = (s32[2,1]{0,1:T(1,128)S(1)}, s32[2,1]{0,1:T(1,128)}, u32[]{:S(2)}) copy-start(s32[2,1]{0,1:T(1,128)} %param.15) | copy-start | bytes 28
  1.6 5.9 %copy-start = (bf16[1536,512]{1,0:T(8,128)(2,1)S(1)}, bf16[1536,512]{1,0:T(8,128)(2,1)}, u32[]{:S(2)}) copy-start(bf16[1536,512]{1,0:T(8,128)(2,1)} %refs_2_.15) | copy-start | bytes 4718596
  1.6 5.9 %copy-start.1 = (bf16[512,512]{1,0:T(8,128)(2,1)S(1)}, bf16[512,512]{1,0:T(8,128)(2,1)}, u32[]{:S(2)}) copy-start(bf16[512,512]{1,0:T(8,128)(2,1)} %refs_3_.15) | copy-start | bytes 1572868
  2.3 8.8 %collective-permute-start = (bf16[776,128]{1,0:T(8,128)(2,1)S(1)}, bf16[776,128]{1,0:T(8,128)(2,1)S(1)}, u32[]{:S(2)}, u32[]{:S(2)}) collective-permute-start(bf16[776,128]{1,0:T(8,128)(2,1)S(1)} %get-tuple-element.133.refs_0_), channel_id=1, source_target_pairs={{0,2},{2,4},{4,6},{6,7},{7,5},{5,3},{3,1},{1,0},{8,10},{10,12},{12... | collective-permute-start | bytes 595976 | tf_op jit(solution)/shard_map/ppermute | solution.py:217
  5.4 7.9 %collective-permute-start.4 = (bf16[776,128]{1,0:T(8,128)(2,1)S(1)}, bf16[776,128]{1,0:T(8,128)(2,1)S(1)}, u32[]{:S(2)}, u32[]{:S(2)}) collective-permute-start(bf16[776,128]{1,0:T(8,128)(2,1)S(1)} %get-tuple-element.134.refs_1_), channel_id=1, source_target_pairs={{2,0},{4,2},{6,4},{7,6},{5,7},{3,5},{1,3},{0,1},{10,8},{12,10},{14... | collective-permute-start | bytes 595976 | tf_op jit(solution)/shard_map/ppermute | solution.py:217
  5.4 10.0 %collective-permute-start.3 = (bf16[776,128]{1,0:T(8,128)(2,1)S(1)}, bf16[776,128]{1,0:T(8,128)(2,1)S(1)}, u32[]{:S(2)}, u32[]{:S(2)}) collective-permute-start(bf16[776,128]{1,0:T(8,128)(2,1)S(1)} %get-tuple-element.134.refs_1_), channel_id=1, source_target_pairs={{0,2},{2,4},{4,6},{6,7},{7,5},{5,3},{3,1},{1,0},{8,10},{10,12},{12... | collective-permute-start | bytes 595976 | tf_op jit(solution)/shard_map/ppermute | solution.py:217
  7.4 10.1 %collective-permute-start.2 = (bf16[776,128]{1,0:T(8,128)(2,1)S(1)}, bf16[776,128]{1,0:T(8,128)(2,1)S(1)}, u32[]{:S(2)}, u32[]{:S(2)}) collective-permute-start(bf16[776,128]{1,0:T(8,128)(2,1)S(1)} %get-tuple-element.133.refs_0_), channel_id=1, source_target_pairs={{2,0},{4,2},{6,4},{7,6},{5,7},{3,5},{1,3},{0,1},{10,8},{12,10},{14... | collective-permute-start | bytes 595976 | tf_op jit(solution)/shard_map/ppermute | solution.py:217
  11.1 8.5 %collective-permute-start.1 = (bf16[776,128]{1,0:T(8,128)(2,1)S(1)}, bf16[776,128]{1,0:T(8,128)(2,1)S(1)}, u32[]{:S(2)}, u32[]{:S(2)}) collective-permute-start(bf16[776,128]{1,0:T(8,128)(2,1)S(1)} %collective-permute-done.refs_0_), channel_id=1, source_target_pairs={{0,2},{2,4},{4,6},{6,7},{7,5},{5,3},{3,1},{1,0},{8,10},{10,12},{12... | collective-permute-start | bytes 595976 | tf_op jit(solution)/shard_map/ppermute | solution.py:217
  13.4 8.4 %collective-permute-start.8 = (bf16[776,128]{1,0:T(8,128)(2,1)S(1)}, bf16[776,128]{1,0:T(8,128)(2,1)S(1)}, u32[]{:S(2)}, u32[]{:S(2)}) collective-permute-start(bf16[776,128]{1,0:T(8,128)(2,1)S(1)} %collective-permute-done.4.refs_1_), channel_id=1, source_target_pairs={{2,0},{4,2},{6,4},{7,6},{5,7},{3,5},{1,3},{0,1},{10,8},{12,10},{14... | collective-permute-start | bytes 595976 | tf_op jit(solution)/shard_map/ppermute | solution.py:217
  15.4 8.5 %collective-permute-start.7 = (bf16[776,128]{1,0:T(8,128)(2,1)S(1)}, bf16[776,128]{1,0:T(8,128)(2,1)S(1)}, u32[]{:S(2)}, u32[]{:S(2)}) collective-permute-start(bf16[776,128]{1,0:T(8,128)(2,1)S(1)} %collective-permute-done.3.refs_0_), channel_id=1, source_target_pairs={{0,2},{2,4},{4,6},{6,7},{7,5},{5,3},{3,1},{1,0},{8,10},{10,12},{12... | collective-permute-start | bytes 595976 | tf_op jit(solution)/shard_map/ppermute | solution.py:217
  17.6 8.4 %collective-permute-start.6 = (bf16[776,128]{1,0:T(8,128)(2,1)S(1)}, bf16[776,128]{1,0:T(8,128)(2,1)S(1)}, u32[]{:S(2)}, u32[]{:S(2)}) collective-permute-start(bf16[776,128]{1,0:T(8,128)(2,1)S(1)} %collective-permute-done.2.refs_1_), channel_id=1, source_target_pairs={{2,0},{4,2},{6,4},{7,6},{5,7},{3,5},{1,3},{0,1},{10,8},{12,10},{14... | collective-permute-start | bytes 595976 | tf_op jit(solution)/shard_map/ppermute | solution.py:217
  19.6 10.0 %collective-permute-start.5 = (bf16[776,128]{1,0:T(8,128)(2,1)S(1)}, bf16[776,128]{1,0:T(8,128)(2,1)S(1)}, u32[]{:S(2)}, u32[]{:S(2)}) collective-permute-start(bf16[776,128]{1,0:T(8,128)(2,1)S(1)} %collective-permute-done.1.refs_0_), channel_id=1, source_target_pairs={{0,2},{2,4},{4,6},{6,7},{7,5},{5,3},{3,1},{1,0},{8,10},{10,12},{12... | collective-permute-start | bytes 595976 | tf_op jit(solution)/shard_map/ppermute | solution.py:217
  21.9 8.4 %collective-permute-start.10 = (bf16[776,128]{1,0:T(8,128)(2,1)S(1)}, bf16[776,128]{1,0:T(8,128)(2,1)S(1)}, u32[]{:S(2)}, u32[]{:S(2)}) collective-permute-start(bf16[776,128]{1,0:T(8,128)(2,1)S(1)} %collective-permute-done.8.refs_1_), channel_id=1, source_target_pairs={{2,0},{4,2},{6,4},{7,6},{5,7},{3,5},{1,3},{0,1},{10,8},{12,10},{14... | collective-permute-start | bytes 595976 | tf_op jit(solution)/shard_map/ppermute | solution.py:217
  26.0 8.5 %collective-permute-start.13 = (bf16[776,128]{1,0:T(8,128)(2,1)S(1)}, bf16[776,128]{1,0:T(8,128)(2,1)S(1)}, u32[]{:S(2)}, u32[]{:S(2)}) collective-permute-start(bf16[776,128]{1,0:T(8,128)(2,1)S(1)} %collective-permute-done.6.refs_1_), channel_id=1, source_target_pairs={{2,0},{4,2},{6,4},{7,6},{5,7},{3,5},{1,3},{0,1},{10,8},{12,10},{14... | collective-permute-start | bytes 595976 | tf_op jit(solution)/shard_map/ppermute | solution.py:217
  26.2 8.4 %collective-permute-start.12 = (bf16[776,128]{1,0:T(8,128)(2,1)S(1)}, bf16[776,128]{1,0:T(8,128)(2,1)S(1)}, u32[]{:S(2)}, u32[]{:S(2)}) collective-permute-start(bf16[776,128]{1,0:T(8,128)(2,1)S(1)} %collective-permute-done.7.refs_0_), channel_id=1, source_target_pairs={{0,2},{2,4},{4,6},{6,7},{7,5},{5,3},{3,1},{1,0},{8,10},{10,12},{12... | collective-permute-start | bytes 595976 | tf_op jit(solution)/shard_map/ppermute | solution.py:217
  30.4 7.0 %collective-permute-start.11 = (bf16[776,128]{1,0:T(8,128)(2,1)S(1)}, bf16[776,128]{1,0:T(8,128)(2,1)S(1)}, u32[]{:S(2)}, u32[]{:S(2)}) collective-permute-start(bf16[776,128]{1,0:T(8,128)(2,1)S(1)} %collective-permute-done.10.refs_1_), channel_id=1, source_target_pairs={{2,0},{4,2},{6,4},{7,6},{5,7},{3,5},{1,3},{0,1},{10,8},{12,10},{14... | collective-permute-start | bytes 595976 | tf_op jit(solution)/shard_map/ppermute | solution.py:217
  30.4 7.0 %collective-permute-start.9 = (bf16[776,128]{1,0:T(8,128)(2,1)S(1)}, bf16[776,128]{1,0:T(8,128)(2,1)S(1)}, u32[]{:S(2)}, u32[]{:S(2)}) collective-permute-start(bf16[776,128]{1,0:T(8,128)(2,1)S(1)} %collective-permute-done.5.refs_0_), channel_id=1, source_target_pairs={{0,2},{2,4},{4,6},{6,7},{7,5},{5,3},{3,1},{1,0},{8,10},{10,12},{12... | collective-permute-start | bytes 595976 | tf_op jit(solution)/shard_map/ppermute | solution.py:217
  33.8 0.9 %copy-start.2 = (s32[16]{0:T(128)S(1)}, s32[16]{0:T(128)}, u32[]{:S(2)}) copy-start(s32[16]{0:T(128)} %owners_ref.5) | copy-start | bytes 196
  36.2 2.9 %collective-permute-start.17 = (f32[128,512]{1,0:T(8,128)S(1)}, f32[128,512]{1,0:T(8,128)S(1)}, u32[]{:S(2)}, u32[]{:S(2)}) collective-permute-start(f32[128,512]{1,0:T(8,128)S(1)} %get-tuple-element.126), channel_id=1, source_target_pairs={{0,8},{8,0},{16,24},{24,16},{1,9},{9,1},{17,25},{25,17},{2,10},{10... | collective-permute-start | bytes 786440 | tf_op jit(solution)/shard_map/ppermute | solution.py:241
  39.0 1.7 %collective-permute-start.14 = (f32[128,512]{1,0:T(8,128)S(1)}, f32[128,512]{1,0:T(8,128)S(1)}, u32[]{:S(2)}, u32[]{:S(2)}) collective-permute-start(f32[128,512]{1,0:T(8,128)S(1)} %get-tuple-element.116), channel_id=1, source_target_pairs={{0,8},{8,0},{16,24},{24,16},{1,9},{9,1},{17,25},{25,17},{2,10},{10... | collective-permute-start | bytes 786440 | tf_op jit(solution)/shard_map/ppermute | solution.py:241
  39.2 6.1 %collective-permute-start.18 = (f16[128,512]{1,0:T(8,128)(2,1)S(1)}, f16[128,512]{1,0:T(8,128)(2,1)S(1)}, u32[]{:S(2)}, u32[]{:S(2)}) collective-permute-start(f16[128,512]{1,0:T(8,128)(2,1)S(1)} %multiply_convert_fusion), channel_id=1, source_target_pairs={{0,16},{8,24},{16,0},{24,8},{1,17},{9,25},{17,1},{25,9},{2,18},{10... | collective-permute-start | bytes 393224 | tf_op jit(solution)/shard_map/ppermute | solution.py:246
  40.8 7.2 %copy-start.3 = (f32[256,512]{1,0:T(8,128)S(1)}, f32[256,512]{1,0:T(8,128)}, u32[]{:S(2)}) copy-start(f32[256,512]{1,0:T(8,128)} %param.19) | copy-start | bytes 1572868
  41.7 6.3 %collective-permute-start.15 = (f32[256,512]{1,0:T(8,128)S(1)}, f32[256,512]{1,0:T(8,128)S(1)}, u32[]{:S(2)}, u32[]{:S(2)}) collective-permute-start(f32[256,512]{1,0:T(8,128)S(1)} %get-tuple-element.122), channel_id=1, source_target_pairs={{0,8},{8,0},{16,24},{24,16},{1,9},{9,1},{17,25},{25,17},{2,10},{10... | collective-permute-start | bytes 1572872 | tf_op jit(solution)/shard_map/ppermute | solution.py:288
  42.0 6.0 %collective-permute-start.16 = (f16[128,512]{1,0:T(8,128)(2,1)S(1)}, f16[128,512]{1,0:T(8,128)(2,1)S(1)}, u32[]{:S(2)}, u32[]{:S(2)}) collective-permute-start(f16[128,512]{1,0:T(8,128)(2,1)S(1)} %multiply_convert_fusion.1), channel_id=1, source_target_pairs={{0,16},{8,24},{16,0},{24,8},{1,17},{9,25},{17,1},{25,9},{2,18},{10... | collective-permute-start | bytes 393224 | tf_op jit(solution)/shard_map/ppermute | solution.py:246
